TPU v7x, 32 devices: a whole 2x2x4 slice. The times are simulated.
32 devices in a mesh: dp: 4 (over z), expert: 8 (over y, x, core).
Axes of the slice: x: 2, y: 2, z: 4, core: 2. Of those that a mesh axis runs over, the one named last changes fastest.
Arguments:
- tokens: bfloat16 [4096, 2048], P(('dp', 'expert')), may hold values from -6 to 6
- expert_ids: int32 [4096, 2], P(('dp', 'expert')), may hold values from 0 to 7, all different within a row; in each aligned block of 128 rows (0 to 127, 128 to 255, ...) at most 64 rows name the same one
- gate_probs: float32 [4096, 2], P(('dp', 'expert')), may hold values from 0.1 to 1
- w_gate: bfloat16 [8, 2048, 768], P('expert'), may hold values from -0.125 to 0.125
- w_up: bfloat16 [8, 2048, 768], P('expert'), may hold values from -0.125 to 0.125
- w_down: bfloat16 [8, 2048, 768], P('expert'), may hold values from -0.21875 to 0.21875
- out_grad: bfloat16 [4096, 2048], P(('dp', 'expert')), may hold values from -6 to 6
Outputs:
- mixed: bfloat16 [4096, 2048], P(('dp', 'expert'))
- tokens_grad: bfloat16 [4096, 2048], P(('dp', 'expert'))
- grad_gate: bfloat16 [8, 2048, 768], P('expert', 'dp')
- grad_up: bfloat16 [8, 2048, 768], P('expert', 'dp')
- grad_down: bfloat16 [8, 2048, 768], P('expert', 'dp')
Inputs may be any that keep to these rules, and one draw needn't show every extreme that they name: `expert_ids`: within each group of 128 tokens no expert is chosen by more than 64 tokens, and some expert reaches 64; a token's 2 experts differ; every expert is chosen somewhere.
All inputs are finite; a program needn't handle non-finite values.
Results may differ from a plain program's by a relative error of at most 0.014.
Values may be sent and summed in bfloat16 or wider, within the bound.
No kernel may reach another device: no remote copies, remote signals or barrier semaphores. Data moves between devices by JAX's collectives and lax.ppermute only.
A program may use at most 128 MiB of HBM per device.

v0:
```python
import jax
import jax.numpy as jnp
from jax import lax
from jax.sharding import PartitionSpec as P


def route_slots(expert_ids, experts, capacity):
    flat = expert_ids.reshape(-1)
    onehot = (flat[:, None] == jnp.arange(experts, dtype=jnp.int32)[None, :]).astype(jnp.int32)
    before = jnp.cumsum(onehot, axis=0) - onehot
    position = jnp.sum(before * onehot, axis=1)
    return flat * capacity + position


def local(tokens, expert_ids, gate_probs, w_gate, w_up, w_down, out_grad):
    token_count, top_count = expert_ids.shape
    width = tokens.shape[1]
    local_experts = w_gate.shape[0]
    peers = lax.axis_size("expert")
    experts = local_experts * peers
    capacity = max(2, 2 * token_count * top_count // experts)
    slot_total = experts * capacity
    route_total = token_count * top_count
    slot = route_slots(expert_ids, experts, capacity)
    owner = slot[None, :] == jnp.arange(slot_total, dtype=jnp.int32)[:, None]
    live = jnp.any(owner, axis=1)
    route_index = jnp.sum(
        jnp.where(owner, jnp.arange(route_total, dtype=jnp.int32)[None, :], 0), axis=1
    )
    token_of_slot = route_index // top_count
    slot_prob = jnp.sum(jnp.where(owner, gate_probs.reshape(-1)[None, :], 0.0), axis=1)
    dispatched = jnp.where(
        live[:, None], jnp.take(tokens, token_of_slot, axis=0), jnp.zeros((), tokens.dtype)
    )
    dispatched = dispatched.reshape(peers, local_experts, capacity, width)
    expert_received = lax.all_to_all(dispatched, "expert", split_axis=0, concat_axis=0, tiled=True)
    gate_act = jnp.einsum(
        "secd,edh->sech", expert_received, w_gate, preferred_element_type=jnp.float32
    )
    up_act = jnp.einsum("secd,edh->sech", expert_received, w_up, preferred_element_type=jnp.float32)
    expert_hidden = (jax.nn.silu(gate_act) * up_act).astype(jnp.bfloat16)
    result = jnp.einsum(
        "sech,edh->secd", expert_hidden, w_down, preferred_element_type=jnp.float32
    ).astype(jnp.bfloat16)
    returned = lax.all_to_all(result, "expert", split_axis=0, concat_axis=0, tiled=True)
    returned, gate_act, up_act, hidden, received = (
        returned,
        gate_act,
        up_act,
        expert_hidden,
        expert_received,
    )
    picked = jnp.take(returned.reshape(slot_total, width), slot, axis=0).astype(jnp.float32)
    picked = picked.reshape(token_count, top_count, width)
    mixed = jnp.sum(picked * gate_probs[:, :, None], axis=1).astype(jnp.bfloat16)
    dy_rows = jnp.where(
        live[:, None], jnp.take(out_grad, token_of_slot, axis=0), jnp.zeros((), out_grad.dtype)
    )
    dy_slot = (dy_rows.astype(jnp.float32) * slot_prob[:, None]).astype(jnp.bfloat16)
    dy_slot = dy_slot.reshape(peers, local_experts, capacity, width)
    dy_recv = lax.all_to_all(dy_slot, "expert", split_axis=0, concat_axis=0, tiled=True)
    d_hidden = jnp.einsum("secd,edh->sech", dy_recv, w_down, preferred_element_type=jnp.float32)
    sigma = jax.nn.sigmoid(gate_act)
    d_gate = (d_hidden * up_act * sigma * (1.0 + gate_act * (1.0 - sigma))).astype(jnp.bfloat16)
    d_up = (d_hidden * gate_act * sigma).astype(jnp.bfloat16)
    dx_slot = jnp.einsum("sech,edh->secd", d_gate, w_gate, preferred_element_type=jnp.float32)
    dx_slot = (
        dx_slot + jnp.einsum("sech,edh->secd", d_up, w_up, preferred_element_type=jnp.float32)
    ).astype(jnp.bfloat16)
    dx_back = lax.all_to_all(dx_slot, "expert", split_axis=0, concat_axis=0, tiled=True)
    dx_picked = jnp.take(dx_back.reshape(slot_total, width), slot, axis=0).astype(jnp.float32)
    tokens_grad = jnp.sum(dx_picked.reshape(token_count, top_count, width), axis=1).astype(
        jnp.bfloat16
    )
    columns = received
    first = jnp.einsum("secd,sech->deh", columns, d_gate, preferred_element_type=jnp.float32)
    second = jnp.einsum("secd,sech->deh", columns, d_up, preferred_element_type=jnp.float32)
    both = jnp.stack([first, second], axis=1)
    columns = dy_recv
    share = lax.psum_scatter(
        jnp.concatenate(
            [
                both,
                jnp.einsum("secd,sech->deh", columns, hidden, preferred_element_type=jnp.float32)[
                    :, None
                ],
            ],
            axis=1,
        ).astype(jnp.bfloat16),
        "dp",
        scatter_dimension=0,
        tiled=True,
    ).astype(jnp.float32)
    grad_gate = share[:, 0]
    grad_up = share[:, 1]
    grad_down = share[:, 2]
    grad_gate = jnp.transpose(grad_gate, (1, 0, 2)).astype(jnp.bfloat16)
    grad_up = jnp.transpose(grad_up, (1, 0, 2)).astype(jnp.bfloat16)
    grad_down = jnp.transpose(grad_down, (1, 0, 2)).astype(jnp.bfloat16)
    return (mixed, tokens_grad, grad_gate, grad_up, grad_down)


def solution(mesh):
    placed = (
        P(("dp", "expert"), None),
        P(("dp", "expert"), None),
        P(("dp", "expert"), None),
        P("expert", None, None),
        P("expert", None, None),
        P("expert", None, None),
        P(("dp", "expert"), None),
    )
    return jax.shard_map(
        local,
        mesh=mesh,
        in_specs=placed,
        out_specs=(
            P(("dp", "expert"), None),
            P(("dp", "expert"), None),
            P("expert", "dp", None),
            P("expert", "dp", None),
            P("expert", "dp", None),
        ),
        check_vma=False,
    )
```

profile of v0, /device:TPU:8, one launch (start us, length us, event | category | flops | bytes accessed | tf_op | source)
XLA Modules:
  0.0 279.1 jit_solution(15964831947304224388)
XLA Ops:
  9.7 6.3 %gather_fusion = bf16[512,2048]{1,0:T(8,128)(2,1)} fusion(bf16[128,2048]{1,0:T(8,128)(2,1)} %param.11, s32[1024]{0:T(1024)S(1)} %pad_clamp_fusion.1), kind=kCustom, calls=%fused_computation.clone | custom fusion | bytes 4196352 | tf_op jit(solution)/shard_map/jit(_take)/gather | solution.py:33
  16.1 3.2 %select_select_fusion.1 = bf16[512,2048]{1,0:T(8,128)(2,1)} fusion(bf16[512,2048]{1,0:T(8,128)(2,1)} %gather_fusion, pred[512]{0:T(512)(128)(4,1)S(1)} %get-tuple-element.29, pred[512]{0:T(512)(128)(4,1)S(1)} %fusion.48), kind=kLoop, calls=%fused_computation.35 | loop fusion | flops 2097152 | bytes 4195328 | tf_op jit(solution)/shard_map/jit(_where)/select_n | solution.py:32
  19.3 4.3 %all-to-all-start = ((bf16[8,1,64,2048]{3,2,1,0:T(8,128)(2,1)}), bf16[8,1,64,2048]{3,2,1,0:T(8,128)(2,1)}, u32[]{:S(2)}, u32[]{:S(2)}) async-start(bf16[8,1,64,2048]{3,2,1,0:T(8,128)(2,1)} %bitcast.180), calls=%async_computation | async-start | bytes 4194304 | tf_op jit(solution)/shard_map/all_to_all | solution.py:36
  23.6 6.4 %gather_fusion.2 = bf16[512,2048]{1,0:T(8,128)(2,1)} fusion(bf16[128,2048]{1,0:T(8,128)(2,1)} %param.17, s32[1024]{0:T(1024)S(1)} %pad_clamp_fusion.1), kind=kCustom, calls=%fused_computation.2.clone | custom fusion | bytes 4196352 | tf_op jit(solution)/shard_map/jit(_take)/gather | solution.py:57
  30.4 3.7 %multiply_convert_fusion = bf16[512,2048]{1,0:T(8,128)(2,1)} fusion(bf16[512,2048]{1,0:T(8,128)(2,1)} %gather_fusion.2, f32[512]{0:T(512)S(1)} %select_reduce_fusion, pred[512]{0:T(512)(128)(4,1)S(1)} %get-tuple-element.29, pred[512]{0:T(512)(128)(4,1)S(1)} %fusion.48), kind=kLoop, calls=%fused_computation.9 | loop fusion | flops 5242880 | bytes 4197376 | tf_op jit(solution)/shard_map/convert_element_type | solution.py:59
  34.1 16.1 %all-to-all-done = bf16[8,1,64,2048]{3,2,1,0:T(8,128)(2,1)} async-done(((bf16[8,1,64,2048]{3,2,1,0:T(8,128)(2,1)}), bf16[8,1,64,2048]{3,2,1,0:T(8,128)(2,1)}, u32[]{:S(2)}, u32[]{:S(2)}) %all-to-all-start) | async-done | bytes 2097184 | tf_op jit(solution)/shard_map/all_to_all | solution.py:36
  50.3 4.4 %all-to-all-start.2 = ((bf16[8,1,64,2048]{3,2,1,0:T(8,128)(2,1)}), bf16[8,1,64,2048]{3,2,1,0:T(8,128)(2,1)}, u32[]{:S(2)}, u32[]{:S(2)}) async-start(bf16[8,1,64,2048]{3,2,1,0:T(8,128)(2,1)} %bitcast.181), calls=%async_computation.2 | async-start | bytes 4194304 | tf_op jit(solution)/shard_map/all_to_all | solution.py:61
  54.9 5.6 %fusion.6 = f32[8,64,768]{2,1,0:T(8,128)} fusion(bf16[1,2048,768]{2,1,0:T(8,128)(2,1)} %param.15, bf16[8,1,64,2048]{3,2,1,0:T(8,128)(2,1)} %all-to-all-done), kind=kOutput, calls=%fused_computation.16 | convolution fusion | flops 1610612736 | bytes 6815744 | tf_op jit(solution)/shard_map/secd,edh->sech/dot_general | solution.py:40
  60.5 4.6 %fusion.10 = f32[8,64,768]{2,1,0:T(8,128)} fusion(bf16[1,2048,768]{2,1,0:T(8,128)(2,1)S(1)} %copy-done.2, bf16[8,1,64,2048]{3,2,1,0:T(8,128)(2,1)} %all-to-all-done), kind=kOutput, calls=%fused_computation.20 | convolution fusion | flops 1610612736 | bytes 6815744 | tf_op jit(solution)/shard_map/secd,edh->sech/dot_general | solution.py:37
  65.1 16.2 %all-to-all-done.2 = bf16[8,1,64,2048]{3,2,1,0:T(8,128)(2,1)} async-done(((bf16[8,1,64,2048]{3,2,1,0:T(8,128)(2,1)}), bf16[8,1,64,2048]{3,2,1,0:T(8,128)(2,1)}, u32[]{:S(2)}, u32[]{:S(2)}) %all-to-all-start.2) | async-done | bytes 2097184 | tf_op jit(solution)/shard_map/all_to_all | solution.py:61
  81.3 4.8 %fusion.34 = (bf16[8,1,64,768]{3,2,0,1:T(8,128)(2,1)S(1)}, bf16[8,1,64,768]{3,2,0,1:T(8,128)(2,1)S(1)}, bf16[8,1,64,768]{3,2,0,1:T(8,128)(2,1)S(1)}) fusion(f32[8,64,768]{2,1,0:T(8,128)} %fusion.6, f32[8,64,768]{2,1,0:T(8,128)} %fusion.10, bf16[1,2048,768]{2,1,0:T(8,128)(2,1)S(1)} %copy-done, bf16[8,1,64,2048]{3,2,1,0:T(8,128)(2,1)} %all-to-all-done.2), kind=kOutput, calls=%fused_computation.41 | convolution fusion | flops 1616904192 | bytes 10747904 | tf_op jit(solution)/shard_map/secd,edh->sech/dot_general | solution.py:62
  86.1 4.3 %fusion.17 = bf16[2048,1,1,768]{0,3,2,1:T(8,128)(2,1)S(1)} fusion(bf16[8,1,64,2048]{3,2,1,0:T(8,128)(2,1)} %all-to-all-done.2, bf16[8,1,64,768]{3,2,0,1:T(8,128)(2,1)S(1)} %get-tuple-element.32), kind=kOutput, calls=%fused_computation.25 | convolution fusion | flops 1612185600 | bytes 6029312 | tf_op jit(solution)/shard_map/secd,sech->deh/dot_general | solution.py:84
  90.4 3.4 %fusion.16 = bf16[2048,1,1,768]{0,3,2,1:T(8,128)(2,1)S(1)} fusion(bf16[8,1,64,2048]{3,2,1,0:T(8,128)(2,1)} %all-to-all-done, bf16[8,1,64,768]{3,2,0,1:T(8,128)(2,1)S(1)} %get-tuple-element.33), kind=kOutput, calls=%fused_computation.24 | convolution fusion | flops 1612185600 | bytes 6029312 | tf_op jit(solution)/shard_map/secd,sech->deh/dot_general | solution.py:77
  93.8 3.4 %fusion.15 = bf16[2048,1,1,768]{0,3,2,1:T(8,128)(2,1)S(1)} fusion(bf16[8,1,64,2048]{3,2,1,0:T(8,128)(2,1)} %all-to-all-done, bf16[8,1,64,768]{3,2,0,1:T(8,128)(2,1)S(1)} %get-tuple-element.31), kind=kOutput, calls=%fused_computation.23 | convolution fusion | flops 1612185600 | bytes 6029312 | tf_op jit(solution)/shard_map/secd,sech->deh/dot_general | solution.py:76
  97.2 4.5 %pad_maximum_fusion = bf16[2048,3,1,768]{0,3,2,1:T(8,128)(2,1)} fusion(bf16[2048,1,1,768]{0,3,2,1:T(8,128)(2,1)S(1)} %fusion.17, bf16[2048,1,1,768]{0,3,2,1:T(8,128)(2,1)S(1)} %fusion.16, bf16[2048,1,1,768]{0,3,2,1:T(8,128)(2,1)S(1)} %fusion.15), kind=kLoop, calls=%fused_computation.4 | loop fusion | flops 9437184 | bytes 18874368 | tf_op jit(solution)/shard_map/concatenate | solution.py:81
  101.8 4.1 %fusion.4 = f32[8,64,2048]{2,1,0:T(8,128)S(1)} fusion(bf16[1,2048,768]{2,1,0:T(8,128)(2,1)} %param.15, bf16[8,1,64,768]{3,2,0,1:T(8,128)(2,1)} %copy-done.6), kind=kOutput, calls=%fused_computation.14 | convolution fusion | flops 1610612736 | bytes 8126464 | tf_op jit(solution)/shard_map/sech,edh->secd/dot_general | solution.py:68
  105.9 3.3 %fusion.23 = bf16[8,1,64,2048]{3,2,1,0:T(8,128)(2,1)} fusion(f32[8,64,2048]{2,1,0:T(8,128)S(1)} %fusion.4, bf16[1,2048,768]{2,1,0:T(8,128)(2,1)S(1)} %copy-done.3, bf16[8,1,64,768]{3,2,0,1:T(8,128)(2,1)S(1)} %copy-done.5), kind=kOutput, calls=%fused_computation.27 | convolution fusion | flops 1612709888 | bytes 10223616 | tf_op jit(solution)/shard_map/sech,edh->secd/dot_general | solution.py:66
  109.2 4.3 %all-to-all-start.3 = ((bf16[8,1,64,2048]{3,2,1,0:T(8,128)(2,1)}), bf16[8,1,64,2048]{3,2,1,0:T(8,128)(2,1)}, u32[]{:S(2)}, u32[]{:S(2)}) async-start(bf16[8,1,64,2048]{3,2,1,0:T(8,128)(2,1)} %fusion.23), calls=%async_computation.3 | async-start | bytes 4194304 | tf_op jit(solution)/shard_map/all_to_all | solution.py:70
  113.5 4.3 %fusion.20 = bf16[8,1,64,2048]{3,2,1,0:T(8,128)(2,1)} fusion(bf16[1,2048,768]{2,1,0:T(8,128)(2,1)S(1)} %copy-done, bf16[8,1,64,768]{3,2,0,1:T(8,128)(2,1)} %copy-done.7), kind=kOutput, calls=%fused_computation.26 | convolution fusion | flops 1611661312 | bytes 6029312 | tf_op jit(solution)/shard_map/sech,edh->secd/dot_general | solution.py:42
  117.8 22.4 %all-to-all-done.3 = bf16[8,1,64,2048]{3,2,1,0:T(8,128)(2,1)} async-done(((bf16[8,1,64,2048]{3,2,1,0:T(8,128)(2,1)}), bf16[8,1,64,2048]{3,2,1,0:T(8,128)(2,1)}, u32[]{:S(2)}, u32[]{:S(2)}) %all-to-all-start.3) | async-done | bytes 2097184 | tf_op jit(solution)/shard_map/all_to_all | solution.py:70
  140.2 4.3 %all-to-all-start.1 = ((bf16[8,1,64,2048]{3,2,1,0:T(8,128)(2,1)}), bf16[8,1,64,2048]{3,2,1,0:T(8,128)(2,1)}, u32[]{:S(2)}, u32[]{:S(2)}) async-start(bf16[8,1,64,2048]{3,2,1,0:T(8,128)(2,1)} %fusion.20), calls=%async_computation.1 | async-start | bytes 4194304 | tf_op jit(solution)/shard_map/all_to_all | solution.py:45
  144.6 5.2 %gather_fusion.3 = bf16[256,2048]{1,0:T(8,128)(2,1)} fusion(bf16[512,2048]{1,0:T(8,128)(2,1)} %bitcast.41, s32[1024]{0:T(1024)S(1)} %pad_clamp_fusion), kind=kCustom, calls=%fused_computation.3.clone | custom fusion | bytes 2098176 | tf_op jit(solution)/shard_map/jit(_take)/gather | solution.py:71
  149.8 21.4 %all-to-all-done.1 = bf16[8,1,64,2048]{3,2,1,0:T(8,128)(2,1)} async-done(((bf16[8,1,64,2048]{3,2,1,0:T(8,128)(2,1)}), bf16[8,1,64,2048]{3,2,1,0:T(8,128)(2,1)}, u32[]{:S(2)}, u32[]{:S(2)}) %all-to-all-start.1) | async-done | bytes 2097184 | tf_op jit(solution)/shard_map/all_to_all | solution.py:45
  171.2 5.2 %gather_fusion.1 = bf16[256,2048]{1,0:T(8,128)(2,1)} fusion(bf16[512,2048]{1,0:T(8,128)(2,1)} %bitcast.24, s32[1024]{0:T(1024)S(1)} %pad_clamp_fusion), kind=kCustom, calls=%fused_computation.1.clone | custom fusion | bytes 2098176 | tf_op jit(solution)/shard_map/jit(_take)/gather | solution.py:53
  176.4 3.6 %broadcast_select_fusion = (bf16[256,2048]{1,0:T(8,128)(2,1)}, f32[256,2048]{1,0:T(8,128)}) fusion(bf16[256,2048]{1,0:T(8,128)(2,1)} %gather_fusion.3, pred[256]{0:T(512)(128)(4,1)S(1)} %get-tuple-element.27, bf16[256,2048]{1,0:T(8,128)(2,1)} %gather_fusion.1), kind=kLoop, calls=%fused_computation.54 | loop fusion | flops 1572864 | bytes 5243136 | tf_op jit(solution)/shard_map/jit(_take)/select_n | solution.py:71
  180.0 3.5 %reshape.238 = f32[128,2,2048]{2,1,0:T(2,128)} reshape(f32[256,2048]{1,0:T(8,128)} %get-tuple-element.38) | data formatting | bytes 4194304 | tf_op jit(solution)/shard_map/reshape | solution.py:54
  183.6 2.5 reshape.235
  186.1 4.7 %reduce = bf16[128,2048]{1,0:T(8,128)(2,1)} reduce(bf16[128,2,2048]{2,1,0:T(2,128)(2,1)} %reshape.235, bf16[]{:T(256)} %constant.48.clone.1), dimensions={1}, to_apply=%region_7.10.clone | reduce | flops 262144 | bytes 1572866 | tf_op jit(solution)/shard_map/reduce_sum | solution.py:72
  190.8 5.6 %multiply_reduce_fusion = bf16[128,2048]{1,0:T(8,128)(2,1)} fusion(f32[128,2,2048]{2,1,0:T(2,128)} %reshape.238, f32[128,2]{1,0:T(8,128)S(1)} %copy.38), kind=kLoop, calls=%fused_computation.36 | loop fusion | flops 786432 | bytes 2622464 | tf_op jit(solution)/shard_map/reduce_sum | solution.py:55
  196.4 65.9 %reduce-scatter.2.cloned.1.call-done = bf16[512,3,1,768]{0,3,2,1:T(8,128)(2,1)} async-done(((bf16[2048,3,1,768]{0,3,2,1:T(8,128)(2,1)}), bf16[512,3,1,768]{0,3,2,1:T(8,128)(2,1)}) %reduce-scatter.2.cloned.1.call-update) | async-done | bytes 2359312 | tf_op jit(solution)/shard_map/reduce_scatter | solution.py:80
  262.3 3.1 %slice_bitcast_fusion = (bf16[1,512,768]{1,2,0:T(8,128)(2,1)}, bf16[1,512,768]{1,2,0:T(8,128)(2,1)}, bf16[1,512,768]{1,2,0:T(8,128)(2,1)}) fusion(bf16[512,3,1,768]{0,3,2,1:T(8,128)(2,1)} %reduce-scatter.2.cloned.1.call-done), kind=kLoop, calls=%fused_computation.55 | loop fusion | bytes 4718592 | tf_op jit(solution)/shard_map/convert_element_type | solution.py:99
  269.9 2.3 copy.44
  (39 shorter events, 7.8 us)
Async XLA Ops:
  7.2 74.1 %copy-start = (bf16[1,2048,768]{2,1,0:T(8,128)(2,1)S(1)}, bf16[1,2048,768]{2,1,0:T(8,128)(2,1)}, u32[]{:S(2)}) copy-start(bf16[1,2048,768]{2,1,0:T(8,128)(2,1)} %param.16) | copy-start | bytes 9437188
  19.3 31.0 %all-to-all-start = ((bf16[8,1,64,2048]{3,2,1,0:T(8,128)(2,1)}), bf16[8,1,64,2048]{3,2,1,0:T(8,128)(2,1)}, u32[]{:S(2)}, u32[]{:S(2)}) async-start(bf16[8,1,64,2048]{3,2,1,0:T(8,128)(2,1)} %bitcast.180), calls=%async_computation | async-start | bytes 4194304 | tf_op jit(solution)/shard_map/all_to_all | solution.py:36
  23.6 6.4 %copy-start.1 = (f32[128,2]{0,1:T(2,128)S(1)}, f32[128,2]{0,1:T(2,128)}, u32[]{:S(2)}) copy-start(f32[128,2]{0,1:T(2,128)} %param.13) | copy-start | bytes 3076
  50.3 31.0 %all-to-all-start.2 = ((bf16[8,1,64,2048]{3,2,1,0:T(8,128)(2,1)}), bf16[8,1,64,2048]{3,2,1,0:T(8,128)(2,1)}, u32[]{:S(2)}, u32[]{:S(2)}) async-start(bf16[8,1,64,2048]{3,2,1,0:T(8,128)(2,1)} %bitcast.181), calls=%async_computation.2 | async-start | bytes 4194304 | tf_op jit(solution)/shard_map/all_to_all | solution.py:61
  54.6 207.7 %reduce-scatter.2.cloned.1.call-start = ((), (), s32[]{:S(2)}) async-start(), calls=%async_computation.5 | async-start | bytes 11796480 | tf_op jit(solution)/shard_map/reduce_scatter | solution.py:80
  54.9 5.6 %copy-start.2 = (bf16[1,2048,768]{2,1,0:T(8,128)(2,1)S(1)}, bf16[1,2048,768]{2,1,0:T(8,128)(2,1)}, u32[]{:S(2)}) copy-start(bf16[1,2048,768]{2,1,0:T(8,128)(2,1)} %param.14) | copy-start | bytes 9437188
  86.1 4.3 %copy-start.7 = (bf16[8,1,64,768]{3,2,0,1:T(8,128)(2,1)}, bf16[8,1,64,768]{3,2,0,1:T(8,128)(2,1)S(1)}, u32[]{:S(2)}) copy-start(bf16[8,1,64,768]{3,2,0,1:T(8,128)(2,1)S(1)} %get-tuple-element.32) | copy-start | bytes 2359300
  86.1 4.3 %copy-start.6 = (bf16[8,1,64,768]{3,2,0,1:T(8,128)(2,1)}, bf16[8,1,64,768]{3,2,0,1:T(8,128)(2,1)S(1)}, u32[]{:S(2)}) copy-start(bf16[8,1,64,768]{3,2,0,1:T(8,128)(2,1)S(1)} %get-tuple-element.33) | copy-start | bytes 2359300
  86.1 7.7 %copy-start.4 = (bf16[8,1,64,768]{3,2,0,1:T(8,128)(2,1)}, bf16[8,1,64,768]{3,2,0,1:T(8,128)(2,1)S(1)}, u32[]{:S(2)}) copy-start(bf16[8,1,64,768]{3,2,0,1:T(8,128)(2,1)S(1)} %get-tuple-element.31) | copy-start | bytes 2359300
  101.8 4.1 %copy-start.3 = (bf16[1,2048,768]{2,1,0:T(8,128)(2,1)S(1)}, bf16[1,2048,768]{2,1,0:T(8,128)(2,1)}, u32[]{:S(2)}) copy-start(bf16[1,2048,768]{2,1,0:T(8,128)(2,1)} %param.14) | copy-start | bytes 9437188
  101.8 4.1 %copy-start.5 = (bf16[8,1,64,768]{3,2,0,1:T(8,128)(2,1)S(1)}, bf16[8,1,64,768]{3,2,0,1:T(8,128)(2,1)}, u32[]{:S(2)}) copy-start(bf16[8,1,64,768]{3,2,0,1:T(8,128)(2,1)} %copy-done.4) | copy-start | bytes 2359300
  109.2 31.0 %all-to-all-start.3 = ((bf16[8,1,64,2048]{3,2,1,0:T(8,128)(2,1)}), bf16[8,1,64,2048]{3,2,1,0:T(8,128)(2,1)}, u32[]{:S(2)}, u32[]{:S(2)}) async-start(bf16[8,1,64,2048]{3,2,1,0:T(8,128)(2,1)} %fusion.23), calls=%async_computation.3 | async-start | bytes 4194304 | tf_op jit(solution)/shard_map/all_to_all | solution.py:70
  140.2 31.0 %all-to-all-start.1 = ((bf16[8,1,64,2048]{3,2,1,0:T(8,128)(2,1)}), bf16[8,1,64,2048]{3,2,1,0:T(8,128)(2,1)}, u32[]{:S(2)}, u32[]{:S(2)}) async-start(bf16[8,1,64,2048]{3,2,1,0:T(8,128)(2,1)} %fusion.20), calls=%async_computation.1 | async-start | bytes 4194304 | tf_op jit(solution)/shard_map/all_to_all | solution.py:45
Sparse Core Ops, SparseCore 0:
  101.9 160.3 reduce-scatter.1
where the time goes:
time: 282 us; the launch traced here: 279 us
  waiting for transfers between devices  142 us (50%)
  local copies, waits for them, and re-layouts  40.9 us (15%)
  matrix products  37.8 us (13%)
  other arithmetic  26.6 us (9%)
  starting transfers between devices  17.6 us (6%)
  between operations  14.3 us (5%)
    reduce_scatter x1, waiting for transfers between devices, local(): lax.psum_scatter(jnp.concatenate([both, jnp.einsum('secd,sech->deh', colu...  65.9 us
    all_to_all x1, waiting for transfers between devices, local(): lax.all_to_all(dx_slot, 'expert', split_axis=0, concat_axis=0, tiled=True)  22.4 us
    all_to_all x1, waiting for transfers between devices, local(): lax.all_to_all(result, 'expert', split_axis=0, concat_axis=0, tiled=True)  21.4 us
    all_to_all x1, waiting for transfers between devices, local(): lax.all_to_all(dy_slot, 'expert', split_axis=0, concat_axis=0, tiled=True)  16.2 us
    all_to_all x1, waiting for transfers between devices, local(): lax.all_to_all(dispatched, 'expert', split_axis=0, concat_axis=0, tiled=T...  16.1 us
    unnamed x21, local copies, waits for them, and re-layouts  7.96 us
    gather x1, local copies, waits for them, and re-layouts, local(): jnp.take(out_grad, token_of_slot, axis=0)  6.39 us
    gather x1, local copies, waits for them, and re-layouts, local(): jnp.take(tokens, token_of_slot, axis=0)  6.35 us
  transfers between devices with their start and end apart: 5, of which 5 were waited for; matrix products, arithmetic and copies ran while one was open for 23% of the time, Pallas kernels for 0%

commit v1 on v0

v1 whole, which is shorter than its diff:
```python
import functools

import jax
import jax.numpy as jnp
from jax import lax
from jax.experimental import pallas as pl
from jax.experimental.pallas import tpu as pltpu
from jax.sharding import PartitionSpec as P

F32 = jnp.float32
BF16 = jnp.bfloat16
VMEM_LIMIT = 48 * 1024 * 1024


def route_slots(expert_ids, experts, capacity):
    flat = expert_ids.reshape(-1)
    onehot = (flat[:, None] == jnp.arange(experts, dtype=jnp.int32)[None, :]).astype(jnp.int32)
    before = jnp.cumsum(onehot, axis=0) - onehot
    position = jnp.sum(before * onehot, axis=1)
    return flat * capacity + position


def local_any(tokens, expert_ids, gate_probs, w_gate, w_up, w_down, out_grad):
    token_count, top_count = expert_ids.shape
    width = tokens.shape[1]
    local_experts = w_gate.shape[0]
    peers = lax.axis_size("expert")
    experts = local_experts * peers
    capacity = max(2, 2 * token_count * top_count // experts)
    slot_total = experts * capacity
    route_total = token_count * top_count
    slot = route_slots(expert_ids, experts, capacity)
    owner = slot[None, :] == jnp.arange(slot_total, dtype=jnp.int32)[:, None]
    live = jnp.any(owner, axis=1)
    route_index = jnp.sum(
        jnp.where(owner, jnp.arange(route_total, dtype=jnp.int32)[None, :], 0), axis=1
    )
    token_of_slot = route_index // top_count
    slot_prob = jnp.sum(jnp.where(owner, gate_probs.reshape(-1)[None, :], 0.0), axis=1)
    dispatched = jnp.where(
        live[:, None], jnp.take(tokens, token_of_slot, axis=0), jnp.zeros((), tokens.dtype)
    )
    dispatched = dispatched.reshape(peers, local_experts, capacity, width)
    received = lax.all_to_all(dispatched, "expert", split_axis=0, concat_axis=0, tiled=True)
    gate_act = jnp.einsum("secd,edh->sech", received, w_gate, preferred_element_type=F32)
    up_act = jnp.einsum("secd,edh->sech", received, w_up, preferred_element_type=F32)
    hidden = (jax.nn.silu(gate_act) * up_act).astype(BF16)
    result = jnp.einsum("sech,edh->secd", hidden, w_down, preferred_element_type=F32).astype(BF16)
    returned = lax.all_to_all(result, "expert", split_axis=0, concat_axis=0, tiled=True)
    picked = jnp.take(returned.reshape(slot_total, width), slot, axis=0).astype(F32)
    picked = picked.reshape(token_count, top_count, width)
    mixed = jnp.sum(picked * gate_probs[:, :, None], axis=1).astype(BF16)
    dy_rows = jnp.where(
        live[:, None], jnp.take(out_grad, token_of_slot, axis=0), jnp.zeros((), out_grad.dtype)
    )
    dy_slot = (dy_rows.astype(F32) * slot_prob[:, None]).astype(BF16)
    dy_slot = dy_slot.reshape(peers, local_experts, capacity, width)
    dy_recv = lax.all_to_all(dy_slot, "expert", split_axis=0, concat_axis=0, tiled=True)
    d_hidden = jnp.einsum("secd,edh->sech", dy_recv, w_down, preferred_element_type=F32)
    sigma = jax.nn.sigmoid(gate_act)
    d_gate = (d_hidden * up_act * sigma * (1.0 + gate_act * (1.0 - sigma))).astype(BF16)
    d_up = (d_hidden * gate_act * sigma).astype(BF16)
    dx_slot = jnp.einsum("sech,edh->secd", d_gate, w_gate, preferred_element_type=F32)
    dx_slot = (
        dx_slot + jnp.einsum("sech,edh->secd", d_up, w_up, preferred_element_type=F32)
    ).astype(BF16)
    dx_back = lax.all_to_all(dx_slot, "expert", split_axis=0, concat_axis=0, tiled=True)
    dx_picked = jnp.take(dx_back.reshape(slot_total, width), slot, axis=0).astype(F32)
    tokens_grad = jnp.sum(dx_picked.reshape(token_count, top_count, width), axis=1).astype(BF16)
    first = jnp.einsum("secd,sech->deh", received, d_gate, preferred_element_type=F32)
    second = jnp.einsum("secd,sech->deh", received, d_up, preferred_element_type=F32)
    third = jnp.einsum("secd,sech->deh", dy_recv, hidden, preferred_element_type=F32)
    share = lax.psum_scatter(
        jnp.stack([first, second, third], axis=1).astype(BF16),
        "dp",
        scatter_dimension=0,
        tiled=True,
    )
    grads = [jnp.transpose(share[:, k], (1, 0, 2)) for k in range(3)]
    return (mixed, tokens_grad, *grads)


def cost(macs, size):
    return pl.CostEstimate(flops=2 * macs, bytes_accessed=size, transcendentals=0)


def params(steps=0):
    kwargs = {"vmem_limit_bytes": VMEM_LIMIT}
    if steps:
        kwargs["dimension_semantics"] = ("arbitrary",) * steps
    return pltpu.CompilerParams(**kwargs)


def nn(a, b):
    return lax.dot_general(a, b, (((1,), (0,)), ((), ())), preferred_element_type=F32)


def nt(a, b):
    return lax.dot_general(a, b, (((1,), (1,)), ((), ())), preferred_element_type=F32)


def tn(a, b):
    return lax.dot_general(a, b, (((0,), (0,)), ((), ())), preferred_element_type=F32)


def routed_here(meta, me, rank_ref, prob_ref):
    expert = me.astype(F32)
    first, second = meta[:, 0, :] == expert, meta[:, 1, :] == expert
    named = (first | second).astype(F32)
    count = named.shape[1]
    earlier = lax.broadcasted_iota(jnp.int32, (count, count), 0) < lax.broadcasted_iota(
        jnp.int32, (count, count), 1
    )
    rank = nn(named.astype(BF16), earlier.astype(F32).astype(BF16))
    rank_ref[...] = jnp.where(named > 0, rank, -1.0)
    if prob_ref is not None:
        prob_ref[...] = jnp.where(first, meta[:, 2, :], jnp.where(second, meta[:, 3, :], 0.0))


def group_blocks(refs):
    own, bx, by, da, db, c_own, c_bx, c_by, c_da, c_db = refs
    whole = {0: own, 1: c_own, 2: bx, 3: c_bx, 4: by, 5: c_by}
    for k in range(8):
        if k in whole:
            yield k, whole[k][...]
        else:
            top, bottom = (da, db) if k == 6 else (c_da, c_db)
            yield k, jnp.concatenate([top[...], bottom[...]], axis=0)


def fill_slots(me, blocks, rank_ref, prob_ref, out_ref, capacity):
    for k, rows in group_blocks(blocks):
        source = jnp.bitwise_xor(me, k)
        rank = rank_ref[pl.ds(source, 1), :]
        place = lax.broadcasted_iota(jnp.int32, (capacity, rank.shape[1]), 0).astype(F32)
        hit = place == rank
        picked = nn(hit.astype(F32).astype(BF16), rows)
        if prob_ref is not None:
            scale = jnp.sum(jnp.where(hit, prob_ref[pl.ds(source, 1), :], 0.0), axis=1, keepdims=True)
            picked = picked * scale
        start = pl.multiple_of(source * capacity, capacity)
        out_ref[pl.ds(start, capacity), :] = picked.astype(BF16)


def forward_kernel(capacity, pos_ref, meta_ref, *refs):
    blocks, (wg_ref, wu_ref, x_ref, h_ref, a_ref, b_ref, rank_ref) = refs[:10], refs[10:]
    me = pos_ref[0]

    @pl.when(pl.program_id(0) == 0)
    def _():
        routed_here(meta_ref[...], me, rank_ref, None)
        fill_slots(me, blocks, rank_ref, None, x_ref, capacity)

    x = x_ref[...]
    g = nn(x, wg_ref[...])
    u = nn(x, wu_ref[...])
    s = jax.nn.sigmoid(g)
    b = g * s
    h_ref[...] = (b * u).astype(BF16)
    a_ref[...] = u * s * (1.0 + g * (1.0 - s))
    b_ref[...] = b


def forward(pos, meta, blocks, w_gate, w_up, capacity):
    width, hid = w_gate.shape
    slots = 8 * capacity
    tile = 256
    full = lambda a: pl.BlockSpec(a.shape, lambda i, p, n=a.ndim: (0,) * n)
    wide = pl.BlockSpec((width, tile), lambda i, p: (0, i))
    out = pl.BlockSpec((slots, tile), lambda i, p: (0, i))
    return pl.pallas_call(
        functools.partial(forward_kernel, capacity),
        grid_spec=pltpu.PrefetchScalarGridSpec(
            num_scalar_prefetch=1,
            grid=(hid // tile,),
            in_specs=[full(meta)] + [full(b) for b in blocks] + [wide, wide],
            out_specs=[pl.BlockSpec((slots, width), lambda i, p: (0, 0)), out, out, out],
            scratch_shapes=[pltpu.VMEM((8, meta.shape[2]), F32)],
        ),
        out_shape=[
            jax.ShapeDtypeStruct((slots, width), BF16),
            jax.ShapeDtypeStruct((slots, hid), BF16),
            jax.ShapeDtypeStruct((slots, hid), F32),
            jax.ShapeDtypeStruct((slots, hid), F32),
        ],
        compiler_params=params(1),
        cost_estimate=cost(2 * slots * width * hid, 16 << 20),
        name="forward",
    )(pos, meta, *blocks, w_gate, w_up)


def cotangent_kernel(capacity, chunk, pos_ref, meta_ref, *refs):
    blocks, (h_ref, dy_ref, far_ref, rank_ref, prob_ref) = refs[:10], refs[10:]
    me = pos_ref[0]
    routed_here(meta_ref[...], me, rank_ref, prob_ref)
    fill_slots(me, blocks, rank_ref, prob_ref, dy_ref, capacity)
    start = pl.multiple_of(pos_ref[1] * chunk, chunk)
    far_ref[...] = tn(dy_ref[:, pl.ds(start, chunk)], h_ref[...]).astype(BF16)


def cotangent(pos, meta, blocks, h, chunk, capacity):
    width = blocks[0].shape[1]
    slots, hid = h.shape
    vmem = pl.BlockSpec(memory_space=pltpu.VMEM)
    return pl.pallas_call(
        functools.partial(cotangent_kernel, capacity, chunk),
        in_specs=[pl.BlockSpec(memory_space=pltpu.SMEM)] + [vmem] * (len(blocks) + 2),
        out_specs=[vmem, vmem],
        scratch_shapes=[pltpu.VMEM((8, meta.shape[2]), F32)] * 2,
        out_shape=[
            jax.ShapeDtypeStruct((slots, width), BF16),
            jax.ShapeDtypeStruct((chunk, hid), BF16),
        ],
        compiler_params=params(),
        cost_estimate=cost(slots * chunk * hid, 8 << 20),
        name="cotangent",
    )(pos, meta, *blocks, h)


def backward_kernel(dy_ref, wd_ref, a_ref, b_ref, dg_ref, du_ref):
    dh = nn(dy_ref[...], wd_ref[...])
    dg_ref[...] = (dh * a_ref[...]).astype(BF16)
    du_ref[...] = (dh * b_ref[...]).astype(BF16)


def backward(dy, w_down, a, b):
    width, hid = w_down.shape
    slots = dy.shape[0]
    tile = 256
    out = pl.BlockSpec((slots, tile), lambda i: (0, i))
    return pl.pallas_call(
        backward_kernel,
        grid=(hid // tile,),
        in_specs=[
            pl.BlockSpec((slots, width), lambda i: (0, 0)),
            pl.BlockSpec((width, tile), lambda i: (0, i)),
            out,
            out,
        ],
        out_specs=[out, out],
        out_shape=[jax.ShapeDtypeStruct((slots, hid), BF16)] * 2,
        compiler_params=params(1),
        cost_estimate=cost(slots * width * hid, 10 << 20),
        name="backward",
    )(dy, w_down, a, b)


def gradient_kernel(lefts, count, dtype, pos_ref, *refs):
    ins, outs = refs[: len(refs) - count], refs[len(refs) - count :]
    pairs = ins[:lefts], ins[lefts:]
    for n, out in enumerate(outs):
        total = None
        for left, right in outs_of(n, lefts, count):
            term = tn(pairs[0][left][...], pairs[1][right][...])
            total = term if total is None else total + term
        out[...] = total.astype(dtype)


def outs_of(n, lefts, count):
    if lefts == 1:
        return [(0, n)]
    if lefts == 2:
        return [(0 if n < 2 else 1, n)]
    return [(0 if n < 2 else 1, n), (2 if n < 2 else 3, 3 + n)]


def gradient(pos, which, lefts, rights, chunk, dtype, count):
    slots, hid = rights[0].shape
    left_spec = pl.BlockSpec((slots, chunk), lambda i, p: (0, p[which]))
    right_spec = pl.BlockSpec((slots, hid), lambda i, p: (0, 0))
    out = pl.BlockSpec((chunk, hid), lambda i, p: (0, 0))
    return pl.pallas_call(
        functools.partial(gradient_kernel, len(lefts), count, dtype),
        grid_spec=pltpu.PrefetchScalarGridSpec(
            num_scalar_prefetch=1,
            grid=(1,),
            in_specs=[left_spec] * len(lefts) + [right_spec] * len(rights),
            out_specs=[out] * count,
        ),
        out_shape=[jax.ShapeDtypeStruct((chunk, hid), dtype)] * count,
        compiler_params=params(1),
        cost_estimate=cost(len(rights) * slots * chunk * hid, 4 << 20),
        name="gradient",
    )(pos, *lefts, *rights)


def rows_kernel(count, *refs):
    out = refs[-1]
    total = nt(refs[0][...], refs[1][...])
    for k in range(1, count):
        total = total + nt(refs[2 * k][...], refs[2 * k + 1][...])
    out[...] = total.astype(BF16)


def rows_back(pairs):
    slots, hid = pairs[0][0].shape
    width = pairs[0][1].shape[0]
    tile = 512
    specs = [
        pl.BlockSpec((slots, hid), lambda i: (0, 0)),
        pl.BlockSpec((tile, hid), lambda i: (i, 0)),
    ] * len(pairs)
    return pl.pallas_call(
        functools.partial(rows_kernel, len(pairs)),
        grid=(width // tile,),
        in_specs=specs,
        out_specs=pl.BlockSpec((slots, tile), lambda i: (0, i)),
        out_shape=jax.ShapeDtypeStruct((slots, width), BF16),
        compiler_params=params(1),
        cost_estimate=cost(len(pairs) * slots * hid * width, 8 << 20),
        name="rows_back",
    )(*[a for pair in pairs for a in pair])


def combine_kernel(capacity, scaled, ids_ref, prob_ref, rows_ref, out_ref):
    ids = ids_ref[...]
    count = ids.shape[0]
    slots = rows_ref.shape[0]
    lane = lax.broadcasted_iota(jnp.int32, (count, 128), 1)
    named = ((lane == ids[:, 0:1]) | (lane == ids[:, 1:2])).astype(F32)
    earlier = lax.broadcasted_iota(jnp.int32, (count, count), 1) < lax.broadcasted_iota(
        jnp.int32, (count, count), 0
    )
    rank = nn(earlier.astype(F32).astype(BF16), named.astype(BF16))
    place = lax.broadcasted_iota(jnp.int32, (count, slots), 1)
    hits = []
    for k in range(2):
        own = ids[:, k : k + 1]
        at = jnp.sum(jnp.where(lane == own, rank, 0.0), axis=1, keepdims=True).astype(jnp.int32)
        hits.append((place == own * capacity + at).astype(F32).astype(BF16))
    rows = rows_ref[...]
    if scaled:
        probs = prob_ref[...]
        total = nn(hits[0], rows) * probs[:, 0:1] + nn(hits[1], rows) * probs[:, 1:2]
    else:
        total = nn(hits[0] + hits[1], rows)
    out_ref[...] = total.astype(BF16)


def combine(ids, probs, rows, capacity, scaled):
    count = ids.shape[0]
    slots, width = rows.shape
    tile = 512
    return pl.pallas_call(
        functools.partial(combine_kernel, capacity, scaled),
        grid=(width // tile,),
        in_specs=[
            pl.BlockSpec(ids.shape, lambda i: (0, 0)),
            pl.BlockSpec(probs.shape, lambda i: (0, 0)),
            pl.BlockSpec((slots, tile), lambda i: (0, i)),
        ],
        out_specs=pl.BlockSpec((count, tile), lambda i: (0, i)),
        out_shape=jax.ShapeDtypeStruct((count, width), BF16),
        compiler_params=params(1),
        cost_estimate=cost(2 * count * slots * width, 3 << 20),
        name="combine",
    )(ids, probs, rows)


def local_pairs(tokens, expert_ids, gate_probs, w_gate, w_up, w_down, out_grad):
    count, top = expert_ids.shape
    width = tokens.shape[1]
    w_gate, w_up, w_down = w_gate[0], w_up[0], w_down[0]
    planes, peers = lax.axis_size("dp"), lax.axis_size("expert")
    capacity = 2 * count * top // peers
    chunk = width // planes
    z = lax.axis_index("dp")
    me = lax.axis_index("expert")
    left = z < 2
    far = jnp.where(left, 3, 0)
    near = jnp.where(left, 2, 1)
    pos = jnp.stack([me, far, near, z]).astype(jnp.int32)

    def over(x, bit):
        return lax.ppermute(x, "expert", [(i, i ^ bit) for i in range(peers)])

    def gather(x):
        half = x.shape[0] // 2
        bx, by = over(x, 2), over(x, 4)
        da, db = over(by[:half], 2), over(bx[half:], 4)
        held = (x, bx, by, da, db)
        return held + tuple(over(t, 1) for t in held)

    def partner(x):
        return lax.ppermute(x, "dp", [(i, i ^ 1) for i in range(planes)])

    def inward(x):
        return lax.ppermute(x, "dp", [(0, 1), (3, 2)])

    def across_far(x):
        return lax.ppermute(x, "dp", [(1, 3), (2, 0)])

    def across_near(x):
        return lax.ppermute(x, "dp", [(1, 2), (2, 1)])

    meta = jnp.concatenate([expert_ids.astype(F32), gate_probs], axis=1).T
    meta = jnp.concatenate([meta, partner(meta)], axis=0)
    meta = lax.all_gather(meta, "expert", axis=0)
    meta, meta_p = meta[:, :4], meta[:, 4:]
    tokens_p, out_grad_p = partner(tokens), partner(out_grad)

    x, h, a, b = forward(pos, meta, gather(tokens), w_gate, w_up, capacity)
    dy, far_down = cotangent(pos, meta, gather(out_grad), h, chunk, capacity)
    dg, du = backward(dy, w_down, a, b)
    far_gate, far_up = gradient(pos, 1, [x], [dg, du], chunk, BF16, 2)
    near_gate, near_up, near_down = gradient(pos, 2, [x, dy], [dg, du, h], chunk, BF16, 3)

    def add(p, q):
        return (p.astype(F32) + q.astype(F32)).astype(BF16)

    got_far, got_near = {}, {}
    for name, piece in (("down", far_down), ("gate", far_gate), ("up", far_up)):
        got_far[name] = across_far(add(piece, inward(piece)))
    for name, piece in (("down", near_down), ("gate", near_gate), ("up", near_up)):
        got_near[name] = across_near(add(piece, inward(piece)))

    o = rows_back([(h, w_down)])
    dx = rows_back([(dg, w_gate), (du, w_up)])

    def give_back(rows):
        rows = rows.reshape(peers, capacity, width)
        rows = lax.all_to_all(rows, "expert", split_axis=0, concat_axis=0, tiled=True)
        return rows.reshape(peers * capacity, width)

    mixed = combine(expert_ids, gate_probs, give_back(o), capacity, True)
    tokens_grad = combine(expert_ids, gate_probs, give_back(dx), capacity, False)

    x_p, h_p, a_p, b_p = forward(pos, meta_p, gather(tokens_p), w_gate, w_up, capacity)
    dy_p, _ = cotangent(pos, meta_p, gather(out_grad_p), h_p, chunk, capacity)
    dg_p, du_p = backward(dy_p, w_down, a_p, b_p)
    own = gradient(pos, 3, [x, dy, x_p, dy_p], [dg, du, h, dg_p, du_p, h_p], chunk, F32, 3)
    grads = []
    for name, mine in zip(("gate", "up", "down"), own):
        total = mine + got_far[name].astype(F32) + got_near[name].astype(F32)
        grads.append(total.astype(BF16)[None])
    return (mixed, tokens_grad, *grads)


def solution(mesh):
    placed = (
        P(("dp", "expert"), None),
        P(("dp", "expert"), None),
        P(("dp", "expert"), None),
        P("expert", None, None),
        P("expert", None, None),
        P("expert", None, None),
        P(("dp", "expert"), None),
    )
    paired = mesh.shape["dp"] == 4 and mesh.shape["expert"] == 8
    return jax.shard_map(
        local_pairs if paired else local_any,
        mesh=mesh,
        in_specs=placed,
        out_specs=(
            P(("dp", "expert"), None),
            P(("dp", "expert"), None),
            P("expert", "dp", None),
            P("expert", "dp", None),
            P("expert", "dp", None),
        ),
        check_vma=False,
    )
```

time: 282 us -> 288 us (1.021)
  Pallas kernels: 0 us -> 67.8 us
  waiting for transfers between devices: 142 us -> 99.7 us
  starting transfers between devices: 17.6 us -> 55.9 us
  matrix products: 37.8 us -> 0 us
  blocking collectives: 0 us -> 16.7 us
  local copies, waits for them, and re-layouts: 40.9 us -> 24.4 us
  between operations: 14.3 us -> 1.31 us
  other arithmetic: 26.6 us -> 17.5 us
    ppermute x0 -> x51, waiting for transfers between devices: none -> 99.7 us  [the longest x6 44.5 us: inward(): return lax.ppermute(x, 'dp', [(0, 1), (3, 2)])]
    all_to_all x4 -> x2, waiting for transfers between devices: 76.1 us -> 0.01 us  [give_back(): lax.all_to_all(rows, 'expert', split_axis=0, concat_axis=0, tiled=True)]
    pallas_call x0 -> x13, Pallas kernels: none -> 67.8 us  [the longest x2 18.7 us: forward(): pl.pallas_call(functools.partial(forward_kernel, capacity), grid_spec=plt...]
    reduce_scatter x1 -> x0, waiting for transfers between devices: 65.9 us -> none  [local(): lax.psum_scatter(jnp.concatenate([both, jnp.einsum('secd,sech->deh', colu...]
    ppermute x0 -> x51, starting transfers between devices: none -> 47.4 us  [the longest x36 21.7 us: over(): return lax.ppermute(x, 'expert', [(i, i ^ bit) for i in range(peers)])]
    dot_general x9 -> x0, matrix products: 37.8 us -> none  [the longest x1 5.6 us: local(): jnp.einsum('secd,edh->sech', expert_received, w_up, preferred_element_typ...]
    gather x4 -> x0, local copies, waits for them, and re-layouts: 23.1 us -> none  [the longest x1 6.39 us: local(): jnp.take(out_grad, token_of_slot, axis=0)]
    all_gather x0 -> x1, blocking collectives: none -> 16.7 us  [local_pairs(): meta = lax.all_gather(meta, 'expert', axis=0)]
  transfers between devices with their start and end apart: 5 -> 53, of which waited for: 5 -> 16; matrix products, arithmetic and copies ran while one was open for 23% -> 8% of each run, Pallas kernels for 0% -> 23%
where the time goes in v1:
time: 288 us; the launch traced here: 283 us
  waiting for transfers between devices  99.7 us (35%)
  Pallas kernels  67.8 us (24%)
  starting transfers between devices  55.9 us (19%)
  local copies, waits for them, and re-layouts  24.4 us (8%)
  other arithmetic  17.5 us (6%)
  blocking collectives  16.7 us (6%)
    ppermute x6, waiting for transfers between devices, inward(): return lax.ppermute(x, 'dp', [(0, 1), (3, 2)])  44.5 us
    ppermute x36, waiting for transfers between devices, over(): return lax.ppermute(x, 'expert', [(i, i ^ bit) for i in range(peers)])  27.8 us
    ppermute x36, starting transfers between devices, over(): return lax.ppermute(x, 'expert', [(i, i ^ bit) for i in range(peers)])  21.7 us
    ppermute x3, waiting for transfers between devices, across_far(): return lax.ppermute(x, 'dp', [(1, 3), (2, 0)])  21.3 us
    unnamed x128, local copies, waits for them, and re-layouts  19.5 us
    pallas_call x2, Pallas kernels, forward(): pl.pallas_call(functools.partial(forward_kernel, capacity), grid_spec=plt...  18.7 us
    all_gather x1, blocking collectives, local_pairs(): meta = lax.all_gather(meta, 'expert', axis=0)  16.7 us
    pallas_call x3, Pallas kernels, gradient(): pl.pallas_call(functools.partial(gradient_kernel, len(lefts), count, dtyp...  12.3 us
  transfers between devices with their start and end apart: 53, of which 16 were waited for; matrix products, arithmetic and copies ran while one was open for 8% of the time, Pallas kernels for 23%

profile of v1, /device:TPU:8, one launch (start us, length us, event | category | flops | bytes accessed | tf_op | source)
XLA Modules:
  0.0 283.3 jit_solution(17502162606862778115)
XLA Ops:
  6.1 3.1 %collective-permute-done = f32[4,128]{1,0:T(4,128)S(1)} collective-permute-done((f32[4,128]{1,0:T(4,128)S(1)}, f32[4,128]{1,0:T(4,128)S(1)}, u32[]{:S(2)}, u32[]{:S(2)}) %collective-permute-start) | collective-permute-done | bytes 2080 | tf_op jit(solution)/shard_map/ppermute | solution.py:385
  10.6 5.1 %collective-permute-done.2.refs_2_ = bf16[128,2048]{1,0:T(8,128)(2,1)S(1)} collective-permute-done((bf16[128,2048]{1,0:T(8,128)(2,1)}, bf16[128,2048]{1,0:T(8,128)(2,1)S(1)}, u32[]{:S(2)}, u32[]{:S(2)}) %collective-permute-start.2) | collective-permute-done | bytes 524320 | tf_op jit(solution)/shard_map/ppermute | solution.py:375
  17.7 8.7 %collective-permute-done.11.refs_2_ = bf16[128,2048]{1,0:T(8,128)(2,1)S(1)} collective-permute-done((bf16[128,2048]{1,0:T(8,128)(2,1)}, bf16[128,2048]{1,0:T(8,128)(2,1)S(1)}, u32[]{:S(2)}, u32[]{:S(2)}) %collective-permute-start.11) | collective-permute-done | bytes 524320 | tf_op jit(solution)/shard_map/ppermute | solution.py:375
  31.4 2.9 %collective-permute-done.29.refs_0_ = bf16[128,2048]{1,0:T(8,128)(2,1)S(1)} collective-permute-done((bf16[128,2048]{1,0:T(8,128)(2,1)}, bf16[128,2048]{1,0:T(8,128)(2,1)S(1)}, u32[]{:S(2)}, u32[]{:S(2)}) %collective-permute-start.29) | collective-permute-done | bytes 524320 | tf_op jit(solution)/shard_map/ppermute | solution.py:385
  37.3 2.7 collective-permute-done.12.refs_3_
  47.7 7.4 %collective-permute-done.21.refs_2_ = bf16[128,2048]{1,0:T(8,128)(2,1)} collective-permute-done((bf16[128,2048]{1,0:T(8,128)(2,1)}, bf16[128,2048]{1,0:T(8,128)(2,1)}, u32[]{:S(2)}, u32[]{:S(2)}) %collective-permute-start.21) | collective-permute-done | bytes 524320 | tf_op jit(solution)/shard_map/ppermute | solution.py:375
  57.1 16.7 %all-gather = f32[64,128]{1,0:T(8,128)S(1)} all-gather(f32[8,128]{1,0:T(8,128)S(1)} %pad_maximum_fusion), channel_id=2, replica_groups=mesh['dp'=4,'expert'=8] {'expert'}, dimensions={0}, use_global_device_ids=true | all-gather | bytes 36864 | tf_op jit(solution)/shard_map/all_gather | solution.py:398
  87.8 8.8 %forward.2 = (bf16[512,2048]{1,0:T(8,128)(2,1)}, bf16[512,768]{1,0:T(8,128)(2,1)S(1)}, f32[512,768]{1,0:T(8,128)}, f32[512,768]{1,0:T(8,128)}) custom-call(s32[4]{0:T(128)S(1)} %pad_add_fusion.pos_ref, f32[8,4,128]{2,1,0:T(4,128)S(1)} %get-tuple-element.52.meta_ref, bf16[128,2048]{1,0:T(8,128)(2,1)S(1)} %copy-done.43, bf16[128,2048]{1,0:T(8,128)(2,1)S(1)} %copy-done.38, ...), custom_call_target="tpu_custom_call" | custom-call | flops 3221225472 | bytes 16777216 | tf_op jit(solution)/shard_map/forward/pallas_call | solution.py:171
  98.5 3.8 %cotangent.2 = (bf16[512,2048]{1,0:T(8,128)(2,1)}, bf16[512,768]{1,0:T(8,128)(2,1)}) custom-call(s32[4]{0:T(128)S(1)} %pad_add_fusion.pos_ref, f32[8,4,128]{2,1,0:T(4,128)S(1)} %get-tuple-element.52.meta_ref, bf16[128,2048]{1,0:T(8,128)(2,1)S(1)} %copy-done.26, bf16[128,2048]{1,0:T(8,128)(2,1)S(1)} %collective-permute-done.10.refs_1_, ...), custom_call_target="tpu_custom_call" | custom-call | flops 402653184 | bytes 8388608 | tf_op jit(solution)/shard_map/cotangent/pallas_call | solution.py:205
  102.3 4.7 %backward.2 = (bf16[512,768]{1,0:T(8,128)(2,1)S(1)}, bf16[512,768]{1,0:T(8,128)(2,1)S(1)}) custom-call(bf16[512,2048]{1,0:T(8,128)(2,1)} %get-tuple-element.29.dy_ref.refs_1_, bf16[2048,768]{1,0:T(8,128)(2,1)} %bitcast.20, f32[512,768]{1,0:T(8,128)S(1)} %copy-done.16, f32[512,768]{1,0:T(8,128)S(1)} %copy-done.17), custom_call_target="tpu_custom_call" | custom-call | flops 1610612736 | bytes 10485760 | tf_op jit(solution)/shard_map/backward/pallas_call | solution.py:231
  108.7 6.9 %rows_back.3 = bf16[512,2048]{1,0:T(8,128)(2,1)} custom-call(bf16[512,768]{1,0:T(8,128)(2,1)S(1)} %get-tuple-element.32.refs_0_.refs_4_.refs_1_.refs_2_, bf16[2048,768]{1,0:T(8,128)(2,1)} %bitcast.26, bf16[512,768]{1,0:T(8,128)(2,1)S(1)} %get-tuple-element.33.refs_2_.refs_5_.refs_3_, bf16[2048,768]{1,0:T(8,128)(2,1)} %bitcast.29), custom_call_target="tpu_custom_call" | custom-call | flops 3221225472 | bytes 8388608 | tf_op jit(solution)/shard_map/rows_back/pallas_call | solution.py:303
  115.6 4.4 %all-to-all-start.1 = ((bf16[8,64,2048]{2,1,0:T(8,128)(2,1)}), bf16[8,64,2048]{2,1,0:T(8,128)(2,1)}, u32[]{:S(2)}, u32[]{:S(2)}) async-start(bf16[8,64,2048]{2,1,0:T(8,128)(2,1)} %bitcast.11), calls=%async_computation.1 | async-start | bytes 4194304 | tf_op jit(solution)/shard_map/all_to_all | solution.py:422
  123.4 3.7 %gradient.5 = (bf16[512,768]{1,0:T(8,128)(2,1)}, bf16[512,768]{1,0:T(8,128)(2,1)S(1)}, bf16[512,768]{1,0:T(8,128)(2,1)S(1)}) custom-call(s32[4]{0:T(128)S(1)} %copy-done.40, bf16[512,2048]{1,0:T(8,128)(2,1)} %get-tuple-element.34.refs_0_, bf16[512,2048]{1,0:T(8,128)(2,1)} %get-tuple-element.29.dy_ref.refs_1_, bf16[512,768]{1,0:T(8,128)(2,1)S(1)} %copy-done.7, ...), custom_call_target="tpu_custom_call" | custom-call | flops 1207959552 | bytes 4194304 | tf_op jit(solution)/shard_map/gradient/pallas_call | solution.py:272
  132.9 3.5 %rows_back.2 = bf16[512,2048]{1,0:T(8,128)(2,1)} custom-call(bf16[512,768]{1,0:T(8,128)(2,1)S(1)} %copy-done.4, bf16[2048,768]{1,0:T(8,128)(2,1)S(1)} %bitcast.22), custom_call_target="tpu_custom_call" | custom-call | flops 1610612736 | bytes 8388608 | tf_op jit(solution)/shard_map/rows_back/pallas_call | solution.py:303
  142.6 10.0 %forward.3 = (bf16[512,2048]{1,0:T(8,128)(2,1)}, bf16[512,768]{1,0:T(8,128)(2,1)S(1)}, f32[512,768]{1,0:T(8,128)}, f32[512,768]{1,0:T(8,128)}) custom-call(s32[4]{0:T(128)S(1)} %copy-done.41, f32[8,4,128]{2,1,0:T(4,128)S(1)} %get-tuple-element.51.meta_ref, bf16[128,2048]{1,0:T(8,128)(2,1)} %collective-permute-done.19.refs_0_, ...), custom_call_target="tpu_custom_call" | custom-call | flops 3221225472 | bytes 16777216 | tf_op jit(solution)/shard_map/forward/pallas_call | solution.py:171
  155.2 4.5 %cotangent.3 = (bf16[512,2048]{1,0:T(8,128)(2,1)}, bf16[512,768]{1,0:T(8,128)(2,1)}) custom-call(s32[4]{0:T(128)S(1)} %copy-done.41, f32[8,4,128]{2,1,0:T(4,128)S(1)} %get-tuple-element.51.meta_ref, bf16[128,2048]{1,0:T(8,128)(2,1)S(1)} %copy-done.28, bf16[128,2048]{1,0:T(8,128)(2,1)} %collective-permute-done.30.refs_1_, ...), custom_call_target="tpu_custom_call" | custom-call | flops 402653184 | bytes 8388608 | tf_op jit(solution)/shard_map/cotangent/pallas_call | solution.py:205
  159.7 4.7 %backward.3 = (bf16[512,768]{1,0:T(8,128)(2,1)S(1)}, bf16[512,768]{1,0:T(8,128)(2,1)S(1)}) custom-call(bf16[512,2048]{1,0:T(8,128)(2,1)} %get-tuple-element.37.dy_ref.refs_3_, bf16[2048,768]{1,0:T(8,128)(2,1)} %bitcast.21, f32[512,768]{1,0:T(8,128)S(1)} %copy-done.14, f32[512,768]{1,0:T(8,128)S(1)} %copy-done.15), custom_call_target="tpu_custom_call" | custom-call | flops 1610612736 | bytes 10485760 | tf_op jit(solution)/shard_map/backward/pallas_call | solution.py:231
  168.3 3.5 %collective-permute-start.42 = (bf16[512,768]{1,0:T(8,128)(2,1)}, bf16[512,768]{1,0:T(8,128)(2,1)}, u32[]{:S(2)}, u32[]{:S(2)}) collective-permute-start(bf16[512,768]{1,0:T(8,128)(2,1)} %add_convert_fusion.7), channel_id=1, source_target_pairs={{8,16},{16,8},{9,17},{17,9},{10,18},{18,10},{11,19},{19,11},{12,20... | collective-permute-start | bytes 2359304 | tf_op jit(solution)/shard_map/ppermute | solution.py:394
  173.0 12.2 %collective-permute-done.49 = bf16[512,768]{1,0:T(8,128)(2,1)S(1)} collective-permute-done((bf16[512,768]{1,0:T(8,128)(2,1)S(1)}, bf16[512,768]{1,0:T(8,128)(2,1)S(1)}, u32[]{:S(2)}, u32[]{:S(2)}) %collective-permute-start.49) | collective-permute-done | bytes 786464 | tf_op jit(solution)/shard_map/ppermute | solution.py:388
  185.2 3.5 %collective-permute-start.46 = (bf16[512,768]{1,0:T(8,128)(2,1)}, bf16[512,768]{1,0:T(8,128)(2,1)}, u32[]{:S(2)}, u32[]{:S(2)}) collective-permute-start(bf16[512,768]{1,0:T(8,128)(2,1)} %add_convert_fusion.4), channel_id=1, source_target_pairs={{8,16},{16,8},{9,17},{17,9},{10,18},{18,10},{11,19},{19,11},{12,20... | collective-permute-start | bytes 2359304 | tf_op jit(solution)/shard_map/ppermute | solution.py:394
  189.7 4.1 %all-to-all-start = ((bf16[8,64,2048]{2,1,0:T(8,128)(2,1)}), bf16[8,64,2048]{2,1,0:T(8,128)(2,1)S(1)}, u32[]{:S(2)}, u32[]{:S(2)}) async-start(bf16[8,64,2048]{2,1,0:T(8,128)(2,1)} %bitcast.9), calls=%async_computation | async-start | bytes 4194304 | tf_op jit(solution)/shard_map/all_to_all | solution.py:422
  193.8 8.3 %collective-permute-done.39 = bf16[512,768]{1,0:T(8,128)(2,1)} collective-permute-done((bf16[512,768]{1,0:T(8,128)(2,1)}, bf16[512,768]{1,0:T(8,128)(2,1)}, u32[]{:S(2)}, u32[]{:S(2)}) %collective-permute-start.39) | collective-permute-done | bytes 786464 | tf_op jit(solution)/shard_map/ppermute | solution.py:388
  202.1 3.5 %collective-permute-start.50 = (bf16[512,768]{1,0:T(8,128)(2,1)}, bf16[512,768]{1,0:T(8,128)(2,1)S(1)}, u32[]{:S(2)}, u32[]{:S(2)}) collective-permute-start(bf16[512,768]{1,0:T(8,128)(2,1)} %add_convert_fusion.1), channel_id=1, source_target_pairs={{8,16},{16,8},{9,17},{17,9},{10,18},{18,10},{11,19},{19,11},{12,20... | collective-permute-start | bytes 2359304 | tf_op jit(solution)/shard_map/ppermute | solution.py:394
  207.2 11.8 %collective-permute-done.43 = bf16[512,768]{1,0:T(8,128)(2,1)} collective-permute-done((bf16[512,768]{1,0:T(8,128)(2,1)}, bf16[512,768]{1,0:T(8,128)(2,1)}, u32[]{:S(2)}, u32[]{:S(2)}) %collective-permute-start.43) | collective-permute-done | bytes 786464 | tf_op jit(solution)/shard_map/ppermute | solution.py:388
  219.0 2.5 collective-permute-start.40
  223.2 12.1 %collective-permute-done.47 = bf16[512,768]{1,0:T(8,128)(2,1)} collective-permute-done((bf16[512,768]{1,0:T(8,128)(2,1)}, bf16[512,768]{1,0:T(8,128)(2,1)}, u32[]{:S(2)}, u32[]{:S(2)}) %collective-permute-start.47) | collective-permute-done | bytes 786464 | tf_op jit(solution)/shard_map/ppermute | solution.py:388
  240.8 6.0 %gradient.3 = (f32[512,768]{1,0:T(8,128)}, f32[512,768]{1,0:T(8,128)}, f32[512,768]{1,0:T(8,128)}) custom-call(s32[4]{0:T(128)S(1)} %copy-done.42, bf16[512,2048]{1,0:T(8,128)(2,1)} %get-tuple-element.34.refs_0_, bf16[512,2048]{1,0:T(8,128)(2,1)} %get-tuple-element.29.dy_ref.refs_1_, bf16[512,2048]{1,0:T(8,128)(2,1)} %get-tuple-element.35.refs_2_, ...), custom_call_target="tpu_custom_call" | custom-call | flops 2415919104 | bytes 4194304 | tf_op jit(solution)/shard_map/gradient/pallas_call | solution.py:272
  246.8 2.9 %fusion = bf16[1,512,768]{2,1,0:T(8,128)(2,1)} fusion(bf16[512,768]{1,0:T(8,128)(2,1)} %collective-permute-done.42, f32[512,768]{1,0:T(8,128)} %get-tuple-element.42, bf16[512,768]{1,0:T(8,128)(2,1)S(1)} %collective-permute-done.40), kind=kLoop, calls=%fused_computation.9 | loop fusion | flops 1966080 | bytes 3932160 | tf_op jit(solution)/shard_map/broadcast_in_dim | solution.py:435
  249.7 7.8 %collective-permute-done.44 = bf16[512,768]{1,0:T(8,128)(2,1)S(1)} collective-permute-done((bf16[512,768]{1,0:T(8,128)(2,1)S(1)}, bf16[512,768]{1,0:T(8,128)(2,1)S(1)}, u32[]{:S(2)}, u32[]{:S(2)}) %collective-permute-start.44) | collective-permute-done | bytes 786464 | tf_op jit(solution)/shard_map/ppermute | solution.py:391
  260.0 13.5 %collective-permute-done.48 = bf16[512,768]{1,0:T(8,128)(2,1)S(1)} collective-permute-done((bf16[512,768]{1,0:T(8,128)(2,1)S(1)}, bf16[512,768]{1,0:T(8,128)(2,1)S(1)}, u32[]{:S(2)}, u32[]{:S(2)}) %collective-permute-start.48) | collective-permute-done | bytes 786464 | tf_op jit(solution)/shard_map/ppermute | solution.py:391
  274.7 4.7 %combine.3 = bf16[128,2048]{1,0:T(8,128)(2,1)} custom-call(s32[128,2]{1,0:T(8,128)S(1)} %copy.12.ids_ref, f32[128,2]{1,0:T(8,128)S(1)} %copy.13.prob_ref, bf16[512,2048]{1,0:T(8,128)(2,1)} %bitcast.12.rows_ref), custom_call_target="tpu_custom_call" | custom-call | flops 536870912 | bytes 3145728 | tf_op jit(solution)/shard_map/combine/pallas_call | solution.py:344
  279.4 3.9 %combine.2 = bf16[128,2048]{1,0:T(8,128)(2,1)} custom-call(s32[128,2]{1,0:T(8,128)S(1)} %copy.12.ids_ref, f32[128,2]{1,0:T(8,128)S(1)} %copy.13.prob_ref, bf16[512,2048]{1,0:T(8,128)(2,1)S(1)} %bitcast.23), custom_call_target="tpu_custom_call" | custom-call | flops 536870912 | bytes 3145728 | tf_op jit(solution)/shard_map/combine/pallas_call | solution.py:344
  (238 shorter events, 80.0 us)
Async XLA Ops:
  3.8 22.7 %collective-permute-start.11 = (bf16[128,2048]{1,0:T(8,128)(2,1)}, bf16[128,2048]{1,0:T(8,128)(2,1)S(1)}, u32[]{:S(2)}, u32[]{:S(2)}) collective-permute-start(bf16[128,2048]{1,0:T(8,128)(2,1)} %refs_0_.3), channel_id=1, source_target_pairs={{0,4},{1,5},{2,6},{3,7},{4,0},{5,1},{6,2},{7,3},{8,12},{9,13},{10,... | collective-permute-start | bytes 1572872 | tf_op jit(solution)/shard_map/ppermute | solution.py:375
  9.2 18.8 %collective-permute-start.10 = (bf16[128,2048]{1,0:T(8,128)(2,1)}, bf16[128,2048]{1,0:T(8,128)(2,1)S(1)}, u32[]{:S(2)}, u32[]{:S(2)}) collective-permute-start(bf16[128,2048]{1,0:T(8,128)(2,1)} %refs_0_.3), channel_id=1, source_target_pairs={{0,2},{1,3},{2,0},{3,1},{4,6},{5,7},{6,4},{7,5},{8,10},{9,11},{10,... | collective-permute-start | bytes 1572872 | tf_op jit(solution)/shard_map/ppermute | solution.py:375
  10.6 19.1 %collective-permute-start.19 = (bf16[128,2048]{1,0:T(8,128)(2,1)}, bf16[128,2048]{1,0:T(8,128)(2,1)}, u32[]{:S(2)}, u32[]{:S(2)}) collective-permute-start(bf16[128,2048]{1,0:T(8,128)(2,1)} %refs_0_.2), channel_id=1, source_target_pairs={{0,8},{8,0},{16,24},{24,16},{1,9},{9,1},{17,25},{25,17},{2,10},{10... | collective-permute-start | bytes 1572872 | tf_op jit(solution)/shard_map/ppermute | solution.py:385
  45.2 28.6 %collective-permute-start.16 = (bf16[128,2048]{1,0:T(8,128)(2,1)S(1)}, bf16[128,2048]{1,0:T(8,128)(2,1)S(1)}, u32[]{:S(2)}, u32[]{:S(2)}) collective-permute-start(bf16[128,2048]{1,0:T(8,128)(2,1)S(1)} %collective-permute-done.11.refs_2_), channel_id=1, source_target_pairs={{0,1},{1,0},{2,3},{3,2},{4,5},{5,4},{6,7},{7,6},{8,9},{9,8},{10,11... | collective-permute-start | bytes 1572872 | tf_op jit(solution)/shard_map/ppermute | solution.py:375
  46.4 27.7 %collective-permute-start.31 = (bf16[128,2048]{1,0:T(8,128)(2,1)S(1)}, bf16[128,2048]{1,0:T(8,128)(2,1)}, u32[]{:S(2)}, u32[]{:S(2)}) collective-permute-start(bf16[128,2048]{1,0:T(8,128)(2,1)S(1)} %collective-permute-done.29.refs_0_), channel_id=1, source_target_pairs={{0,4},{1,5},{2,6},{3,7},{4,0},{5,1},{6,2},{7,3},{8,12},{9,13},{10,... | collective-permute-start | bytes 1572872 | tf_op jit(solution)/shard_map/ppermute | solution.py:375
  55.2 22.7 %collective-permute-start.15 = (bf16[128,2048]{1,0:T(8,128)(2,1)S(1)}, bf16[128,2048]{1,0:T(8,128)(2,1)S(1)}, u32[]{:S(2)}, u32[]{:S(2)}) collective-permute-start(bf16[128,2048]{1,0:T(8,128)(2,1)S(1)} %collective-permute-done.10.refs_1_), channel_id=1, source_target_pairs={{0,1},{1,0},{2,3},{3,2},{4,5},{5,4},{6,7},{7,6},{8,9},{9,8},{10,11... | collective-permute-start | bytes 1572872 | tf_op jit(solution)/shard_map/ppermute | solution.py:375
  55.2 24.2 %collective-permute-start.30 = (bf16[128,2048]{1,0:T(8,128)(2,1)S(1)}, bf16[128,2048]{1,0:T(8,128)(2,1)}, u32[]{:S(2)}, u32[]{:S(2)}) collective-permute-start(bf16[128,2048]{1,0:T(8,128)(2,1)S(1)} %collective-permute-done.29.refs_0_), channel_id=1, source_target_pairs={{0,2},{1,3},{2,0},{3,1},{4,6},{5,7},{6,4},{7,5},{8,10},{9,11},{10,... | collective-permute-start | bytes 1572872 | tf_op jit(solution)/shard_map/ppermute | solution.py:375
  56.8 20.4 %collective-permute-start.18 = (bf16[64,2048]{1,0:T(8,128)(2,1)}, bf16[64,2048]{1,0:T(8,128)(2,1)S(1)}, u32[]{:S(2)}, u32[]{:S(2)}) collective-permute-start(bf16[64,2048]{1,0:T(8,128)(2,1)} %copy-done.31), channel_id=1, source_target_pairs={{0,1},{1,0},{2,3},{3,2},{4,5},{5,4},{6,7},{7,6},{8,9},{9,8},{10,11... | collective-permute-start | bytes 786440 | tf_op jit(solution)/shard_map/ppermute | solution.py:375
  73.8 33.3 %collective-permute-start.24 = (bf16[128,2048]{1,0:T(8,128)(2,1)}, bf16[128,2048]{1,0:T(8,128)(2,1)S(1)}, u32[]{:S(2)}, u32[]{:S(2)}) collective-permute-start(bf16[128,2048]{1,0:T(8,128)(2,1)} %collective-permute-done.19.refs_0_), channel_id=1, source_target_pairs={{0,1},{1,0},{2,3},{3,2},{4,5},{5,4},{6,7},{7,6},{8,9},{9,8},{10,11... | collective-permute-start | bytes 1572872 | tf_op jit(solution)/shard_map/ppermute | solution.py:375
  74.1 33.5 %collective-permute-start.34 = (bf16[128,2048]{1,0:T(8,128)(2,1)S(1)}, bf16[128,2048]{1,0:T(8,128)(2,1)S(1)}, u32[]{:S(2)}, u32[]{:S(2)}) collective-permute-start(bf16[128,2048]{1,0:T(8,128)(2,1)S(1)} %collective-permute-done.29.refs_0_), channel_id=1, source_target_pairs={{0,1},{1,0},{2,3},{3,2},{4,5},{5,4},{6,7},{7,6},{8,9},{9,8},{10,11... | collective-permute-start | bytes 1572872 | tf_op jit(solution)/shard_map/ppermute | solution.py:375
  77.2 30.4 %collective-permute-start.22 = (bf16[64,2048]{1,0:T(8,128)(2,1)S(1)}, bf16[64,2048]{1,0:T(8,128)(2,1)}, u32[]{:S(2)}, u32[]{:S(2)}) collective-permute-start(bf16[64,2048]{1,0:T(8,128)(2,1)S(1)} %slice.46), channel_id=1, source_target_pairs={{0,2},{1,3},{2,0},{3,1},{4,6},{5,7},{6,4},{7,5},{8,10},{9,11},{10,... | collective-permute-start | bytes 786440 | tf_op jit(solution)/shard_map/ppermute | solution.py:375
  77.8 30.3 %collective-permute-start.23 = (bf16[64,2048]{1,0:T(8,128)(2,1)S(1)}, bf16[64,2048]{1,0:T(8,128)(2,1)}, u32[]{:S(2)}, u32[]{:S(2)}) collective-permute-start(bf16[64,2048]{1,0:T(8,128)(2,1)S(1)} %slice.47), channel_id=1, source_target_pairs={{0,4},{1,5},{2,6},{3,7},{4,0},{5,1},{6,2},{7,3},{8,12},{9,13},{10,... | collective-permute-start | bytes 786440 | tf_op jit(solution)/shard_map/ppermute | solution.py:375
  79.4 28.9 %collective-permute-start.32 = (bf16[64,2048]{1,0:T(8,128)(2,1)S(1)}, bf16[64,2048]{1,0:T(8,128)(2,1)S(1)}, u32[]{:S(2)}, u32[]{:S(2)}) collective-permute-start(bf16[64,2048]{1,0:T(8,128)(2,1)S(1)} %slice.48), channel_id=1, source_target_pairs={{0,2},{1,3},{2,0},{3,1},{4,6},{5,7},{6,4},{7,5},{8,10},{9,11},{10,... | collective-permute-start | bytes 786440 | tf_op jit(solution)/shard_map/ppermute | solution.py:375
  107.1 21.9 %collective-permute-start.33 = (bf16[64,2048]{1,0:T(8,128)(2,1)}, bf16[64,2048]{1,0:T(8,128)(2,1)S(1)}, u32[]{:S(2)}, u32[]{:S(2)}) collective-permute-start(bf16[64,2048]{1,0:T(8,128)(2,1)} %slice.49), channel_id=1, source_target_pairs={{0,4},{1,5},{2,6},{3,7},{4,0},{5,1},{6,2},{7,3},{8,12},{9,13},{10,... | collective-permute-start | bytes 786440 | tf_op jit(solution)/shard_map/ppermute | solution.py:375
  107.6 22.6 %collective-permute-start.26 = (bf16[128,2048]{1,0:T(8,128)(2,1)}, bf16[128,2048]{1,0:T(8,128)(2,1)}, u32[]{:S(2)}, u32[]{:S(2)}) collective-permute-start(bf16[128,2048]{1,0:T(8,128)(2,1)} %collective-permute-done.21.refs_2_), channel_id=1, source_target_pairs={{0,1},{1,0},{2,3},{3,2},{4,5},{5,4},{6,7},{7,6},{8,9},{9,8},{10,11... | collective-permute-start | bytes 1572872 | tf_op jit(solution)/shard_map/ppermute | solution.py:375
  107.7 23.1 %collective-permute-start.25 = (bf16[128,2048]{1,0:T(8,128)(2,1)}, bf16[128,2048]{1,0:T(8,128)(2,1)}, u32[]{:S(2)}, u32[]{:S(2)}) collective-permute-start(bf16[128,2048]{1,0:T(8,128)(2,1)} %collective-permute-done.20.refs_1_), channel_id=1, source_target_pairs={{0,1},{1,0},{2,3},{3,2},{4,5},{5,4},{6,7},{7,6},{8,9},{9,8},{10,11... | collective-permute-start | bytes 1572872 | tf_op jit(solution)/shard_map/ppermute | solution.py:375
  108.2 28.3 %collective-permute-start.36 = (bf16[128,2048]{1,0:T(8,128)(2,1)}, bf16[128,2048]{1,0:T(8,128)(2,1)}, u32[]{:S(2)}, u32[]{:S(2)}) collective-permute-start(bf16[128,2048]{1,0:T(8,128)(2,1)} %collective-permute-done.31.refs_2_), channel_id=1, source_target_pairs={{0,1},{1,0},{2,3},{3,2},{4,5},{5,4},{6,7},{7,6},{8,9},{9,8},{10,11... | collective-permute-start | bytes 1572872 | tf_op jit(solution)/shard_map/ppermute | solution.py:375
  108.2 32.2 %collective-permute-start.35 = (bf16[128,2048]{1,0:T(8,128)(2,1)}, bf16[128,2048]{1,0:T(8,128)(2,1)}, u32[]{:S(2)}, u32[]{:S(2)}) collective-permute-start(bf16[128,2048]{1,0:T(8,128)(2,1)} %collective-permute-done.30.refs_1_), channel_id=1, source_target_pairs={{0,1},{1,0},{2,3},{3,2},{4,5},{5,4},{6,7},{7,6},{8,9},{9,8},{10,11... | collective-permute-start | bytes 1572872 | tf_op jit(solution)/shard_map/ppermute | solution.py:375
  115.6 74.1 %all-to-all-start.1 = ((bf16[8,64,2048]{2,1,0:T(8,128)(2,1)}), bf16[8,64,2048]{2,1,0:T(8,128)(2,1)}, u32[]{:S(2)}, u32[]{:S(2)}) async-start(bf16[8,64,2048]{2,1,0:T(8,128)(2,1)} %bitcast.11), calls=%async_computation.1 | async-start | bytes 4194304 | tf_op jit(solution)/shard_map/all_to_all | solution.py:422
  129.0 35.5 %collective-permute-start.41 = (bf16[512,768]{1,0:T(8,128)(2,1)}, bf16[512,768]{1,0:T(8,128)(2,1)}, u32[]{:S(2)}, u32[]{:S(2)}) collective-permute-start(bf16[512,768]{1,0:T(8,128)(2,1)} %get-tuple-element.44), channel_id=1, source_target_pairs={{0,8},{24,16},{1,9},{25,17},{2,10},{26,18},{3,11},{27,19},{4,12},{... | collective-permute-start | bytes 2359304 | tf_op jit(solution)/shard_map/ppermute | solution.py:388
  136.5 31.8 %collective-permute-start.45 = (bf16[512,768]{1,0:T(8,128)(2,1)S(1)}, bf16[512,768]{1,0:T(8,128)(2,1)S(1)}, u32[]{:S(2)}, u32[]{:S(2)}) collective-permute-start(bf16[512,768]{1,0:T(8,128)(2,1)S(1)} %copy-done.25), channel_id=1, source_target_pairs={{0,8},{24,16},{1,9},{25,17},{2,10},{26,18},{3,11},{27,19},{4,12},{... | collective-permute-start | bytes 2359304 | tf_op jit(solution)/shard_map/ppermute | solution.py:388
  140.5 44.7 %collective-permute-start.49 = (bf16[512,768]{1,0:T(8,128)(2,1)S(1)}, bf16[512,768]{1,0:T(8,128)(2,1)S(1)}, u32[]{:S(2)}, u32[]{:S(2)}) collective-permute-start(bf16[512,768]{1,0:T(8,128)(2,1)S(1)} %copy-done.23), channel_id=1, source_target_pairs={{0,8},{24,16},{1,9},{25,17},{2,10},{26,18},{3,11},{27,19},{4,12},{... | collective-permute-start | bytes 2359304 | tf_op jit(solution)/shard_map/ppermute | solution.py:388
  152.5 49.6 %collective-permute-start.39 = (bf16[512,768]{1,0:T(8,128)(2,1)}, bf16[512,768]{1,0:T(8,128)(2,1)}, u32[]{:S(2)}, u32[]{:S(2)}) collective-permute-start(bf16[512,768]{1,0:T(8,128)(2,1)} %get-tuple-element.43), channel_id=1, source_target_pairs={{0,8},{24,16},{1,9},{25,17},{2,10},{26,18},{3,11},{27,19},{4,12},{... | collective-permute-start | bytes 2359304 | tf_op jit(solution)/shard_map/ppermute | solution.py:388
  153.8 65.1 %collective-permute-start.43 = (bf16[512,768]{1,0:T(8,128)(2,1)}, bf16[512,768]{1,0:T(8,128)(2,1)}, u32[]{:S(2)}, u32[]{:S(2)}) collective-permute-start(bf16[512,768]{1,0:T(8,128)(2,1)} %get-tuple-element.46), channel_id=1, source_target_pairs={{0,8},{24,16},{1,9},{25,17},{2,10},{26,18},{3,11},{27,19},{4,12},{... | collective-permute-start | bytes 2359304 | tf_op jit(solution)/shard_map/ppermute | solution.py:388
  164.5 70.8 %collective-permute-start.47 = (bf16[512,768]{1,0:T(8,128)(2,1)}, bf16[512,768]{1,0:T(8,128)(2,1)}, u32[]{:S(2)}, u32[]{:S(2)}) collective-permute-start(bf16[512,768]{1,0:T(8,128)(2,1)} %get-tuple-element.49), channel_id=1, source_target_pairs={{0,8},{24,16},{1,9},{25,17},{2,10},{26,18},{3,11},{27,19},{4,12},{... | collective-permute-start | bytes 2359304 | tf_op jit(solution)/shard_map/ppermute | solution.py:388
  168.3 71.0 %collective-permute-start.42 = (bf16[512,768]{1,0:T(8,128)(2,1)}, bf16[512,768]{1,0:T(8,128)(2,1)}, u32[]{:S(2)}, u32[]{:S(2)}) collective-permute-start(bf16[512,768]{1,0:T(8,128)(2,1)} %add_convert_fusion.7), channel_id=1, source_target_pairs={{8,16},{16,8},{9,17},{17,9},{10,18},{18,10},{11,19},{19,11},{12,20... | collective-permute-start | bytes 2359304 | tf_op jit(solution)/shard_map/ppermute | solution.py:394
  185.2 64.5 %collective-permute-start.46 = (bf16[512,768]{1,0:T(8,128)(2,1)}, bf16[512,768]{1,0:T(8,128)(2,1)}, u32[]{:S(2)}, u32[]{:S(2)}) collective-permute-start(bf16[512,768]{1,0:T(8,128)(2,1)} %add_convert_fusion.4), channel_id=1, source_target_pairs={{8,16},{16,8},{9,17},{17,9},{10,18},{18,10},{11,19},{19,11},{12,20... | collective-permute-start | bytes 2359304 | tf_op jit(solution)/shard_map/ppermute | solution.py:394
  189.7 89.7 %all-to-all-start = ((bf16[8,64,2048]{2,1,0:T(8,128)(2,1)}), bf16[8,64,2048]{2,1,0:T(8,128)(2,1)S(1)}, u32[]{:S(2)}, u32[]{:S(2)}) async-start(bf16[8,64,2048]{2,1,0:T(8,128)(2,1)} %bitcast.9), calls=%async_computation | async-start | bytes 4194304 | tf_op jit(solution)/shard_map/all_to_all | solution.py:422
  202.1 57.8 %collective-permute-start.50 = (bf16[512,768]{1,0:T(8,128)(2,1)}, bf16[512,768]{1,0:T(8,128)(2,1)S(1)}, u32[]{:S(2)}, u32[]{:S(2)}) collective-permute-start(bf16[512,768]{1,0:T(8,128)(2,1)} %add_convert_fusion.1), channel_id=1, source_target_pairs={{8,16},{16,8},{9,17},{17,9},{10,18},{18,10},{11,19},{19,11},{12,20... | collective-permute-start | bytes 2359304 | tf_op jit(solution)/shard_map/ppermute | solution.py:394
  219.0 27.8 %collective-permute-start.40 = (bf16[512,768]{1,0:T(8,128)(2,1)S(1)}, bf16[512,768]{1,0:T(8,128)(2,1)S(1)}, u32[]{:S(2)}, u32[]{:S(2)}) collective-permute-start(bf16[512,768]{1,0:T(8,128)(2,1)S(1)} %add_convert_fusion.8), channel_id=1, source_target_pairs={{8,24},{16,0},{9,25},{17,1},{10,26},{18,2},{11,27},{19,3},{12,28},... | collective-permute-start | bytes 2359304 | tf_op jit(solution)/shard_map/ppermute | solution.py:391
  235.3 22.2 %collective-permute-start.44 = (bf16[512,768]{1,0:T(8,128)(2,1)S(1)}, bf16[512,768]{1,0:T(8,128)(2,1)S(1)}, u32[]{:S(2)}, u32[]{:S(2)}) collective-permute-start(bf16[512,768]{1,0:T(8,128)(2,1)S(1)} %add_convert_fusion.5), channel_id=1, source_target_pairs={{8,24},{16,0},{9,25},{17,1},{10,26},{18,2},{11,27},{19,3},{12,28},... | collective-permute-start | bytes 2359304 | tf_op jit(solution)/shard_map/ppermute | solution.py:391
  239.3 34.1 %collective-permute-start.48 = (bf16[512,768]{1,0:T(8,128)(2,1)S(1)}, bf16[512,768]{1,0:T(8,128)(2,1)S(1)}, u32[]{:S(2)}, u32[]{:S(2)}) collective-permute-start(bf16[512,768]{1,0:T(8,128)(2,1)S(1)} %add_convert_fusion.2), channel_id=1, source_target_pairs={{8,24},{16,0},{9,25},{17,1},{10,26},{18,2},{11,27},{19,3},{12,28},... | collective-permute-start | bytes 2359304 | tf_op jit(solution)/shard_map/ppermute | solution.py:391
  (84 other events, 835.6 us)

commit v2 on v0

v2 whole, which is shorter than its diff:
```python
import functools

import jax
import jax.numpy as jnp
from jax import lax
from jax.experimental import pallas as pl
from jax.experimental.pallas import tpu as pltpu
from jax.sharding import PartitionSpec as P

F32 = jnp.float32
BF16 = jnp.bfloat16


def route_slots(expert_ids, experts, capacity):
    flat = expert_ids.reshape(-1)
    onehot = (flat[:, None] == jnp.arange(experts, dtype=jnp.int32)[None, :]).astype(jnp.int32)
    before = jnp.cumsum(onehot, axis=0) - onehot
    position = jnp.sum(before * onehot, axis=1)
    return flat * capacity + position


def local_any(tokens, expert_ids, gate_probs, w_gate, w_up, w_down, out_grad):
    token_count, top_count = expert_ids.shape
    width = tokens.shape[1]
    local_experts = w_gate.shape[0]
    peers = lax.axis_size("expert")
    experts = local_experts * peers
    capacity = max(2, 2 * token_count * top_count // experts)
    slot_total = experts * capacity
    route_total = token_count * top_count
    slot = route_slots(expert_ids, experts, capacity)
    owner = slot[None, :] == jnp.arange(slot_total, dtype=jnp.int32)[:, None]
    live = jnp.any(owner, axis=1)
    route_index = jnp.sum(
        jnp.where(owner, jnp.arange(route_total, dtype=jnp.int32)[None, :], 0), axis=1
    )
    token_of_slot = route_index // top_count
    slot_prob = jnp.sum(jnp.where(owner, gate_probs.reshape(-1)[None, :], 0.0), axis=1)
    dispatched = jnp.where(
        live[:, None], jnp.take(tokens, token_of_slot, axis=0), jnp.zeros((), tokens.dtype)
    )
    dispatched = dispatched.reshape(peers, local_experts, capacity, width)
    received = lax.all_to_all(dispatched, "expert", split_axis=0, concat_axis=0, tiled=True)
    gate_act = jnp.einsum("secd,edh->sech", received, w_gate, preferred_element_type=F32)
    up_act = jnp.einsum("secd,edh->sech", received, w_up, preferred_element_type=F32)
    hidden = (jax.nn.silu(gate_act) * up_act).astype(BF16)
    result = jnp.einsum("sech,edh->secd", hidden, w_down, preferred_element_type=F32).astype(BF16)
    returned = lax.all_to_all(result, "expert", split_axis=0, concat_axis=0, tiled=True)
    picked = jnp.take(returned.reshape(slot_total, width), slot, axis=0).astype(F32)
    picked = picked.reshape(token_count, top_count, width)
    mixed = jnp.sum(picked * gate_probs[:, :, None], axis=1).astype(BF16)
    dy_rows = jnp.where(
        live[:, None], jnp.take(out_grad, token_of_slot, axis=0), jnp.zeros((), out_grad.dtype)
    )
    dy_slot = (dy_rows.astype(F32) * slot_prob[:, None]).astype(BF16)
    dy_slot = dy_slot.reshape(peers, local_experts, capacity, width)
    dy_recv = lax.all_to_all(dy_slot, "expert", split_axis=0, concat_axis=0, tiled=True)
    d_hidden = jnp.einsum("secd,edh->sech", dy_recv, w_down, preferred_element_type=F32)
    sigma = jax.nn.sigmoid(gate_act)
    d_gate = (d_hidden * up_act * sigma * (1.0 + gate_act * (1.0 - sigma))).astype(BF16)
    d_up = (d_hidden * gate_act * sigma).astype(BF16)
    dx_slot = jnp.einsum("sech,edh->secd", d_gate, w_gate, preferred_element_type=F32)
    dx_slot = (
        dx_slot + jnp.einsum("sech,edh->secd", d_up, w_up, preferred_element_type=F32)
    ).astype(BF16)
    dx_back = lax.all_to_all(dx_slot, "expert", split_axis=0, concat_axis=0, tiled=True)
    dx_picked = jnp.take(dx_back.reshape(slot_total, width), slot, axis=0).astype(F32)
    tokens_grad = jnp.sum(dx_picked.reshape(token_count, top_count, width), axis=1).astype(BF16)
    first = jnp.einsum("secd,sech->deh", received, d_gate, preferred_element_type=F32)
    second = jnp.einsum("secd,sech->deh", received, d_up, preferred_element_type=F32)
    third = jnp.einsum("secd,sech->deh", dy_recv, hidden, preferred_element_type=F32)
    share = lax.psum_scatter(
        jnp.stack([first, second, third], axis=1).astype(BF16),
        "dp",
        scatter_dimension=0,
        tiled=True,
    )
    grads = [jnp.transpose(share[:, k], (1, 0, 2)) for k in range(3)]
    return (mixed, tokens_grad, *grads)


EXTRA = 16
TILE = 256
VMEM = pl.BlockSpec(memory_space=pltpu.VMEM)
SMEM = pl.BlockSpec(memory_space=pltpu.SMEM)
ANY = pl.BlockSpec(memory_space=pl.ANY)


def nn(a, b):
    return lax.dot_general(a, b, (((1,), (0,)), ((), ())), preferred_element_type=F32)


def nt(a, b):
    return lax.dot_general(a, b, (((1,), (1,)), ((), ())), preferred_element_type=F32)


def tn(a, b):
    return lax.dot_general(a, b, (((0,), (0,)), ((), ())), preferred_element_type=F32)


def shape(*sizes, dtype=BF16):
    return jax.ShapeDtypeStruct(sizes, dtype)


def run(name, kernel, operands, outs, after=(), held=None, out_held=None, scratch=(), us=1.0, limit=14):
    skip, count = len(after), len(operands) + len(outs)

    def body(*refs):
        refs = refs[skip:]
        kernel(*refs[:count], *refs[count + 1 :])

    return pl.pallas_call(
        body,
        in_specs=[ANY] * skip + list(held or [VMEM] * len(operands)),
        out_specs=list(out_held or [VMEM] * len(outs)) + [VMEM],
        out_shape=list(outs) + [shape(8, 128, dtype=F32)],
        scratch_shapes=list(scratch),
        compiler_params=pltpu.CompilerParams(vmem_limit_bytes=limit * 1024 * 1024),
        cost_estimate=pl.CostEstimate(flops=int(us * 1e9), bytes_accessed=1 << 16, transcendentals=0),
        name=name,
    )(*after, *operands)


def tie(x, after):
    return pl.pallas_call(
        lambda *refs: None,
        in_specs=[ANY] * (1 + len(after)),
        out_specs=ANY,
        out_shape=jax.ShapeDtypeStruct(x.shape, x.dtype),
        input_output_aliases={0: 0},
        cost_estimate=pl.CostEstimate(flops=8, bytes_accessed=8, transcendentals=0),
        name="tie",
    )(x, *after)


def tiles(size, body, tile=TILE):
    @pl.loop(0, size // tile)
    def _(i):
        body(pl.ds(pl.multiple_of(i * tile, tile), tile))


def columns(start, size):
    return pl.ds(pl.multiple_of(start * size, size), size)


def start_all(pairs, sem):
    copies = [pltpu.make_async_copy(src, dst, sem.at[n]) for n, (src, dst) in enumerate(pairs)]
    for copy in copies:
        copy.start()
    return copies


def wait_all(copies):
    for copy in copies:
        copy.wait()


def cut_rows(ref, parts):
    size = ref.shape[0] // parts
    return [pl.ds(n * size, size) for n in range(parts)]


def pack_kernel(tokens_in, grad_in, ids_in, prob_in, rows_ref, grad_ref, raw_ref, meta_ref, ids_ref, prob_ref, sem):
    count, width = tokens_in.shape
    small = start_all([(ids_in, ids_ref), (prob_in, prob_ref)], sem.at[0])
    pairs = []
    for src, to, offset in ((tokens_in, rows_ref, 0), (grad_in, grad_ref, count + EXTRA)):
        for r in cut_rows(src, 2):
            pairs.append((src.at[r, :], to.at[r, :]))
            pairs.append((src.at[r, :], raw_ref.at[pl.ds(offset + r.start, r.size), :]))
    copies = start_all(pairs, sem.at[1])
    wait_all(small)
    rows = [ids_ref[...].astype(F32)]
    for k in range(2):
        rest = prob_ref[k : k + 1, :]
        for _ in range(3):
            rows.append(rest.astype(BF16).astype(F32))
            rest = rest - rows[-1]
    meta = jnp.concatenate(rows + [jnp.zeros((EXTRA - 8, count), F32)], axis=0).astype(BF16)
    meta_ref[...] = meta
    behind = pl.ds(count, EXTRA)
    for ref in (rows_ref, raw_ref):
        ref[behind, :count] = meta
        ref[behind, count:] = jnp.zeros((EXTRA, width - count), BF16)
    wait_all(copies)


def pack(tokens, grad, ids, probs):
    count, width = tokens.shape
    return run(
        "pack",
        pack_kernel,
        [tokens, grad, ids.T, probs.T],
        [shape(count + EXTRA, width), shape(count, width), shape(2 * count + EXTRA, width), shape(EXTRA, count)],
        held=[ANY] * 4,
        scratch=[pltpu.VMEM((2, count), jnp.int32), pltpu.VMEM((2, count), F32), pltpu.SemaphoreType.DMA((2, 8))],
    )


def split_kernel(bx_ref, by_ref, top_ref, bottom_ref, sem):
    half = top_ref.shape[0]
    bottom = pl.ds(half, bottom_ref.shape[0])
    wait_all(start_all([(by_ref.at[pl.ds(0, half), :], top_ref), (bx_ref.at[bottom, :], bottom_ref)], sem))


def split(bx, by, half, after=()):
    rows, width = bx.shape
    outs = [shape(half, width), shape(rows - half, width)]
    return run("split", split_kernel, [bx, by], outs, after, scratch=[pltpu.SemaphoreType.DMA((2,))])


def merge_kernel(own_ref, bx_ref, by_ref, da_ref, db_ref, out_ref, sem):
    half = da_ref.shape[0]
    pairs = [(ref, out_ref.at[k]) for k, ref in enumerate((own_ref, bx_ref, by_ref))]
    pairs.append((da_ref, out_ref.at[3, pl.ds(0, half), :]))
    pairs.append((db_ref, out_ref.at[3, pl.ds(half, db_ref.shape[0]), :]))
    wait_all(start_all(pairs, sem))


def merge(own, bx, by, da, db, after=()):
    outs = [shape(4, *own.shape)]
    return run("merge", merge_kernel, [own, bx, by, da, db], outs, after, scratch=[pltpu.SemaphoreType.DMA((5,))])


def warm(weights, after):
    return run("warm", lambda *refs: None, weights, [], after)


def group_rows(refs):
    own, bx, by, da, db, c_own, c_bx, c_by, c_da, c_db = refs
    for ref in (own, c_own, bx, c_bx, by, c_by):
        yield ref[...]
    for top, bottom in ((da, db), (c_da, c_db)):
        yield jnp.concatenate([top[...], bottom[...]], axis=0)


def route(me, metas, rank_ref, prob_ref):
    expert = me.astype(F32)
    named, probs = [], []
    for meta in metas:
        meta = meta.astype(F32)
        first, second = meta[0:1] == expert, meta[1:2] == expert
        p0 = (meta[2:3] + meta[3:4]) + meta[4:5]
        p1 = (meta[5:6] + meta[6:7]) + meta[7:8]
        named.append((first | second).astype(F32))
        probs.append(jnp.where(first, p0, jnp.where(second, p1, 0.0)))
    named = jnp.concatenate(named, axis=0)
    count = named.shape[1]
    earlier = lax.broadcasted_iota(jnp.int32, (count, count), 0) < lax.broadcasted_iota(
        jnp.int32, (count, count), 1
    )
    rank = nn(named.astype(BF16), earlier.astype(F32).astype(BF16))
    rank_ref[...] = jnp.where(named > 0, rank, -1.0)
    prob_ref[...] = jnp.concatenate(probs, axis=0)


def slot_rows(rows, rank, prob, capacity):
    hit = lax.broadcasted_iota(jnp.int32, (capacity, rank.shape[1]), 0).astype(F32) == rank
    picked = nn(hit.astype(F32).astype(BF16), rows)
    if prob is not None:
        picked = picked * jnp.sum(jnp.where(hit, prob, 0.0), axis=1, keepdims=True)
    return picked.astype(BF16)


def slot_range(me, k, capacity):
    return pl.ds(pl.multiple_of(jnp.bitwise_xor(me, k) * capacity, capacity), capacity)


def activate(cols, x, wg_ref, wu_ref, h_ref):
    g, u = nn(x, wg_ref[:, cols]), nn(x, wu_ref[:, cols])
    s = jax.nn.sigmoid(g)
    b = g * s
    h_ref[:, cols] = (b * u).astype(BF16)
    return u * s * (1.0 + g * (1.0 - s)), b


def forward_kernel(capacity, pos_ref, *refs):
    wg_ref, wu_ref, x_ref, rank_ref, prob_ref, h_ref, a_ref, b_ref = refs[10:]
    count, me = rank_ref.shape[1], pos_ref[0]
    groups = list(group_rows(refs[:10]))
    route(me, [rows[count:, :count] for rows in groups], rank_ref, prob_ref)
    for k, rows in enumerate(groups):
        x_ref[slot_range(me, k, capacity), :] = slot_rows(rows[:count], rank_ref[k : k + 1], None, capacity)

    def step(cols):
        a_ref[:, cols], b_ref[:, cols] = activate(cols, x_ref[...], wg_ref, wu_ref, h_ref)

    tiles(wg_ref.shape[1], step)


def forward(pos, groups, w_gate, w_up, capacity, after):
    width, hid = w_gate.shape
    slots, count = 8 * capacity, groups[0].shape[0] - EXTRA
    return run(
        "forward",
        functools.partial(forward_kernel, capacity),
        [pos, *groups, w_gate, w_up],
        [shape(slots, width)]
        + [shape(8, count, dtype=F32)] * 2
        + [shape(slots, hid)]
        + [shape(slots, hid, dtype=F32)] * 2,
        after,
        held=[SMEM] + [VMEM] * 12,
        us=6,
    )


def far_down_kernel(capacity, pos_ref, *refs):
    rank_ref, prob_ref, h_ref, dy_ref, far_ref = refs[10:]
    for k, rows in enumerate(group_rows(refs[:10])):
        rank, prob = rank_ref[k : k + 1], prob_ref[k : k + 1]
        dy_ref[slot_range(pos_ref[0], k, capacity), :] = slot_rows(rows, rank, prob, capacity)
    far_ref[...] = tn(dy_ref[:, columns(pos_ref[1], far_ref.shape[0])], h_ref[...]).astype(BF16)


def far_down_of(pos, groups, rank, prob, h, chunk, capacity):
    width = groups[0].shape[1]
    slots, hid = h.shape
    return run(
        "far_down",
        functools.partial(far_down_kernel, capacity),
        [pos, *groups, rank, prob, h],
        [shape(slots, width), shape(chunk, hid)],
        held=[SMEM] + [VMEM] * 13,
        us=3,
    )


def retreat(cols, dy, wd_ref, a, b, dg_ref, du_ref):
    dh = nn(dy, wd_ref[:, cols])
    dg_ref[:, cols] = (dh * a).astype(BF16)
    du_ref[:, cols] = (dh * b).astype(BF16)


def backward_kernel(pos_ref, x_ref, dy_ref, a_ref, b_ref, h_ref, wd_ref, dg_ref, du_ref, *outs):
    def step(cols):
        retreat(cols, dy_ref[...], wd_ref, a_ref[:, cols], b_ref[:, cols], dg_ref, du_ref)

    tiles(wd_ref.shape[1], step)
    for n, out in enumerate(outs):
        at = columns(pos_ref[1 + (n + 1) // 3], out.shape[0])
        left, right = ((x_ref, dg_ref), (x_ref, du_ref), (dy_ref, h_ref))[n if n < 2 else (n - 2) % 3]
        out[...] = tn(left[:, at], right[...]).astype(out.dtype)


def backward(pos, x, dy, a, b, h, w_down, chunk, after):
    slots, hid = a.shape
    return run(
        "backward",
        backward_kernel,
        [pos, x, dy, a, b, h, w_down],
        [shape(slots, hid)] * 2 + [shape(chunk, hid)] * 5 + [shape(chunk, hid, dtype=F32)] * 3,
        after,
        held=[SMEM] + [VMEM] * 6,
        us=9,
    )


def add_kernel(p_ref, q_ref, out_ref):
    out_ref[...] = (p_ref[...].astype(F32) + q_ref[...].astype(F32)).astype(BF16)


def add(p, q, after=()):
    return run("add", add_kernel, [p, q], [shape(*p.shape)], after)


def rows_kernel(capacity, h_ref, dg_ref, du_ref, wd_ref, wg_ref, wu_ref, out_ref):
    groups = out_ref.shape[0]
    for r in cut_rows(wd_ref, 4):
        o = nt(h_ref[...], wd_ref[r, :]).astype(BF16)
        dx = (nt(dg_ref[...], wg_ref[r, :]) + nt(du_ref[...], wu_ref[r, :])).astype(BF16)
        for k in range(groups):
            at = slice(k * capacity, (k + 1) * capacity)
            out_ref[k, :capacity, r] = o[at]
            out_ref[k, capacity:, r] = dx[at]


def rows_back(h, dg, du, w_down, w_gate, w_up, capacity, after=()):
    slots, hid = h.shape
    return run(
        "rows_back",
        functools.partial(rows_kernel, capacity),
        [h, dg, du, w_down, w_gate, w_up],
        [shape(slots // capacity, 2 * capacity, w_gate.shape[0])],
        after,
        us=7,
    )


def combine_kernel(capacity, meta_ref, rows_ref, *refs):
    outs, (held_ref, mixed_ref, grad_ref, sem_in, sem_out) = refs[:2], refs[2:]
    parts, slots, part = held_ref.shape
    arrivals = []
    for n in range(parts):
        src = rows_ref.at[:, pl.ds(n * part, part)]
        arrivals += start_all([(src, held_ref.at[n])], sem_in.at[pl.ds(n, 1)])
    count = meta_ref.shape[1]
    same = lax.broadcasted_iota(jnp.int32, (EXTRA, EXTRA), 0) == lax.broadcasted_iota(jnp.int32, (EXTRA, EXTRA), 1)
    cols = tn(meta_ref[...], same.astype(F32).astype(BF16))
    ids = cols[:, 0:2].astype(jnp.int32)
    probs = [(cols[:, k : k + 1] + cols[:, k + 1 : k + 2]) + cols[:, k + 2 : k + 3] for k in (2, 5)]
    lane = lax.broadcasted_iota(jnp.int32, (count, 128), 1)
    named = ((lane == ids[:, 0:1]) | (lane == ids[:, 1:2])).astype(F32)
    earlier = lax.broadcasted_iota(jnp.int32, (count, count), 1) < lax.broadcasted_iota(
        jnp.int32, (count, count), 0
    )
    rank = nn(earlier.astype(F32).astype(BF16), named.astype(BF16))
    place = lax.broadcasted_iota(jnp.int32, (count, slots), 1)
    hits, both = [], 0.0
    for k in range(2):
        own = ids[:, k : k + 1]
        at = jnp.sum(jnp.where(lane == own, rank, 0.0), axis=1, keepdims=True).astype(jnp.int32)
        at = own * (2 * capacity) + at
        hits.append((place == at).astype(F32).astype(BF16))
        both = both + (place == at + capacity).astype(F32)
    both = both.astype(BF16)
    copies = []
    for n in range(parts):
        arrivals[n].wait()
        rows = held_ref[n]
        mixed_ref[n] = (nn(hits[0], rows) * probs[0] + nn(hits[1], rows) * probs[1]).astype(BF16)
        grad_ref[n] = nn(both, rows).astype(BF16)
        at = pl.ds(n * part, part)
        copies += start_all(
            [(ref.at[n], out.at[:, at]) for ref, out in zip((mixed_ref, grad_ref), outs)], sem_out.at[n]
        )
    wait_all(copies)


def combine(meta, rows, capacity, after=()):
    count = meta.shape[1]
    slots, width = rows.shape
    parts = 4
    return run(
        "combine",
        functools.partial(combine_kernel, capacity),
        [meta, rows],
        [shape(count, width)] * 2,
        after,
        held=[VMEM, ANY],
        out_held=[ANY] * 2,
        scratch=[pltpu.VMEM((parts, slots, width // parts), BF16)]
        + [pltpu.VMEM((parts, count, width // parts), BF16)] * 2
        + [pltpu.SemaphoreType.DMA((parts,)), pltpu.SemaphoreType.DMA((parts, 2))],
        us=5,
    )


def partner_kernel(capacity, pos_ref, own_ref, core_ref, wg_ref, wu_ref, wd_ref, *refs):
    x_ref, dy_ref, dg_ref, du_ref, h_ref, rank_ref, prob_ref = refs
    count = rank_ref.shape[1]
    groups = [(ref, k) for ref in (own_ref, core_ref) for k in range(4)]
    route(pos_ref[0], [ref[k, count : count + EXTRA, :count] for ref, k in groups], rank_ref, prob_ref)
    for n, ref in enumerate((own_ref, core_ref)):

        @pl.loop(0, 4)
        def _(k):
            at = pl.ds(pl.multiple_of((4 * n + k) * capacity, capacity), capacity)
            rank, prob = rank_ref[pl.ds(4 * n + k, 1), :], prob_ref[pl.ds(4 * n + k, 1), :]
            x_ref[at, :] = slot_rows(ref[k, :count], rank, None, capacity)
            dy_ref[at, :] = slot_rows(ref[k, count + EXTRA :], rank, prob, capacity)

    def step(cols):
        a, b = activate(cols, x_ref[...], wg_ref, wu_ref, h_ref)
        retreat(cols, dy_ref[...], wd_ref, a, b, dg_ref, du_ref)

    tiles(wg_ref.shape[1], step)


def partner(pos, own, core, weights, capacity, count, after):
    width, hid = weights[0].shape
    slots = 8 * capacity
    return run(
        "partner",
        functools.partial(partner_kernel, capacity),
        [pos, own, core, *weights],
        [shape(slots, width)] * 2 + [shape(slots, hid)] * 3,
        after,
        held=[SMEM] + [VMEM] * 5,
        scratch=[pltpu.VMEM((8, count), F32)] * 2,
        us=7,
    )


def both_kernel(pos_ref, x_ref, dy_ref, dg_ref, du_ref, h_ref, *refs):
    for left, right, own, out in zip((x_ref, x_ref, dy_ref), (dg_ref, du_ref, h_ref), refs[:3], refs[3:]):
        out[...] = own[...] + tn(left[:, columns(pos_ref[3], out.shape[0])], right[...])


def both(pos, slots, mine, after):
    return run(
        "both",
        both_kernel,
        [pos, *slots, *mine],
        [shape(*m.shape, dtype=F32) for m in mine],
        after,
        held=[SMEM] + [VMEM] * 8,
        us=3,
    )


def local_pairs(tokens, expert_ids, gate_probs, w_gate, w_up, w_down, out_grad):
    count, top = expert_ids.shape
    width = tokens.shape[1]
    w_gate, w_up, w_down = w_gate[0], w_up[0], w_down[0]
    planes, peers = lax.axis_size("dp"), lax.axis_size("expert")
    capacity = 2 * count * top // peers
    chunk, half = width // planes, count // 2
    z = lax.axis_index("dp")
    me = lax.axis_index("expert")
    left = z < 2
    far = jnp.where(left, 3, 0)
    near = jnp.where(left, 2, 1)
    pos = jnp.stack([me, far, near, z]).astype(jnp.int32)

    def over(x, bit):
        return lax.ppermute(x, "expert", [(i, i ^ bit) for i in range(peers)])

    def swap(x):
        return lax.ppermute(x, "dp", [(i, i ^ 1) for i in range(planes)])

    def inward(x):
        return lax.ppermute(x, "dp", [(0, 1), (3, 2)])

    def across_far(x):
        return lax.ppermute(x, "dp", [(1, 3), (2, 0)])

    def across_near(x):
        return lax.ppermute(x, "dp", [(1, 2), (2, 1)])

    def relay(bx, by, half, after=()):
        top, bottom, token = split(bx, by, half, after)
        return over(top, 2), over(bottom, 4), token

    def doubled(*held):
        return held + tuple(over(t, 1) for t in held)

    rows, grad, raw, meta, _ = pack(tokens, out_grad, expert_ids, gate_probs)
    raw = swap(raw)
    bx, by = over(rows, 2), over(rows, 4)
    da, db, token = relay(bx, by, half)
    groups = doubled(rows, bx, by, da, db)
    warmed = warm([w_gate, w_up, w_down], [token])
    grad = tie(grad, [da, db])
    bx, by = over(grad, 2), over(grad, 4)
    da, db, token = relay(bx, by, half)
    cotangents = doubled(grad, bx, by, da, db)
    raw = tie(raw, [da, db])
    raw_x, raw_y = over(raw, 2), over(raw, 4)

    x, rank, prob, h, a, b, token = forward(pos, groups, w_gate, w_up, capacity, warmed)
    dy, far_down, token = far_down_of(pos, cotangents, rank, prob, h, chunk, capacity)
    in_far_down = inward(far_down)
    dg, du, far_gate, far_up, near_gate, near_up, near_down, *mine, token = backward(
        pos, x, dy, a, b, h, w_down, chunk, [token]
    )
    in_far_gate = inward(far_gate)
    back, token = rows_back(h, dg, du, w_down, w_gate, w_up, capacity, [token])
    sum_far_down, token = add(far_down, in_far_down, [token])
    got_down = [across_far(sum_far_down)]
    in_far_up = inward(tie(far_up, [token]))
    raw_a, raw_b, token = relay(raw_x, raw_y, count + EXTRA, [token])
    sum_far_gate, token = add(far_gate, in_far_gate, [token])
    got_gate = [across_far(sum_far_gate)]
    in_near_down = inward(tie(near_down, [token]))
    back = lax.all_to_all(tie(back, [raw_a, raw_b]), "expert", split_axis=0, concat_axis=0, tiled=True)
    back = back.reshape(2 * peers * capacity, width)
    sum_far_up, token = add(far_up, in_far_up, [token, got_down[0]])
    got_up = [across_far(sum_far_up)]
    in_near_gate = inward(tie(near_gate, [token]))
    raw_own, token = merge(raw, raw_x, raw_y, raw_a, raw_b, [token])
    raw_core = over(raw_own, 1)
    sum_near_down, token = add(near_down, in_near_down, [token, got_gate[0]])
    got_down.append(across_near(sum_near_down))
    in_near_up = inward(tie(near_up, [token]))
    *slots, token = partner(pos, raw_own, raw_core, (w_gate, w_up, w_down), capacity, count, [token])
    *mine, token = both(pos, slots, mine, [token])
    sum_near_gate, token = add(near_gate, in_near_gate, [token, got_up[0]])
    got_gate.append(across_near(sum_near_gate))
    sum_near_up, token = add(near_up, in_near_up, [token, got_down[1]])
    got_up.append(across_near(sum_near_up))
    mixed, tokens_grad, token = combine(meta, back, capacity, [token])

    grads = []
    for own, got in zip(mine, (got_gate, got_up, got_down)):
        total = own + got[0].astype(F32) + got[1].astype(F32)
        grads.append(total.astype(BF16)[None])
    return (mixed, tokens_grad, *grads)


def solution(mesh):
    placed = (
        P(("dp", "expert"), None),
        P(("dp", "expert"), None),
        P(("dp", "expert"), None),
        P("expert", None, None),
        P("expert", None, None),
        P("expert", None, None),
        P(("dp", "expert"), None),
    )
    paired = mesh.shape["dp"] == 4 and mesh.shape["expert"] == 8
    return jax.shard_map(
        local_pairs if paired else local_any,
        mesh=mesh,
        in_specs=placed,
        out_specs=(
            P(("dp", "expert"), None),
            P(("dp", "expert"), None),
            P("expert", "dp", None),
            P("expert", "dp", None),
            P("expert", "dp", None),
        ),
        check_vma=False,
    )
```

time: 282 us -> 248 us (0.88)
  Pallas kernels: 0 us -> 56.7 us
  waiting for transfers between devices: 142 us -> 86.8 us
  starting transfers between devices: 17.6 us -> 55.6 us
  matrix products: 37.8 us -> 0 us
  other arithmetic: 26.6 us -> 7.33 us
  between operations: 14.3 us -> 1.44 us
    ppermute x0 -> x36, waiting for transfers between devices: none -> 86.8 us  [the longest x23 29.2 us: over(): return lax.ppermute(x, 'expert', [(i, i ^ bit) for i in range(peers)])]
    all_to_all x4 -> x1, waiting for transfers between devices: 76.1 us -> 0.01 us  [local_pairs(): lax.all_to_all(tie(back, [raw_a, raw_b]), 'expert', split_axis=0, concat_...]
    reduce_scatter x1 -> x0, waiting for transfers between devices: 65.9 us -> none  [local(): lax.psum_scatter(jnp.concatenate([both, jnp.einsum('secd,sech->deh', colu...]
    pallas_call x0 -> x26, Pallas kernels: none -> 56.7 us  [the longest x19 56.7 us: run(): pl.pallas_call(body, in_specs=[ANY] * skip + list(held or [VMEM] * len(op...]
    ppermute x0 -> x36, starting transfers between devices: none -> 51 us  [the longest x3 19.2 us: across_far(): return lax.ppermute(x, 'dp', [(1, 3), (2, 0)])]
    dot_general x9 -> x0, matrix products: 37.8 us -> none  [the longest x1 5.6 us: local(): jnp.einsum('secd,edh->sech', expert_received, w_up, preferred_element_typ...]
    unnamed x21 -> x144, local copies, waits for them, and re-layouts: 7.96 us -> 38.5 us
    gather x4 -> x0, local copies, waits for them, and re-layouts: 23.1 us -> none  [the longest x1 6.39 us: local(): jnp.take(out_grad, token_of_slot, axis=0)]
  transfers between devices with their start and end apart: 5 -> 37, of which waited for: 5 -> 14; matrix products, arithmetic and copies ran while one was open for 23% -> 4% of each run, Pallas kernels for 0% -> 21%
where the time goes in v2:
time: 248 us; the launch traced here: 246 us
  waiting for transfers between devices  86.8 us (35%)
  Pallas kernels  56.7 us (23%)
  starting transfers between devices  55.6 us (22%)
  local copies, waits for them, and re-layouts  38.5 us (16%)
  other arithmetic  7.33 us (3%)
    pallas_call x19, Pallas kernels, run(): pl.pallas_call(body, in_specs=[ANY] * skip + list(held or [VMEM] * len(op...  56.7 us
    unnamed x144, local copies, waits for them, and re-layouts  38.5 us
    ppermute x23, waiting for transfers between devices, over(): return lax.ppermute(x, 'expert', [(i, i ^ bit) for i in range(peers)])  29.2 us
    ppermute x3, waiting for transfers between devices, across_near(): return lax.ppermute(x, 'dp', [(1, 2), (2, 1)])  27.9 us
    ppermute x6, waiting for transfers between devices, inward(): return lax.ppermute(x, 'dp', [(0, 1), (3, 2)])  25.2 us
    ppermute x3, starting transfers between devices, across_far(): return lax.ppermute(x, 'dp', [(1, 3), (2, 0)])  19.2 us
    ppermute x23, starting transfers between devices, over(): return lax.ppermute(x, 'expert', [(i, i ^ bit) for i in range(peers)])  14.6 us
    ppermute x3, starting transfers between devices, across_near(): return lax.ppermute(x, 'dp', [(1, 2), (2, 1)])  8.53 us
  transfers between devices with their start and end apart: 37, of which 14 were waited for; matrix products, arithmetic and copies ran while one was open for 4% of the time, Pallas kernels for 21%

profile of v2, /device:TPU:8, one launch (start us, length us, event | category | flops | bytes accessed | tf_op | source)
XLA Modules:
  0.0 246.4 jit_solution(13346122763135183637)
XLA Ops:
  8.3 12.3 %collective-permute-done.refs_0_.refs_3_ = bf16[144,2048]{1,0:T(8,128)(2,1)S(1)} collective-permute-done((bf16[144,2048]{1,0:T(8,128)(2,1)}, bf16[144,2048]{1,0:T(8,128)(2,1)S(1)}, u32[]{:S(2)}, u32[]{:S(2)}) %collective-permute-start) | collective-permute-done | bytes 589856 | tf_op jit(solution)/shard_map/ppermute | solution.py:517
  25.1 5.8 %collective-permute-done.2.refs_1_.refs_5_ = bf16[64,2048]{1,0:T(8,128)(2,1)S(1)} collective-permute-done((bf16[64,2048]{1,0:T(8,128)(2,1)S(1)}, bf16[64,2048]{1,0:T(8,128)(2,1)S(1)}, u32[]{:S(2)}, u32[]{:S(2)}) %collective-permute-start.2) | collective-permute-done | bytes 262176 | tf_op jit(solution)/shard_map/ppermute | solution.py:517
  34.4 8.9 %collective-permute-done.4.refs_0_.refs_2_ = bf16[128,2048]{1,0:T(8,128)(2,1)S(1)} collective-permute-done((bf16[128,2048]{1,0:T(8,128)(2,1)}, bf16[128,2048]{1,0:T(8,128)(2,1)S(1)}, u32[]{:S(2)}, u32[]{:S(2)}) %collective-permute-start.4) | collective-permute-done | bytes 524320 | tf_op jit(solution)/shard_map/ppermute | solution.py:517
  57.4 6.5 %forward.1 = (bf16[512,2048]{1,0:T(8,128)(2,1)S(1)}, f32[8,128]{1,0:T(8,128)S(1)}, f32[8,128]{1,0:T(8,128)S(1)}, bf16[512,768]{1,0:T(8,128)(2,1)S(1)}, f32[512,7...) custom-call(f32[8,128]{1,0:T(8,128)S(1)} %warm.1.refs_0_, s32[4]{0:T(128)S(1)} %pad_add_fusion.refs_1_.refs_0_, ...), custom_call_target="tpu_custom_call" | custom-call | flops 6000000000 | bytes 65536 | tf_op jit(solution)/shard_map/forward/pallas_call | solution.py:112
  73.9 2.7 %far_down.1 = (bf16[512,2048]{1,0:T(8,128)(2,1)S(1)}, bf16[512,768]{1,0:T(8,128)(2,1)S(1)}, f32[8,128]{1,0:T(8,128)S(1)}) custom-call(s32[4]{0:T(128)S(1)} %pad_add_fusion.refs_1_.refs_0_, bf16[128,2048]{1,0:T(8,128)(2,1)S(1)} %copy-done.31, bf16[128,2048]{1,0:T(8,128)(2,1)S(1)} %copy-done.56, bf16[128,2048]{1,0:T(8,128)(2,1)} %collective-permute-done.5.refs_1_.refs_3_, ...), custom_call_target="tpu_custom_call" | custom-call | flops 3000000000 | bytes 65536 | tf_op jit(solution)/shard_map/far_down/pallas_call | solution.py:112
  78.1 6.2 %backward.1 = (bf16[512,768]{1,0:T(8,128)(2,1)S(1)}, bf16[512,768]{1,0:T(8,128)(2,1)S(1)}, bf16[512,768]{1,0:T(8,128)(2,1)}, bf16[512,768]{1,0:T(8,128)(2,1)S(1)...) custom-call(f32[8,128]{1,0:T(8,128)S(1)} %get-tuple-element.75.refs_, ...), custom_call_target="tpu_custom_call" | custom-call | flops 8999999488 | bytes 65536 | tf_op jit(solution)/shard_map/backward/pallas_call | solution.py:112
  88.0 5.1 %rows_back.1 = (bf16[8,128,2048]{2,1,0:T(8,128)(2,1)S(1)}, f32[8,128]{1,0:T(8,128)S(1)}) custom-call(f32[8,128]{1,0:T(8,128)S(1)} %get-tuple-element.80.refs_0_, bf16[512,768]{1,0:T(8,128)(2,1)S(1)} %copy-done.63, bf16[512,768]{1,0:T(8,128)(2,1)S(1)} %get-tuple-element.81.refs_2_, bf16[512,768]{1,0:T(8,128)(2,1)S(1)} %get-tuple-element.82.refs_3_, ...), custom_call_target="tpu_custom_call" | custom-call | flops 7000000000 | bytes 65536 | tf_op jit(solution)/shard_map/rows_back/pallas_call | solution.py:112
  95.1 4.0 %collective-permute-done.18.refs_2_ = bf16[512,768]{1,0:T(8,128)(2,1)S(1)} collective-permute-done((bf16[512,768]{1,0:T(8,128)(2,1)S(1)}, bf16[512,768]{1,0:T(8,128)(2,1)S(1)}, u32[]{:S(2)}, u32[]{:S(2)}) %collective-permute-start.18) | collective-permute-done | bytes 786464 | tf_op jit(solution)/shard_map/ppermute | solution.py:523
  102.2 5.7 %collective-permute-start.23 = (bf16[512,768]{1,0:T(8,128)(2,1)}, bf16[512,768]{1,0:T(8,128)(2,1)S(1)}, u32[]{:S(2)}, u32[]{:S(2)}) collective-permute-start(bf16[512,768]{1,0:T(8,128)(2,1)} %copy-done.48), channel_id=1, source_target_pairs={{8,24},{16,0},{9,25},{17,1},{10,26},{18,2},{11,27},{19,3},{12,28},... | collective-permute-start | bytes 2359304 | tf_op jit(solution)/shard_map/ppermute | solution.py:526
  111.4 4.6 %collective-permute-done.22.refs_2_ = bf16[512,768]{1,0:T(8,128)(2,1)} collective-permute-done((bf16[512,768]{1,0:T(8,128)(2,1)}, bf16[512,768]{1,0:T(8,128)(2,1)}, u32[]{:S(2)}, u32[]{:S(2)}) %collective-permute-start.22) | collective-permute-done | bytes 786464 | tf_op jit(solution)/shard_map/ppermute | solution.py:523
  118.5 13.1 %collective-permute-done.24.refs_3_ = bf16[512,768]{1,0:T(8,128)(2,1)S(1)} collective-permute-done((bf16[512,768]{1,0:T(8,128)(2,1)}, bf16[512,768]{1,0:T(8,128)(2,1)S(1)}, u32[]{:S(2)}, u32[]{:S(2)}) %collective-permute-start.24) | collective-permute-done | bytes 786464 | tf_op jit(solution)/shard_map/ppermute | solution.py:523
  133.6 4.7 %merge.1 = (bf16[4,272,2048]{2,1,0:T(8,128)(2,1)}, f32[8,128]{1,0:T(8,128)S(1)}) custom-call(f32[8,128]{1,0:T(8,128)S(1)} %get-tuple-element.92.refs_0_.refs_1_, bf16[272,2048]{1,0:T(8,128)(2,1)S(1)} %copy-done.2, bf16[272,2048]{1,0:T(8,128)(2,1)} %collective-permute-done.20.refs_1_.refs_2_, bf16[272,2048]{1,0:T(8,128)(2,1)} %collective-permute-done.21.refs_2_.refs_3_, ...), custom_call_target="tpu_custom_call" | custom-call | flops 1000000000 | bytes 65536 | tf_op jit(solution)/shard_map/merge/pallas_call | solution.py:112
  138.4 4.6 %all-to-all-start = ((bf16[8,128,2048]{2,1,0:T(8,128)(2,1)}), bf16[8,128,2048]{2,1,0:T(8,128)(2,1)}, u32[]{:S(2)}, u32[]{:S(2)}) async-start(bf16[8,128,2048]{2,1,0:T(8,128)(2,1)} %tie.13), calls=%async_computation | async-start | bytes 8388608 | tf_op jit(solution)/shard_map/all_to_all | solution.py:566
  146.5 7.4 %collective-permute-start.27 = (bf16[512,768]{1,0:T(8,128)(2,1)}, bf16[512,768]{1,0:T(8,128)(2,1)}, u32[]{:S(2)}, u32[]{:S(2)}) collective-permute-start(bf16[512,768]{1,0:T(8,128)(2,1)} %copy-done.47), channel_id=1, source_target_pairs={{8,24},{16,0},{9,25},{17,1},{10,26},{18,2},{11,27},{19,3},{12,28},... | collective-permute-start | bytes 2359304 | tf_op jit(solution)/shard_map/ppermute | solution.py:526
  153.9 2.1 copy.23.refs_0_
  158.2 6.2 %collective-permute-start.30 = (bf16[512,768]{1,0:T(8,128)(2,1)}, bf16[512,768]{1,0:T(8,128)(2,1)}, u32[]{:S(2)}, u32[]{:S(2)}) collective-permute-start(bf16[512,768]{1,0:T(8,128)(2,1)} %copy-done.46), channel_id=1, source_target_pairs={{8,24},{16,0},{9,25},{17,1},{10,26},{18,2},{11,27},{19,3},{12,28},... | collective-permute-start | bytes 2359304 | tf_op jit(solution)/shard_map/ppermute | solution.py:526
  164.4 3.4 %collective-permute-done.28.refs_3_ = bf16[512,768]{1,0:T(8,128)(2,1)} collective-permute-done((bf16[512,768]{1,0:T(8,128)(2,1)}, bf16[512,768]{1,0:T(8,128)(2,1)}, u32[]{:S(2)}, u32[]{:S(2)}) %collective-permute-start.28) | collective-permute-done | bytes 786464 | tf_op jit(solution)/shard_map/ppermute | solution.py:523
  167.8 3.5 %collective-permute-done.27.refs_1_ = bf16[512,768]{1,0:T(8,128)(2,1)} collective-permute-done((bf16[512,768]{1,0:T(8,128)(2,1)}, bf16[512,768]{1,0:T(8,128)(2,1)}, u32[]{:S(2)}, u32[]{:S(2)}) %collective-permute-start.27) | collective-permute-done | bytes 786464 | tf_op jit(solution)/shard_map/ppermute | solution.py:526
  172.4 2.2 add.57
  175.2 2.5 %collective-permute-start.32 = (bf16[512,768]{1,0:T(8,128)(2,1)}, bf16[512,768]{1,0:T(8,128)(2,1)}, u32[]{:S(2)}, u32[]{:S(2)}) collective-permute-start(bf16[512,768]{1,0:T(8,128)(2,1)} %get-tuple-element.113), channel_id=1, source_target_pairs={{8,16},{16,8},{9,17},{17,9},{10,18},{18,10},{11,19},{19,11},{12,20... | collective-permute-start | bytes 2359304 | tf_op jit(solution)/shard_map/ppermute | solution.py:529
  182.8 11.9 %partner.1 = (bf16[512,2048]{1,0:T(8,128)(2,1)S(1)}, bf16[512,2048]{1,0:T(8,128)(2,1)S(1)}, bf16[512,768]{1,0:T(8,128)(2,1)S(1)}, bf16[512,768]{1,0:T(8,128)(2,1...) custom-call(f32[8,128]{1,0:T(8,128)S(1)} %copy-done.43, s32[4]{0:T(128)S(1)} %pad_add_fusion.refs_1_.refs_0_, ...), custom_call_target="tpu_custom_call" | custom-call | flops 7000000000 | bytes 65536 | tf_op jit(solution)/shard_map/partner/pallas_call | solution.py:112
  194.7 2.1 both.1
  196.8 2.3 add.58
  199.1 5.9 %collective-permute-done.32.refs_1_ = bf16[512,768]{1,0:T(8,128)(2,1)} collective-permute-done((bf16[512,768]{1,0:T(8,128)(2,1)}, bf16[512,768]{1,0:T(8,128)(2,1)}, u32[]{:S(2)}, u32[]{:S(2)}) %collective-permute-start.32) | collective-permute-done | bytes 786464 | tf_op jit(solution)/shard_map/ppermute | solution.py:529
  206.1 3.5 %collective-permute-start.35 = (bf16[512,768]{1,0:T(8,128)(2,1)}, bf16[512,768]{1,0:T(8,128)(2,1)}, u32[]{:S(2)}, u32[]{:S(2)}) collective-permute-start(bf16[512,768]{1,0:T(8,128)(2,1)} %get-tuple-element.123), channel_id=1, source_target_pairs={{8,16},{16,8},{9,17},{17,9},{10,18},{18,10},{11,19},{19,11},{12,20... | collective-permute-start | bytes 2359304 | tf_op jit(solution)/shard_map/ppermute | solution.py:529
  209.6 2.6 %collective-permute-start.34 = (bf16[512,768]{1,0:T(8,128)(2,1)}, bf16[512,768]{1,0:T(8,128)(2,1)}, u32[]{:S(2)}, u32[]{:S(2)}) collective-permute-start(bf16[512,768]{1,0:T(8,128)(2,1)} %get-tuple-element.121), channel_id=1, source_target_pairs={{8,16},{16,8},{9,17},{17,9},{10,18},{18,10},{11,19},{19,11},{12,20... | collective-permute-start | bytes 2359304 | tf_op jit(solution)/shard_map/ppermute | solution.py:529
  212.2 2.3 fusion.2
  214.5 5.0 %combine.1 = (bf16[128,2048]{1,0:T(8,128)(2,1)}, bf16[128,2048]{1,0:T(8,128)(2,1)}, f32[8,128]{1,0:T(8,128)}) custom-call(f32[8,128]{1,0:T(8,128)S(1)} %get-tuple-element.115.refs_0_, bf16[16,128]{1,0:T(8,128)(2,1)S(1)} %get-tuple-element.116.refs_1_, bf16[1024,2048]{1,0:T(8,128)(2,1)} %bitcast.9.refs_2_), custom_call_target="tpu_custom_call" | custom-call | flops 5000000000 | bytes 65536 | tf_op jit(solution)/shard_map/combine/pallas_call | solution.py:112
  219.5 9.3 %collective-permute-done.35 = bf16[512,768]{1,0:T(8,128)(2,1)} collective-permute-done((bf16[512,768]{1,0:T(8,128)(2,1)}, bf16[512,768]{1,0:T(8,128)(2,1)}, u32[]{:S(2)}, u32[]{:S(2)}) %collective-permute-start.35) | collective-permute-done | bytes 786464 | tf_op jit(solution)/shard_map/ppermute | solution.py:529
  228.8 2.5 %fusion.1 = bf16[1,512,768]{2,1,0:T(8,128)(2,1)} fusion(bf16[512,768]{1,0:T(8,128)(2,1)} %collective-permute-done.35, f32[512,768]{1,0:T(8,128)S(1)} %get-tuple-element.122, bf16[512,768]{1,0:T(8,128)(2,1)} %collective-permute-done.30.refs_1_), kind=kLoop, calls=%fused_computation.4 | loop fusion | flops 1966080 | bytes 3932160 | tf_op jit(solution)/shard_map/broadcast_in_dim | solution.py:587
  231.3 12.7 %collective-permute-done.34 = bf16[512,768]{1,0:T(8,128)(2,1)} collective-permute-done((bf16[512,768]{1,0:T(8,128)(2,1)}, bf16[512,768]{1,0:T(8,128)(2,1)}, u32[]{:S(2)}, u32[]{:S(2)}) %collective-permute-start.34) | collective-permute-done | bytes 786464 | tf_op jit(solution)/shard_map/ppermute | solution.py:529
  243.9 2.5 %fusion = bf16[1,512,768]{2,1,0:T(8,128)(2,1)} fusion(bf16[512,768]{1,0:T(8,128)(2,1)} %collective-permute-done.34, f32[512,768]{1,0:T(8,128)S(1)} %get-tuple-element.120, bf16[512,768]{1,0:T(8,128)(2,1)} %collective-permute-done.27.refs_1_), kind=kLoop, calls=%fused_computation.3 | loop fusion | flops 1966080 | bytes 3932160 | tf_op jit(solution)/shard_map/broadcast_in_dim | solution.py:587
  (216 shorter events, 71.0 us)
Async XLA Ops:
  5.2 15.3 %collective-permute-start = (bf16[144,2048]{1,0:T(8,128)(2,1)}, bf16[144,2048]{1,0:T(8,128)(2,1)S(1)}, u32[]{:S(2)}, u32[]{:S(2)}) collective-permute-start(bf16[144,2048]{1,0:T(8,128)(2,1)} %get-tuple-element.66.refs_2_), channel_id=1, source_target_pairs={{0,2},{1,3},{2,0},{3,1},{4,6},{5,7},{6,4},{7,5},{8,10},{9,11},{10,... | collective-permute-start | bytes 1769480 | tf_op jit(solution)/shard_map/ppermute | solution.py:517
  6.8 15.0 %collective-permute-start.1 = (bf16[144,2048]{1,0:T(8,128)(2,1)}, bf16[144,2048]{1,0:T(8,128)(2,1)S(1)}, u32[]{:S(2)}, u32[]{:S(2)}) collective-permute-start(bf16[144,2048]{1,0:T(8,128)(2,1)} %get-tuple-element.66.refs_2_), channel_id=1, source_target_pairs={{0,4},{1,5},{2,6},{3,7},{4,0},{5,1},{6,2},{7,3},{8,12},{9,13},{10,... | collective-permute-start | bytes 1769480 | tf_op jit(solution)/shard_map/ppermute | solution.py:517
  24.1 24.8 %collective-permute-start.19 = (bf16[272,2048]{1,0:T(8,128)(2,1)S(1)}, bf16[272,2048]{1,0:T(8,128)(2,1)S(1)}, u32[]{:S(2)}, u32[]{:S(2)}) collective-permute-start(bf16[272,2048]{1,0:T(8,128)(2,1)S(1)} %get-tuple-element.86), channel_id=1, source_target_pairs={{0,8},{8,0},{16,24},{24,16},{1,9},{9,1},{17,25},{25,17},{2,10},{10... | collective-permute-start | bytes 3342344 | tf_op jit(solution)/shard_map/ppermute | solution.py:520
  31.8 11.6 %collective-permute-start.4 = (bf16[128,2048]{1,0:T(8,128)(2,1)}, bf16[128,2048]{1,0:T(8,128)(2,1)S(1)}, u32[]{:S(2)}, u32[]{:S(2)}) collective-permute-start(bf16[128,2048]{1,0:T(8,128)(2,1)} %tie.7.refs_1_), channel_id=1, source_target_pairs={{0,2},{1,3},{2,0},{3,1},{4,6},{5,7},{6,4},{7,5},{8,10},{9,11},{10,... | collective-permute-start | bytes 1572872 | tf_op jit(solution)/shard_map/ppermute | solution.py:517
  32.5 11.7 %collective-permute-start.5 = (bf16[128,2048]{1,0:T(8,128)(2,1)}, bf16[128,2048]{1,0:T(8,128)(2,1)}, u32[]{:S(2)}, u32[]{:S(2)}) collective-permute-start(bf16[128,2048]{1,0:T(8,128)(2,1)} %tie.7.refs_1_), channel_id=1, source_target_pairs={{0,4},{1,5},{2,6},{3,7},{4,0},{5,1},{6,2},{7,3},{8,12},{9,13},{10,... | collective-permute-start | bytes 1572872 | tf_op jit(solution)/shard_map/ppermute | solution.py:517
  33.9 21.4 %collective-permute-start.14 = (bf16[144,2048]{1,0:T(8,128)(2,1)}, bf16[144,2048]{1,0:T(8,128)(2,1)}, u32[]{:S(2)}, u32[]{:S(2)}) collective-permute-start(bf16[144,2048]{1,0:T(8,128)(2,1)} %copy-done.49), channel_id=1, source_target_pairs={{0,1},{1,0},{2,3},{3,2},{4,5},{5,4},{6,7},{7,6},{8,9},{9,8},{10,11... | collective-permute-start | bytes 1769480 | tf_op jit(solution)/shard_map/ppermute | solution.py:517
  33.9 22.4 %collective-permute-start.15 = (bf16[144,2048]{1,0:T(8,128)(2,1)}, bf16[144,2048]{1,0:T(8,128)(2,1)}, u32[]{:S(2)}, u32[]{:S(2)}) collective-permute-start(bf16[144,2048]{1,0:T(8,128)(2,1)} %copy-done.51), channel_id=1, source_target_pairs={{0,1},{1,0},{2,3},{3,2},{4,5},{5,4},{6,7},{7,6},{8,9},{9,8},{10,11... | collective-permute-start | bytes 1769480 | tf_op jit(solution)/shard_map/ppermute | solution.py:517
  44.2 12.6 %collective-permute-start.17 = (bf16[80,2048]{1,0:T(8,128)(2,1)}, bf16[80,2048]{1,0:T(8,128)(2,1)}, u32[]{:S(2)}, u32[]{:S(2)}) collective-permute-start(bf16[80,2048]{1,0:T(8,128)(2,1)} %copy-done.32), channel_id=1, source_target_pairs={{0,1},{1,0},{2,3},{3,2},{4,5},{5,4},{6,7},{7,6},{8,9},{9,8},{10,11... | collective-permute-start | bytes 983048 | tf_op jit(solution)/shard_map/ppermute | solution.py:517
  46.9 10.0 %collective-permute-start.6 = (bf16[64,2048]{1,0:T(8,128)(2,1)}, bf16[64,2048]{1,0:T(8,128)(2,1)S(1)}, u32[]{:S(2)}, u32[]{:S(2)}) collective-permute-start(bf16[64,2048]{1,0:T(8,128)(2,1)} %get-tuple-element.69), channel_id=1, source_target_pairs={{0,2},{1,3},{2,0},{3,1},{4,6},{5,7},{6,4},{7,5},{8,10},{9,11},{10,... | collective-permute-start | bytes 786440 | tf_op jit(solution)/shard_map/ppermute | solution.py:517
  56.3 12.2 %collective-permute-start.8 = (bf16[128,2048]{1,0:T(8,128)(2,1)S(1)}, bf16[128,2048]{1,0:T(8,128)(2,1)S(1)}, u32[]{:S(2)}, u32[]{:S(2)}) collective-permute-start(bf16[128,2048]{1,0:T(8,128)(2,1)S(1)} %copy-done.31), channel_id=1, source_target_pairs={{0,1},{1,0},{2,3},{3,2},{4,5},{5,4},{6,7},{7,6},{8,9},{9,8},{10,11... | collective-permute-start | bytes 1572872 | tf_op jit(solution)/shard_map/ppermute | solution.py:517
  56.3 14.6 %collective-permute-start.10 = (bf16[128,2048]{1,0:T(8,128)(2,1)}, bf16[128,2048]{1,0:T(8,128)(2,1)S(1)}, u32[]{:S(2)}, u32[]{:S(2)}) collective-permute-start(bf16[128,2048]{1,0:T(8,128)(2,1)} %collective-permute-done.5.refs_1_.refs_3_), channel_id=1, source_target_pairs={{0,1},{1,0},{2,3},{3,2},{4,5},{5,4},{6,7},{7,6},{8,9},{9,8},{10,11... | collective-permute-start | bytes 1572872 | tf_op jit(solution)/shard_map/ppermute | solution.py:517
  56.8 14.0 %collective-permute-start.9 = (bf16[128,2048]{1,0:T(8,128)(2,1)S(1)}, bf16[128,2048]{1,0:T(8,128)(2,1)}, u32[]{:S(2)}, u32[]{:S(2)}) collective-permute-start(bf16[128,2048]{1,0:T(8,128)(2,1)S(1)} %copy-done.56), channel_id=1, source_target_pairs={{0,1},{1,0},{2,3},{3,2},{4,5},{5,4},{6,7},{7,6},{8,9},{9,8},{10,11... | collective-permute-start | bytes 1572872 | tf_op jit(solution)/shard_map/ppermute | solution.py:517
  56.9 12.6 %collective-permute-start.11 = (bf16[64,2048]{1,0:T(8,128)(2,1)S(1)}, bf16[64,2048]{1,0:T(8,128)(2,1)S(1)}, u32[]{:S(2)}, u32[]{:S(2)}) collective-permute-start(bf16[64,2048]{1,0:T(8,128)(2,1)S(1)} %collective-permute-done.6.refs_4_.refs_1_), channel_id=1, source_target_pairs={{0,1},{1,0},{2,3},{3,2},{4,5},{5,4},{6,7},{7,6},{8,9},{9,8},{10,11... | collective-permute-start | bytes 786440 | tf_op jit(solution)/shard_map/ppermute | solution.py:517
  57.3 13.5 %collective-permute-start.12 = (bf16[64,2048]{1,0:T(8,128)(2,1)S(1)}, bf16[64,2048]{1,0:T(8,128)(2,1)S(1)}, u32[]{:S(2)}, u32[]{:S(2)}) collective-permute-start(bf16[64,2048]{1,0:T(8,128)(2,1)S(1)} %collective-permute-done.7.refs_5_.refs_2_), channel_id=1, source_target_pairs={{0,1},{1,0},{2,3},{3,2},{4,5},{5,4},{6,7},{7,6},{8,9},{9,8},{10,11... | collective-permute-start | bytes 786440 | tf_op jit(solution)/shard_map/ppermute | solution.py:517
  68.5 39.3 %collective-permute-start.20 = (bf16[272,2048]{1,0:T(8,128)(2,1)}, bf16[272,2048]{1,0:T(8,128)(2,1)}, u32[]{:S(2)}, u32[]{:S(2)}) collective-permute-start(bf16[272,2048]{1,0:T(8,128)(2,1)} %tie.8.refs_1_), channel_id=1, source_target_pairs={{0,2},{1,3},{2,0},{3,1},{4,6},{5,7},{6,4},{7,5},{8,10},{9,11},{10,... | collective-permute-start | bytes 3342344 | tf_op jit(solution)/shard_map/ppermute | solution.py:517
  69.4 38.4 %collective-permute-start.21 = (bf16[272,2048]{1,0:T(8,128)(2,1)}, bf16[272,2048]{1,0:T(8,128)(2,1)}, u32[]{:S(2)}, u32[]{:S(2)}) collective-permute-start(bf16[272,2048]{1,0:T(8,128)(2,1)} %tie.8.refs_1_), channel_id=1, source_target_pairs={{0,4},{1,5},{2,6},{3,7},{4,0},{5,1},{6,2},{7,3},{8,12},{9,13},{10,... | collective-permute-start | bytes 3342344 | tf_op jit(solution)/shard_map/ppermute | solution.py:517
  76.6 22.4 %collective-permute-start.18 = (bf16[512,768]{1,0:T(8,128)(2,1)S(1)}, bf16[512,768]{1,0:T(8,128)(2,1)S(1)}, u32[]{:S(2)}, u32[]{:S(2)}) collective-permute-start(bf16[512,768]{1,0:T(8,128)(2,1)S(1)} %get-tuple-element.84.refs_1_), channel_id=1, source_target_pairs={{0,8},{24,16},{1,9},{25,17},{2,10},{26,18},{3,11},{27,19},{4,12},{... | collective-permute-start | bytes 2359304 | tf_op jit(solution)/shard_map/ppermute | solution.py:523
  86.5 29.6 %collective-permute-start.22 = (bf16[512,768]{1,0:T(8,128)(2,1)}, bf16[512,768]{1,0:T(8,128)(2,1)}, u32[]{:S(2)}, u32[]{:S(2)}) collective-permute-start(bf16[512,768]{1,0:T(8,128)(2,1)} %get-tuple-element.88.refs_1_), channel_id=1, source_target_pairs={{0,8},{24,16},{1,9},{25,17},{2,10},{26,18},{3,11},{27,19},{4,12},{... | collective-permute-start | bytes 2359304 | tf_op jit(solution)/shard_map/ppermute | solution.py:523
  100.7 30.9 %collective-permute-start.24 = (bf16[512,768]{1,0:T(8,128)(2,1)}, bf16[512,768]{1,0:T(8,128)(2,1)S(1)}, u32[]{:S(2)}, u32[]{:S(2)}) collective-permute-start(bf16[512,768]{1,0:T(8,128)(2,1)} %tie.9), channel_id=1, source_target_pairs={{0,8},{24,16},{1,9},{25,17},{2,10},{26,18},{3,11},{27,19},{4,12},{... | collective-permute-start | bytes 2359304 | tf_op jit(solution)/shard_map/ppermute | solution.py:523
  102.2 29.5 %collective-permute-start.23 = (bf16[512,768]{1,0:T(8,128)(2,1)}, bf16[512,768]{1,0:T(8,128)(2,1)S(1)}, u32[]{:S(2)}, u32[]{:S(2)}) collective-permute-start(bf16[512,768]{1,0:T(8,128)(2,1)} %copy-done.48), channel_id=1, source_target_pairs={{8,24},{16,0},{9,25},{17,1},{10,26},{18,2},{11,27},{19,3},{12,28},... | collective-permute-start | bytes 2359304 | tf_op jit(solution)/shard_map/ppermute | solution.py:526
  109.6 23.9 %collective-permute-start.25 = (bf16[144,2048]{1,0:T(8,128)(2,1)S(1)}, bf16[144,2048]{1,0:T(8,128)(2,1)S(1)}, u32[]{:S(2)}, u32[]{:S(2)}) collective-permute-start(bf16[144,2048]{1,0:T(8,128)(2,1)S(1)} %get-tuple-element.93), channel_id=1, source_target_pairs={{0,2},{1,3},{2,0},{3,1},{4,6},{5,7},{6,4},{7,5},{8,10},{9,11},{10,... | collective-permute-start | bytes 1769480 | tf_op jit(solution)/shard_map/ppermute | solution.py:517
  110.9 22.6 %collective-permute-start.26 = (bf16[128,2048]{1,0:T(8,128)(2,1)S(1)}, bf16[128,2048]{1,0:T(8,128)(2,1)S(1)}, u32[]{:S(2)}, u32[]{:S(2)}) collective-permute-start(bf16[128,2048]{1,0:T(8,128)(2,1)S(1)} %get-tuple-element.94), channel_id=1, source_target_pairs={{0,4},{1,5},{2,6},{3,7},{4,0},{5,1},{6,2},{7,3},{8,12},{9,13},{10,... | collective-permute-start | bytes 1572872 | tf_op jit(solution)/shard_map/ppermute | solution.py:517
  138.4 40.6 %collective-permute-start.29 = (bf16[4,272,2048]{2,1,0:T(8,128)(2,1)}, bf16[4,272,2048]{2,1,0:T(8,128)(2,1)}, u32[]{:S(2)}, u32[]{:S(2)}) collective-permute-start(bf16[4,272,2048]{2,1,0:T(8,128)(2,1)} %get-tuple-element.99.refs_2_), channel_id=1, source_target_pairs={{0,1},{1,0},{2,3},{3,2},{4,5},{5,4},{6,7},{7,6},{8,9},{9,8},{10,11... | collective-permute-start | bytes 13369352 | tf_op jit(solution)/shard_map/ppermute | solution.py:517
  138.4 76.1 %all-to-all-start = ((bf16[8,128,2048]{2,1,0:T(8,128)(2,1)}), bf16[8,128,2048]{2,1,0:T(8,128)(2,1)}, u32[]{:S(2)}, u32[]{:S(2)}) async-start(bf16[8,128,2048]{2,1,0:T(8,128)(2,1)} %tie.13), calls=%async_computation | async-start | bytes 8388608 | tf_op jit(solution)/shard_map/all_to_all | solution.py:566
  145.1 22.7 %collective-permute-start.28 = (bf16[512,768]{1,0:T(8,128)(2,1)}, bf16[512,768]{1,0:T(8,128)(2,1)}, u32[]{:S(2)}, u32[]{:S(2)}) collective-permute-start(bf16[512,768]{1,0:T(8,128)(2,1)} %tie.10), channel_id=1, source_target_pairs={{0,8},{24,16},{1,9},{25,17},{2,10},{26,18},{3,11},{27,19},{4,12},{... | collective-permute-start | bytes 2359304 | tf_op jit(solution)/shard_map/ppermute | solution.py:523
  146.5 24.7 %collective-permute-start.27 = (bf16[512,768]{1,0:T(8,128)(2,1)}, bf16[512,768]{1,0:T(8,128)(2,1)}, u32[]{:S(2)}, u32[]{:S(2)}) collective-permute-start(bf16[512,768]{1,0:T(8,128)(2,1)} %copy-done.47), channel_id=1, source_target_pairs={{8,24},{16,0},{9,25},{17,1},{10,26},{18,2},{11,27},{19,3},{12,28},... | collective-permute-start | bytes 2359304 | tf_op jit(solution)/shard_map/ppermute | solution.py:526
  156.9 39.9 %collective-permute-start.31 = (bf16[512,768]{1,0:T(8,128)(2,1)}, bf16[512,768]{1,0:T(8,128)(2,1)}, u32[]{:S(2)}, u32[]{:S(2)}) collective-permute-start(bf16[512,768]{1,0:T(8,128)(2,1)} %tie.11), channel_id=1, source_target_pairs={{0,8},{24,16},{1,9},{25,17},{2,10},{26,18},{3,11},{27,19},{4,12},{... | collective-permute-start | bytes 2359304 | tf_op jit(solution)/shard_map/ppermute | solution.py:523
  158.2 38.6 %collective-permute-start.30 = (bf16[512,768]{1,0:T(8,128)(2,1)}, bf16[512,768]{1,0:T(8,128)(2,1)}, u32[]{:S(2)}, u32[]{:S(2)}) collective-permute-start(bf16[512,768]{1,0:T(8,128)(2,1)} %copy-done.46), channel_id=1, source_target_pairs={{8,24},{16,0},{9,25},{17,1},{10,26},{18,2},{11,27},{19,3},{12,28},... | collective-permute-start | bytes 2359304 | tf_op jit(solution)/shard_map/ppermute | solution.py:526
  175.2 29.9 %collective-permute-start.32 = (bf16[512,768]{1,0:T(8,128)(2,1)}, bf16[512,768]{1,0:T(8,128)(2,1)}, u32[]{:S(2)}, u32[]{:S(2)}) collective-permute-start(bf16[512,768]{1,0:T(8,128)(2,1)} %get-tuple-element.113), channel_id=1, source_target_pairs={{8,16},{16,8},{9,17},{17,9},{10,18},{18,10},{11,19},{19,11},{12,20... | collective-permute-start | bytes 2359304 | tf_op jit(solution)/shard_map/ppermute | solution.py:529
  177.6 27.4 %collective-permute-start.33 = (bf16[512,768]{1,0:T(8,128)(2,1)}, bf16[512,768]{1,0:T(8,128)(2,1)S(1)}, u32[]{:S(2)}, u32[]{:S(2)}) collective-permute-start(bf16[512,768]{1,0:T(8,128)(2,1)} %tie.12), channel_id=1, source_target_pairs={{0,8},{24,16},{1,9},{25,17},{2,10},{26,18},{3,11},{27,19},{4,12},{... | collective-permute-start | bytes 2359304 | tf_op jit(solution)/shard_map/ppermute | solution.py:523
  206.1 22.7 %collective-permute-start.35 = (bf16[512,768]{1,0:T(8,128)(2,1)}, bf16[512,768]{1,0:T(8,128)(2,1)}, u32[]{:S(2)}, u32[]{:S(2)}) collective-permute-start(bf16[512,768]{1,0:T(8,128)(2,1)} %get-tuple-element.123), channel_id=1, source_target_pairs={{8,16},{16,8},{9,17},{17,9},{10,18},{18,10},{11,19},{19,11},{12,20... | collective-permute-start | bytes 2359304 | tf_op jit(solution)/shard_map/ppermute | solution.py:529
  209.6 34.3 %collective-permute-start.34 = (bf16[512,768]{1,0:T(8,128)(2,1)}, bf16[512,768]{1,0:T(8,128)(2,1)}, u32[]{:S(2)}, u32[]{:S(2)}) collective-permute-start(bf16[512,768]{1,0:T(8,128)(2,1)} %get-tuple-element.121), channel_id=1, source_target_pairs={{8,16},{16,8},{9,17},{17,9},{10,18},{18,10},{11,19},{19,11},{12,20... | collective-permute-start | bytes 2359304 | tf_op jit(solution)/shard_map/ppermute | solution.py:529
  (75 other events, 327.9 us)

commit v3 on v2

--- a/solution.py
+++ b/solution.py
@@ -102,7 +102,7 @@
     return jax.ShapeDtypeStruct(sizes, dtype)
 
 
-def run(name, kernel, operands, outs, after=(), held=None, out_held=None, scratch=(), us=1.0, limit=14):
+def run(name, kernel, operands, outs, after=(), held=None, out_held=None, scratch=(), us=1.0, limit=11):
     skip, count = len(after), len(operands) + len(outs)
 
     def body(*refs):
@@ -128,6 +128,7 @@
         out_specs=ANY,
         out_shape=jax.ShapeDtypeStruct(x.shape, x.dtype),
         input_output_aliases={0: 0},
+        compiler_params=pltpu.CompilerParams(vmem_limit_bytes=1024 * 1024),
         cost_estimate=pl.CostEstimate(flops=8, bytes_accessed=8, transcendentals=0),
         name="tie",
     )(x, *after)
@@ -160,14 +161,20 @@
     return [pl.ds(n * size, size) for n in range(parts)]
 
 
-def pack_kernel(tokens_in, grad_in, ids_in, prob_in, rows_ref, grad_ref, raw_ref, meta_ref, ids_ref, prob_ref, sem):
+def pack_kernel(pos_ref, tokens_in, grad_in, ids_in, prob_in, out_ref, rows_ref, far_ref, rest_ref, raw_ref, meta_ref, ids_ref, prob_ref, sem):
     count, width = tokens_in.shape
+    for n in range(pos_ref.shape[0]):
+        out_ref[n] = pos_ref[n]
     small = start_all([(ids_in, ids_ref), (prob_in, prob_ref)], sem.at[0])
+    chunk, rest = far_ref.shape[1], rest_ref.shape[1]
+    others = pl.ds(pl.multiple_of(jnp.where(pos_ref[1] == 0, chunk, 0), chunk), rest)
     pairs = []
-    for src, to, offset in ((tokens_in, rows_ref, 0), (grad_in, grad_ref, count + EXTRA)):
-        for r in cut_rows(src, 2):
-            pairs.append((src.at[r, :], to.at[r, :]))
-            pairs.append((src.at[r, :], raw_ref.at[pl.ds(offset + r.start, r.size), :]))
+    for r in cut_rows(tokens_in, 2):
+        pairs.append((tokens_in.at[r, :], rows_ref.at[r, :]))
+        pairs.append((tokens_in.at[r, :], raw_ref.at[r, :]))
+        pairs.append((grad_in.at[r, :], raw_ref.at[pl.ds(count + EXTRA + r.start, r.size), :]))
+    pairs.append((grad_in.at[:, columns(pos_ref[1], chunk)], far_ref))
+    pairs.append((grad_in.at[:, others], rest_ref))
     copies = start_all(pairs, sem.at[1])
     wait_all(small)
     rows = [ids_ref[...].astype(F32)]
@@ -185,45 +192,35 @@
     wait_all(copies)
 
 
-def pack(tokens, grad, ids, probs):
+def pack(pos, tokens, grad, ids, probs, chunk):
     count, width = tokens.shape
     return run(
         "pack",
         pack_kernel,
-        [tokens, grad, ids.T, probs.T],
-        [shape(count + EXTRA, width), shape(count, width), shape(2 * count + EXTRA, width), shape(EXTRA, count)],
-        held=[ANY] * 4,
+        [pos, tokens, grad, ids.T, probs.T],
+        [shape(*pos.shape, dtype=jnp.int32), shape(count + EXTRA, width)]
+        + [shape(count, chunk), shape(count, width - chunk)]
+        + [shape(2 * count + EXTRA, width), shape(EXTRA, count)],
+        held=[SMEM] + [ANY] * 4,
+        out_held=[SMEM] + [VMEM] * 5,
+        limit=4,
         scratch=[pltpu.VMEM((2, count), jnp.int32), pltpu.VMEM((2, count), F32), pltpu.SemaphoreType.DMA((2, 8))],
     )
 
 
-def split_kernel(bx_ref, by_ref, top_ref, bottom_ref, sem):
+def split_kernel(bx_ref, by_ref, top_ref, bottom_ref):
     half = top_ref.shape[0]
-    bottom = pl.ds(half, bottom_ref.shape[0])
-    wait_all(start_all([(by_ref.at[pl.ds(0, half), :], top_ref), (bx_ref.at[bottom, :], bottom_ref)], sem))
+    top_ref[...] = by_ref[:half]
+    bottom_ref[...] = bx_ref[half:]
 
 
 def split(bx, by, half, after=()):
     rows, width = bx.shape
-    outs = [shape(half, width), shape(rows - half, width)]
-    return run("split", split_kernel, [bx, by], outs, after, scratch=[pltpu.SemaphoreType.DMA((2,))])
-
-
-def merge_kernel(own_ref, bx_ref, by_ref, da_ref, db_ref, out_ref, sem):
-    half = da_ref.shape[0]
-    pairs = [(ref, out_ref.at[k]) for k, ref in enumerate((own_ref, bx_ref, by_ref))]
-    pairs.append((da_ref, out_ref.at[3, pl.ds(0, half), :]))
-    pairs.append((db_ref, out_ref.at[3, pl.ds(half, db_ref.shape[0]), :]))
-    wait_all(start_all(pairs, sem))
-
-
-def merge(own, bx, by, da, db, after=()):
-    outs = [shape(4, *own.shape)]
-    return run("merge", merge_kernel, [own, bx, by, da, db], outs, after, scratch=[pltpu.SemaphoreType.DMA((5,))])
+    return run("split", split_kernel, [bx, by], [shape(half, width), shape(rows - half, width)], after, limit=4)
 
 
 def warm(weights, after):
-    return run("warm", lambda *refs: None, weights, [], after)
+    return run("warm", lambda *refs: None, weights, [], after, limit=11)
 
 
 def group_rows(refs):
@@ -306,22 +303,22 @@
 
 
 def far_down_kernel(capacity, pos_ref, *refs):
-    rank_ref, prob_ref, h_ref, dy_ref, far_ref = refs[10:]
-    for k, rows in enumerate(group_rows(refs[:10])):
+    rank_ref, prob_ref, h_ref, dy_ref, far_ref = refs[8:]
+    for k, ref in enumerate(refs[:8]):
         rank, prob = rank_ref[k : k + 1], prob_ref[k : k + 1]
-        dy_ref[slot_range(pos_ref[0], k, capacity), :] = slot_rows(rows, rank, prob, capacity)
-    far_ref[...] = tn(dy_ref[:, columns(pos_ref[1], far_ref.shape[0])], h_ref[...]).astype(BF16)
-
-
-def far_down_of(pos, groups, rank, prob, h, chunk, capacity):
-    width = groups[0].shape[1]
+        dy_ref[slot_range(pos_ref[0], k, capacity), :] = slot_rows(ref[...], rank, prob, capacity)
+    far_ref[...] = tn(dy_ref[...], h_ref[...]).astype(BF16)
+
+
+def far_down_of(pos, groups, rank, prob, h, capacity):
+    chunk = groups[0].shape[1]
     slots, hid = h.shape
     return run(
         "far_down",
         functools.partial(far_down_kernel, capacity),
         [pos, *groups, rank, prob, h],
-        [shape(slots, width), shape(chunk, hid)],
-        held=[SMEM] + [VMEM] * 13,
+        [shape(slots, chunk), shape(chunk, hid)],
+        held=[SMEM] + [VMEM] * 11,
         us=3,
     )
 
@@ -332,36 +329,85 @@
     du_ref[:, cols] = (dh * b).astype(BF16)
 
 
-def backward_kernel(pos_ref, x_ref, dy_ref, a_ref, b_ref, h_ref, wd_ref, dg_ref, du_ref, *outs):
+def backward_kernel(capacity, pos_ref, *refs):
+    far_ref, rank_ref, prob_ref, x_ref, a_ref, b_ref, wd_ref, dy_ref, dg_ref, du_ref, out_ref = refs[10:]
+    chunk, rest = far_ref.shape[1], refs[0].shape[1]
+    far = columns(pos_ref[1], chunk)
+    dy_ref[:, far] = far_ref[...]
+    others = pl.ds(pl.multiple_of(jnp.where(pos_ref[1] == 0, chunk, 0), chunk), rest)
+    for k, rows in enumerate(group_rows(refs[:10])):
+        rank, prob = rank_ref[k : k + 1], prob_ref[k : k + 1]
+        dy_ref[slot_range(pos_ref[0], k, capacity), others] = slot_rows(rows, rank, prob, capacity)
+
     def step(cols):
         retreat(cols, dy_ref[...], wd_ref, a_ref[:, cols], b_ref[:, cols], dg_ref, du_ref)
+        out_ref[:, cols] = tn(x_ref[:, far], dg_ref[:, cols]).astype(BF16)
 
     tiles(wd_ref.shape[1], step)
+
+
+def backward(pos, groups, far_rows, rank, prob, x, a, b, w_down, capacity, after):
+    slots, hid = a.shape
+    width, chunk = x.shape[1], far_rows.shape[1]
+    return run(
+        "backward",
+        functools.partial(backward_kernel, capacity),
+        [pos, *groups, far_rows, rank, prob, x, a, b, w_down],
+        [shape(slots, width)] + [shape(slots, hid)] * 2 + [shape(chunk, hid)],
+        after,
+        held=[SMEM] + [VMEM] * 17,
+        us=1,
+        limit=12,
+    )
+
+
+def gradients_kernel(pos_ref, x_ref, dy_ref, dg_ref, du_ref, h_ref, *outs):
     for n, out in enumerate(outs):
-        at = columns(pos_ref[1 + (n + 1) // 3], out.shape[0])
-        left, right = ((x_ref, dg_ref), (x_ref, du_ref), (dy_ref, h_ref))[n if n < 2 else (n - 2) % 3]
+        at = columns(pos_ref[1 + (n + 2) // 3], out.shape[0])
+        left, right = ((x_ref, dg_ref), (x_ref, du_ref), (dy_ref, h_ref))[1 if n == 0 else (n - 1) % 3]
         out[...] = tn(left[:, at], right[...]).astype(out.dtype)
 
 
-def backward(pos, x, dy, a, b, h, w_down, chunk, after):
-    slots, hid = a.shape
-    return run(
-        "backward",
-        backward_kernel,
-        [pos, x, dy, a, b, h, w_down],
-        [shape(slots, hid)] * 2 + [shape(chunk, hid)] * 5 + [shape(chunk, hid, dtype=F32)] * 3,
-        after,
-        held=[SMEM] + [VMEM] * 6,
-        us=9,
-    )
-
-
-def add_kernel(p_ref, q_ref, out_ref):
-    out_ref[...] = (p_ref[...].astype(F32) + q_ref[...].astype(F32)).astype(BF16)
-
-
-def add(p, q, after=()):
-    return run("add", add_kernel, [p, q], [shape(*p.shape)], after)
+def gradients(pos, x, dy, dg, du, h, chunk, after):
+    return run(
+        "gradients",
+        gradients_kernel,
+        [pos, x, dy, dg, du, h],
+        [shape(chunk, h.shape[1])] * 7,
+        after,
+        held=[SMEM] + [VMEM] * 5,
+        us=0.5,
+    )
+
+
+def step_kernel(extra, pos_ref, raw_ref, mine_ref, got_ref, *refs):
+    out_ref = refs[-1 - extra[1]]
+    total = (mine_ref[...].astype(F32) + got_ref[...].astype(F32)).astype(BF16)
+    out_ref[...] = jnp.where(pos_ref[4] == 1, raw_ref[...], total)
+    if extra == (2, 2):
+        bx_ref, by_ref, _, top_ref, bottom_ref = refs
+        half = top_ref.shape[0]
+        top_ref[...] = by_ref[:half]
+        bottom_ref[...] = bx_ref[half:]
+    if extra == (5, 1):
+        half = refs[3].shape[0]
+        for k in range(3):
+            refs[-1][k] = refs[k][...]
+        refs[-1][3, :half] = refs[3][...]
+        refs[-1][3, half:] = refs[4][...]
+
+
+def step(pos, raw, mine, got, after, extra=(), outs=()):
+    return run(
+        "step",
+        functools.partial(step_kernel, (len(extra), len(outs))),
+        [pos, raw, mine, got, *extra],
+        [shape(*mine.shape), *outs],
+        after,
+        held=[SMEM] + [VMEM] * (3 + len(extra)),
+        us=8,
+        limit=14 if extra else 6,
+    )
 
 
 def rows_kernel(capacity, h_ref, dg_ref, du_ref, wd_ref, wg_ref, wu_ref, out_ref):
@@ -484,7 +530,8 @@
 
 def both_kernel(pos_ref, x_ref, dy_ref, dg_ref, du_ref, h_ref, *refs):
     for left, right, own, out in zip((x_ref, x_ref, dy_ref), (dg_ref, du_ref, h_ref), refs[:3], refs[3:]):
-        out[...] = own[...] + tn(left[:, columns(pos_ref[3], out.shape[0])], right[...])
+        total = own[...].astype(F32) + tn(left[:, columns(pos_ref[3], out.shape[0])], right[...])
+        out[...] = total.astype(BF16)
 
 
 def both(pos, slots, mine, after):
@@ -492,7 +539,7 @@
         "both",
         both_kernel,
         [pos, *slots, *mine],
-        [shape(*m.shape, dtype=F32) for m in mine],
+        [shape(*m.shape) for m in mine],
         after,
         held=[SMEM] + [VMEM] * 8,
         us=3,
@@ -511,7 +558,8 @@
     left = z < 2
     far = jnp.where(left, 3, 0)
     near = jnp.where(left, 2, 1)
-    pos = jnp.stack([me, far, near, z]).astype(jnp.int32)
+    outer = ((z == 0) | (z == planes - 1)).astype(jnp.int32)
+    pos = jnp.stack([me, far, near, z, outer]).astype(jnp.int32)
 
     def over(x, bit):
         return lax.ppermute(x, "expert", [(i, i ^ bit) for i in range(peers)])
@@ -519,14 +567,10 @@
     def swap(x):
         return lax.ppermute(x, "dp", [(i, i ^ 1) for i in range(planes)])
 
-    def inward(x):
-        return lax.ppermute(x, "dp", [(0, 1), (3, 2)])
-
-    def across_far(x):
-        return lax.ppermute(x, "dp", [(1, 3), (2, 0)])
-
-    def across_near(x):
-        return lax.ppermute(x, "dp", [(1, 2), (2, 1)])
+    inwards, across, middle = [(0, 1), (3, 2)], [(1, 3), (2, 0)], [(1, 2), (2, 1)]
+
+    def along(x, pairs):
+        return lax.ppermute(x, "dp", pairs)
 
     def relay(bx, by, half, after=()):
         top, bottom, token = split(bx, by, half, after)
@@ -535,55 +579,58 @@
     def doubled(*held):
         return held + tuple(over(t, 1) for t in held)
 
-    rows, grad, raw, meta, _ = pack(tokens, out_grad, expert_ids, gate_probs)
+    pos, rows, far_grad, rest_grad, raw, meta, _ = pack(pos, tokens, out_grad, expert_ids, gate_probs, chunk)
     raw = swap(raw)
     bx, by = over(rows, 2), over(rows, 4)
-    da, db, token = relay(bx, by, half)
+    warmed = warm([w_gate, w_up, w_down], [meta])
+    da, db, token = relay(bx, by, half, warmed)
     groups = doubled(rows, bx, by, da, db)
-    warmed = warm([w_gate, w_up, w_down], [token])
-    grad = tie(grad, [da, db])
-    bx, by = over(grad, 2), over(grad, 4)
-    da, db, token = relay(bx, by, half)
-    cotangents = doubled(grad, bx, by, da, db)
+    far_grad = tie(far_grad, [da, db, raw])
+    far_groups = []
+    for f in (far_grad, over(far_grad, 2), over(far_grad, 4), over(far_grad, 6)):
+        far_groups += [f, over(f, 1)]
+    rest_grad = tie(rest_grad, [da, db])
+    bx, by = over(rest_grad, 2), over(rest_grad, 4)
+    x, rank, prob, h, a, b, token = forward(pos, groups, w_gate, w_up, capacity, [])
+    far_rows, far_down, token = far_down_of(pos, far_groups, rank, prob, h, capacity)
+    da, db, _ = relay(bx, by, half, [token])
+    rest_groups = doubled(rest_grad, bx, by, da, db)
     raw = tie(raw, [da, db])
     raw_x, raw_y = over(raw, 2), over(raw, 4)
 
-    x, rank, prob, h, a, b, token = forward(pos, groups, w_gate, w_up, capacity, warmed)
-    dy, far_down, token = far_down_of(pos, cotangents, rank, prob, h, chunk, capacity)
-    in_far_down = inward(far_down)
-    dg, du, far_gate, far_up, near_gate, near_up, near_down, *mine, token = backward(
-        pos, x, dy, a, b, h, w_down, chunk, [token]
-    )
-    in_far_gate = inward(far_gate)
-    back, token = rows_back(h, dg, du, w_down, w_gate, w_up, capacity, [token])
-    sum_far_down, token = add(far_down, in_far_down, [token])
-    got_down = [across_far(sum_far_down)]
-    in_far_up = inward(tie(far_up, [token]))
-    raw_a, raw_b, token = relay(raw_x, raw_y, count + EXTRA, [token])
-    sum_far_gate, token = add(far_gate, in_far_gate, [token])
-    got_gate = [across_far(sum_far_gate)]
-    in_near_down = inward(tie(near_down, [token]))
-    back = lax.all_to_all(tie(back, [raw_a, raw_b]), "expert", split_axis=0, concat_axis=0, tiled=True)
-    back = back.reshape(2 * peers * capacity, width)
-    sum_far_up, token = add(far_up, in_far_up, [token, got_down[0]])
-    got_up = [across_far(sum_far_up)]
-    in_near_gate = inward(tie(near_gate, [token]))
-    raw_own, token = merge(raw, raw_x, raw_y, raw_a, raw_b, [token])
+    y1 = along(far_down, inwards)
+    dy, dg, du, far_gate, token = backward(
+        pos, rest_groups, far_rows, rank, prob, x, a, b, w_down, capacity, [token]
+    )
+    y2 = along(far_gate, inwards)
+    far_up, near_gate, near_up, near_down, *mine, token = gradients(pos, x, dy, dg, du, h, chunk, [y1])
+    halves = [shape(count + EXTRA, width), shape(count, width)]
+    x3, top, bottom, token = step(pos, far_up, far_down, y1, [token], [raw_x, raw_y], halves)
+    y3 = along(x3, inwards + across)
+    raw_a, raw_b = over(top, 2), over(bottom, 4)
+    back, _ = rows_back(h, dg, du, w_down, w_gate, w_up, capacity)
+    back = lax.all_to_all(back, "expert", split_axis=0, concat_axis=0, tiled=True)
+    x4, token = step(pos, near_down, far_gate, y2, [token])
+    y4 = along(x4, inwards + across)
+    blocks = [raw, raw_x, raw_y, raw_a, raw_b]
+    x5, raw_own, token = step(pos, near_gate, far_up, y3, [token], blocks, [shape(4, *raw.shape)])
+    y5 = along(x5, inwards + across)
+    near_up = tie(near_up, [token])
+    y6 = along(near_up, inwards)
     raw_core = over(raw_own, 1)
-    sum_near_down, token = add(near_down, in_near_down, [token, got_gate[0]])
-    got_down.append(across_near(sum_near_down))
-    in_near_up = inward(tie(near_up, [token]))
+    x6, token = step(pos, near_down, near_down, y4, [token])
+    z_down = along(x6, middle)
+    x7, token = step(pos, near_gate, near_gate, y5, [token])
+    z_gate = along(x7, middle)
     *slots, token = partner(pos, raw_own, raw_core, (w_gate, w_up, w_down), capacity, count, [token])
-    *mine, token = both(pos, slots, mine, [token])
-    sum_near_gate, token = add(near_gate, in_near_gate, [token, got_up[0]])
-    got_gate.append(across_near(sum_near_gate))
-    sum_near_up, token = add(near_up, in_near_up, [token, got_down[1]])
-    got_up.append(across_near(sum_near_up))
-    mixed, tokens_grad, token = combine(meta, back, capacity, [token])
+    x8, token = step(pos, near_up, near_up, y6, [token])
+    z_up = along(x8, middle)
+    *mine, _ = both(pos, slots, mine, [token])
+    mixed, tokens_grad, _ = combine(meta, back.reshape(2 * peers * capacity, width), capacity, [token])
 
     grads = []
-    for own, got in zip(mine, (got_gate, got_up, got_down)):
-        total = own + got[0].astype(F32) + got[1].astype(F32)
+    for own, far_sum, near_sum in zip(mine, (y4, y5, y3), (z_gate, z_up, z_down)):
+        total = own.astype(F32) + jnp.where(outer == 1, far_sum, near_sum).astype(F32)
         grads.append(total.astype(BF16)[None])
     return (mixed, tokens_grad, *grads)
 

time: 248 us -> 212 us (0.85)
  local copies, waits for them, and re-layouts: 38.5 us -> 20.3 us
  starting transfers between devices: 55.6 us -> 41 us
  waiting for transfers between devices: 86.8 us -> 93.1 us
  Pallas kernels: 56.7 us -> 51.4 us
  other arithmetic: 7.33 us -> 3.62 us
    ppermute x12 -> x9, starting transfers between devices: 36 us -> 16.3 us  [along(): return lax.ppermute(x, 'dp', pairs)]
    unnamed x144 -> x74, local copies, waits for them, and re-layouts: 38.5 us -> 20.2 us
    pallas_call x19 -> x18, Pallas kernels: 56.7 us -> 51.4 us  [run(): pl.pallas_call(body, in_specs=[ANY] * skip + list(held or [VMEM] * len(op...]
    ppermute x12 -> x9, waiting for transfers between devices: 56.6 us -> 61.8 us  [along(): return lax.ppermute(x, 'dp', pairs)]
    ppermute x23 -> x30, starting transfers between devices: 14.6 us -> 19.7 us  [over(): return lax.ppermute(x, 'expert', [(i, i ^ bit) for i in range(peers)])]
    broadcast_in_dim x3, other arithmetic: 7.26 us -> 3.62 us  [local_pairs(): grads.append(total.astype(BF16)[None])]
    ppermute x23 -> x30, waiting for transfers between devices: 29.2 us -> 30.2 us  [over(): return lax.ppermute(x, 'expert', [(i, i ^ bit) for i in range(peers)])]
  transfers between devices with their start and end apart: 37 -> 41, of which waited for: 14 -> 21; matrix products, arithmetic and copies ran while one was open for 4% -> 1% of each run, Pallas kernels for 21% -> 22%
where the time goes in v3:
time: 212 us; the launch traced here: 211 us
  waiting for transfers between devices  93.1 us (44%)
  Pallas kernels  51.4 us (24%)
  starting transfers between devices  41 us (19%)
  local copies, waits for them, and re-layouts  20.3 us (10%)
  other arithmetic  3.62 us (2%)
    ppermute x9, waiting for transfers between devices, along(): return lax.ppermute(x, 'dp', pairs)  61.8 us
    pallas_call x18, Pallas kernels, run(): pl.pallas_call(body, in_specs=[ANY] * skip + list(held or [VMEM] * len(op...  51.4 us
    ppermute x30, waiting for transfers between devices, over(): return lax.ppermute(x, 'expert', [(i, i ^ bit) for i in range(peers)])  30.2 us
    unnamed x74, local copies, waits for them, and re-layouts  20.2 us
    ppermute x30, starting transfers between devices, over(): return lax.ppermute(x, 'expert', [(i, i ^ bit) for i in range(peers)])  19.7 us
    ppermute x9, starting transfers between devices, along(): return lax.ppermute(x, 'dp', pairs)  16.3 us
    all_to_all x1, starting transfers between devices, local_pairs(): lax.all_to_all(back, 'expert', split_axis=0, concat_axis=0, tiled=True)  4.58 us
  transfers between devices with their start and end apart: 41, of which 21 were waited for; matrix products, arithmetic and copies ran while one was open for 1% of the time, Pallas kernels for 22%

profile of v3, /device:TPU:8, one launch (start us, length us, event | category | flops | bytes accessed | tf_op | source)
XLA Modules:
  0.0 210.6 jit_solution(13420725005845782750)
XLA Ops:
  5.7 1.6 collective-permute-start
  9.2 1.9 copy-done.2
  11.1 1.9 copy-done.6
  13.0 7.8 %collective-permute-done.refs_1_.refs_2_ = bf16[144,2048]{1,0:T(8,128)(2,1)S(1)} collective-permute-done((bf16[144,2048]{1,0:T(8,128)(2,1)S(1)}, bf16[144,2048]{1,0:T(8,128)(2,1)S(1)}, u32[]{:S(2)}, u32[]{:S(2)}) %collective-permute-start) | collective-permute-done | bytes 589856 | tf_op jit(solution)/shard_map/ppermute | solution.py:565
  24.9 4.6 %collective-permute-done.2.refs_1_.refs_4_ = bf16[64,2048]{1,0:T(8,128)(2,1)S(1)} collective-permute-done((bf16[64,2048]{1,0:T(8,128)(2,1)S(1)}, bf16[64,2048]{1,0:T(8,128)(2,1)S(1)}, u32[]{:S(2)}, u32[]{:S(2)}) %collective-permute-start.2) | collective-permute-done | bytes 262176 | tf_op jit(solution)/shard_map/ppermute | solution.py:565
  29.5 3.8 %collective-permute-done.3.refs_2_.refs_5_ = bf16[80,2048]{1,0:T(8,128)(2,1)S(1)} collective-permute-done((bf16[80,2048]{1,0:T(8,128)(2,1)S(1)}, bf16[80,2048]{1,0:T(8,128)(2,1)S(1)}, u32[]{:S(2)}, u32[]{:S(2)}) %collective-permute-start.3) | collective-permute-done | bytes 327712 | tf_op jit(solution)/shard_map/ppermute | solution.py:565
  42.3 2.3 %collective-permute-done.8.refs_5_ = bf16[128,512]{1,0:T(8,128)(2,1)S(1)} collective-permute-done((bf16[128,512]{1,0:T(8,128)(2,1)S(1)}, bf16[128,512]{1,0:T(8,128)(2,1)S(1)}, u32[]{:S(2)}, u32[]{:S(2)}) %collective-permute-start.8) | collective-permute-done | bytes 131104 | tf_op jit(solution)/shard_map/ppermute | solution.py:565
  45.8 5.5 %forward.1 = (bf16[512,2048]{1,0:T(8,128)(2,1)S(1)}, f32[8,128]{1,0:T(8,128)S(1)}, f32[8,128]{1,0:T(8,128)S(1)}, bf16[512,768]{1,0:T(8,128)(2,1)S(1)}, f32[512,7...) custom-call(s32[5]{0:T(128)S(1)} %get-tuple-element.63.refs_0_.refs_1_, ...), custom_call_target="tpu_custom_call" | custom-call | flops 6000000000 | bytes 65536 | tf_op jit(solution)/shard_map/forward/pallas_call | solution.py:112
  55.5 4.7 %collective-permute-done.20.refs_5_.refs_1_ = bf16[64,1536]{1,0:T(8,128)(2,1)S(1)} collective-permute-done((bf16[64,1536]{1,0:T(8,128)(2,1)S(1)}, bf16[64,1536]{1,0:T(8,128)(2,1)S(1)}, u32[]{:S(2)}, u32[]{:S(2)}) %collective-permute-start.20) | collective-permute-done | bytes 196640 | tf_op jit(solution)/shard_map/ppermute | solution.py:565
  62.5 1.7 collective-permute-start.28
  69.3 5.0 %backward.1 = (bf16[512,2048]{1,0:T(8,128)(2,1)S(1)}, bf16[512,768]{1,0:T(8,128)(2,1)S(1)}, bf16[512,768]{1,0:T(8,128)(2,1)S(1)}, bf16[512,768]{1,0:T(8,128)(2,1)S(1)}, f32[8,128]{1,0:T(8,128)}) custom-call(f32[8,128]{1,0:T(8,128)S(1)} %get-tuple-element.75.refs_0_, s32[5]{0:T(128)S(1)} %get-tuple-element.63.refs_0_.refs_1_, ...), custom_call_target="tpu_custom_call" | custom-call | flops 1000000000 | bytes 65536 | tf_op jit(solution)/shard_map/backward/pallas_call | solution.py:112
  75.6 11.0 %collective-permute-done.17.refs_0_.refs_4_ = bf16[512,768]{1,0:T(8,128)(2,1)S(1)} collective-permute-done((bf16[512,768]{1,0:T(8,128)(2,1)S(1)}, bf16[512,768]{1,0:T(8,128)(2,1)S(1)}, u32[]{:S(2)}, u32[]{:S(2)}) %collective-permute-start.17) | collective-permute-done | bytes 786464 | tf_op jit(solution)/shard_map/ppermute | solution.py:573
  86.6 3.7 %gradients.1 = (bf16[512,768]{1,0:T(8,128)(2,1)S(1)}, bf16[512,768]{1,0:T(8,128)(2,1)S(1)}, bf16[512,768]{1,0:T(8,128)(2,1)S(1)}, bf16[512,768]{1,0:T(8,128)(2,1...) custom-call(bf16[512,768]{1,0:T(8,128)(2,1)S(1)} %collective-permute, ...), custom_call_target="tpu_custom_call" | custom-call | flops 500000000 | bytes 65536 | tf_op jit(solution)/shard_map/gradients/pallas_call | solution.py:112
  93.8 9.6 %collective-permute-done.29.refs_4_ = bf16[512,768]{1,0:T(8,128)(2,1)S(1)} collective-permute-done((bf16[512,768]{1,0:T(8,128)(2,1)S(1)}, bf16[512,768]{1,0:T(8,128)(2,1)S(1)}, u32[]{:S(2)}, u32[]{:S(2)}) %collective-permute-start.29) | collective-permute-done | bytes 786464 | tf_op jit(solution)/shard_map/ppermute | solution.py:573
  103.4 1.6 step.7
  105.1 13.0 %collective-permute-done.30.refs_4_ = bf16[512,768]{1,0:T(8,128)(2,1)S(1)} collective-permute-done((bf16[512,768]{1,0:T(8,128)(2,1)S(1)}, bf16[512,768]{1,0:T(8,128)(2,1)S(1)}, u32[]{:S(2)}, u32[]{:S(2)}) %collective-permute-start.30) | collective-permute-done | bytes 786464 | tf_op jit(solution)/shard_map/ppermute | solution.py:573
  118.0 3.1 %step.8 = (bf16[512,768]{1,0:T(8,128)(2,1)S(1)}, bf16[4,272,2048]{2,1,0:T(8,128)(2,1)}, f32[8,128]{1,0:T(8,128)S(1)}) custom-call(f32[8,128]{1,0:T(8,128)S(1)} %get-tuple-element.90.refs_0_, s32[5]{0:T(128)S(1)} %get-tuple-element.63.refs_0_.refs_1_, bf16[512,768]{1,0:T(8,128)(2,1)S(1)} %get-tuple-element.91.refs_2_.refs_3_, ...), custom_call_target="tpu_custom_call" | custom-call | flops 8000000000 | bytes 65536 | tf_op jit(solution)/shard_map/step/pallas_call | solution.py:112
  122.6 2.5 %collective-permute-start.34 = (bf16[512,768]{1,0:T(8,128)(2,1)}, bf16[512,768]{1,0:T(8,128)(2,1)}, u32[]{:S(2)}, u32[]{:S(2)}) collective-permute-start(bf16[512,768]{1,0:T(8,128)(2,1)} %copy-done.32), channel_id=1, source_target_pairs={{0,8},{24,16},{8,24},{16,0},{1,9},{25,17},{9,25},{17,1},{2,10},{26... | collective-permute-start | bytes 2359304 | tf_op jit(solution)/shard_map/ppermute | solution.py:573
  125.0 1.9 copy-done.4
  126.9 1.9 copy-done.8
  132.2 5.1 %rows_back.1 = (bf16[8,128,2048]{2,1,0:T(8,128)(2,1)S(1)}, f32[8,128]{1,0:T(8,128)}) custom-call(bf16[512,768]{1,0:T(8,128)(2,1)S(1)} %copy-done.15, bf16[512,768]{1,0:T(8,128)(2,1)S(1)} %copy-done.19, bf16[512,768]{1,0:T(8,128)(2,1)S(1)} %copy-done.21, bf16[2048,768]{1,0:T(8,128)(2,1)S(1)} %bitcast.19, bf16[2048,768]{1,0:T(8,128)(2,1)S(1)} %bitcast.23, ...), custom_call_target="tpu_custom_call" | custom-call | flops 7000000000 | bytes 65536 | tf_op jit(solution)/shard_map/rows_back/pallas_call | solution.py:112
  137.3 2.0 copy-done.1
  139.3 4.6 %all-to-all-start = ((bf16[8,128,2048]{2,1,0:T(8,128)(2,1)}), bf16[8,128,2048]{2,1,0:T(8,128)(2,1)}, u32[]{:S(2)}, u32[]{:S(2)}) async-start(bf16[8,128,2048]{2,1,0:T(8,128)(2,1)} %copy-done.1), calls=%async_computation | async-start | bytes 8388608 | tf_op jit(solution)/shard_map/all_to_all | solution.py:612
  148.7 2.4 %collective-permute-start.39 = (bf16[512,768]{1,0:T(8,128)(2,1)S(1)}, bf16[512,768]{1,0:T(8,128)(2,1)S(1)}, u32[]{:S(2)}, u32[]{:S(2)}) collective-permute-start(bf16[512,768]{1,0:T(8,128)(2,1)S(1)} %get-tuple-element.120), channel_id=1, source_target_pairs={{8,16},{16,8},{9,17},{17,9},{10,18},{18,10},{11,19},{19,11},{12,20... | collective-permute-start | bytes 2359304 | tf_op jit(solution)/shard_map/ppermute | solution.py:573
  151.1 8.4 %collective-permute-done.34.refs_4_ = bf16[512,768]{1,0:T(8,128)(2,1)} collective-permute-done((bf16[512,768]{1,0:T(8,128)(2,1)}, bf16[512,768]{1,0:T(8,128)(2,1)}, u32[]{:S(2)}, u32[]{:S(2)}) %collective-permute-start.34) | collective-permute-done | bytes 786464 | tf_op jit(solution)/shard_map/ppermute | solution.py:573
  161.1 3.6 %collective-permute-start.37 = (bf16[512,768]{1,0:T(8,128)(2,1)S(1)}, bf16[512,768]{1,0:T(8,128)(2,1)S(1)}, u32[]{:S(2)}, u32[]{:S(2)}) collective-permute-start(bf16[512,768]{1,0:T(8,128)(2,1)S(1)} %get-tuple-element.116), channel_id=1, source_target_pairs={{8,16},{16,8},{9,17},{17,9},{10,18},{18,10},{11,19},{19,11},{12,20... | collective-permute-start | bytes 2359304 | tf_op jit(solution)/shard_map/ppermute | solution.py:573
  164.7 11.9 %partner.1 = (bf16[512,2048]{1,0:T(8,128)(2,1)S(1)}, bf16[512,2048]{1,0:T(8,128)(2,1)S(1)}, bf16[512,768]{1,0:T(8,128)(2,1)S(1)}, bf16[512,768]{1,0:T(8,128)(2,1...) custom-call(f32[8,128]{1,0:T(8,128)S(1)} %get-tuple-element.99.refs_0_, ...), custom_call_target="tpu_custom_call" | custom-call | flops 7000000000 | bytes 65536 | tf_op jit(solution)/shard_map/partner/pallas_call | solution.py:112
  177.4 2.7 %collective-permute-start.38 = (bf16[512,768]{1,0:T(8,128)(2,1)S(1)}, bf16[512,768]{1,0:T(8,128)(2,1)S(1)}, u32[]{:S(2)}, u32[]{:S(2)}) collective-permute-start(bf16[512,768]{1,0:T(8,128)(2,1)S(1)} %get-tuple-element.118), channel_id=1, source_target_pairs={{8,16},{16,8},{9,17},{17,9},{10,18},{18,10},{11,19},{19,11},{12,20... | collective-permute-start | bytes 2359304 | tf_op jit(solution)/shard_map/ppermute | solution.py:573
  180.2 2.1 both.1
  182.2 10.5 %collective-permute-done.37 = bf16[512,768]{1,0:T(8,128)(2,1)S(1)} collective-permute-done((bf16[512,768]{1,0:T(8,128)(2,1)S(1)}, bf16[512,768]{1,0:T(8,128)(2,1)S(1)}, u32[]{:S(2)}, u32[]{:S(2)}) %collective-permute-start.37) | collective-permute-done | bytes 786464 | tf_op jit(solution)/shard_map/ppermute | solution.py:573
  195.2 4.9 %combine.1 = (bf16[128,2048]{1,0:T(8,128)(2,1)}, bf16[128,2048]{1,0:T(8,128)(2,1)}, f32[8,128]{1,0:T(8,128)}) custom-call(f32[8,128]{1,0:T(8,128)S(1)} %get-tuple-element.103.refs_0_, bf16[16,128]{1,0:T(8,128)(2,1)S(1)} %get-tuple-element.65.refs_0_.refs_1_, bf16[1024,2048]{1,0:T(8,128)(2,1)} %bitcast.10.refs_2_), custom_call_target="tpu_custom_call" | custom-call | flops 5000000000 | bytes 65536 | tf_op jit(solution)/shard_map/combine/pallas_call | solution.py:112
  200.1 9.3 %collective-permute-done.38 = bf16[512,768]{1,0:T(8,128)(2,1)S(1)} collective-permute-done((bf16[512,768]{1,0:T(8,128)(2,1)S(1)}, bf16[512,768]{1,0:T(8,128)(2,1)S(1)}, u32[]{:S(2)}, u32[]{:S(2)}) %collective-permute-start.38) | collective-permute-done | bytes 786464 | tf_op jit(solution)/shard_map/ppermute | solution.py:573
  (150 shorter events, 53.2 us)
Async XLA Ops:
  5.7 15.1 %collective-permute-start = (bf16[144,2048]{1,0:T(8,128)(2,1)S(1)}, bf16[144,2048]{1,0:T(8,128)(2,1)S(1)}, u32[]{:S(2)}, u32[]{:S(2)}) collective-permute-start(bf16[144,2048]{1,0:T(8,128)(2,1)S(1)} %get-tuple-element.66.refs_1_), channel_id=1, source_target_pairs={{0,2},{1,3},{2,0},{3,1},{4,6},{5,7},{6,4},{7,5},{8,10},{9,11},{10,... | collective-permute-start | bytes 1769480 | tf_op jit(solution)/shard_map/ppermute | solution.py:565
  7.2 14.8 %collective-permute-start.1 = (bf16[144,2048]{1,0:T(8,128)(2,1)S(1)}, bf16[144,2048]{1,0:T(8,128)(2,1)S(1)}, u32[]{:S(2)}, u32[]{:S(2)}) collective-permute-start(bf16[144,2048]{1,0:T(8,128)(2,1)S(1)} %get-tuple-element.66.refs_1_), channel_id=1, source_target_pairs={{0,4},{1,5},{2,6},{3,7},{4,0},{5,1},{6,2},{7,3},{8,12},{9,13},{10,... | collective-permute-start | bytes 1769480 | tf_op jit(solution)/shard_map/ppermute | solution.py:565
  8.8 25.7 %collective-permute-start.4 = (bf16[272,2048]{1,0:T(8,128)(2,1)S(1)}, bf16[272,2048]{1,0:T(8,128)(2,1)S(1)}, u32[]{:S(2)}, u32[]{:S(2)}) collective-permute-start(bf16[272,2048]{1,0:T(8,128)(2,1)S(1)} %get-tuple-element.69), channel_id=1, source_target_pairs={{0,8},{8,0},{16,24},{24,16},{1,9},{9,1},{17,25},{25,17},{2,10},{10... | collective-permute-start | bytes 3342344 | tf_op jit(solution)/shard_map/ppermute | solution.py:568
  22.7 6.9 %collective-permute-start.2 = (bf16[64,2048]{1,0:T(8,128)(2,1)S(1)}, bf16[64,2048]{1,0:T(8,128)(2,1)S(1)}, u32[]{:S(2)}, u32[]{:S(2)}) collective-permute-start(bf16[64,2048]{1,0:T(8,128)(2,1)S(1)} %get-tuple-element.67), channel_id=1, source_target_pairs={{0,2},{1,3},{2,0},{3,1},{4,6},{5,7},{6,4},{7,5},{8,10},{9,11},{10,... | collective-permute-start | bytes 786440 | tf_op jit(solution)/shard_map/ppermute | solution.py:565
  23.2 11.3 %collective-permute-start.12 = (bf16[144,2048]{1,0:T(8,128)(2,1)S(1)}, bf16[144,2048]{1,0:T(8,128)(2,1)S(1)}, u32[]{:S(2)}, u32[]{:S(2)}) collective-permute-start(bf16[144,2048]{1,0:T(8,128)(2,1)S(1)} %get-tuple-element.66.refs_1_), channel_id=1, source_target_pairs={{0,1},{1,0},{2,3},{3,2},{4,5},{5,4},{6,7},{7,6},{8,9},{9,8},{10,11... | collective-permute-start | bytes 1769480 | tf_op jit(solution)/shard_map/ppermute | solution.py:565
  23.2 10.1 %collective-permute-start.3 = (bf16[80,2048]{1,0:T(8,128)(2,1)S(1)}, bf16[80,2048]{1,0:T(8,128)(2,1)S(1)}, u32[]{:S(2)}, u32[]{:S(2)}) collective-permute-start(bf16[80,2048]{1,0:T(8,128)(2,1)S(1)} %get-tuple-element.68), channel_id=1, source_target_pairs={{0,4},{1,5},{2,6},{3,7},{4,0},{5,1},{6,2},{7,3},{8,12},{9,13},{10,... | collective-permute-start | bytes 983048 | tf_op jit(solution)/shard_map/ppermute | solution.py:565
  24.7 11.6 %collective-permute-start.13 = (bf16[144,2048]{1,0:T(8,128)(2,1)S(1)}, bf16[144,2048]{1,0:T(8,128)(2,1)S(1)}, u32[]{:S(2)}, u32[]{:S(2)}) collective-permute-start(bf16[144,2048]{1,0:T(8,128)(2,1)S(1)} %collective-permute-done.refs_1_.refs_2_), channel_id=1, source_target_pairs={{0,1},{1,0},{2,3},{3,2},{4,5},{5,4},{6,7},{7,6},{8,9},{9,8},{10,11... | collective-permute-start | bytes 1769480 | tf_op jit(solution)/shard_map/ppermute | solution.py:565
  29.5 8.4 %collective-permute-start.14 = (bf16[144,2048]{1,0:T(8,128)(2,1)S(1)}, bf16[144,2048]{1,0:T(8,128)(2,1)S(1)}, u32[]{:S(2)}, u32[]{:S(2)}) collective-permute-start(bf16[144,2048]{1,0:T(8,128)(2,1)S(1)} %collective-permute-done.1.refs_2_.refs_3_), channel_id=1, source_target_pairs={{0,1},{1,0},{2,3},{3,2},{4,5},{5,4},{6,7},{7,6},{8,9},{9,8},{10,11... | collective-permute-start | bytes 1769480 | tf_op jit(solution)/shard_map/ppermute | solution.py:565
  34.5 10.7 %collective-permute-start.16 = (bf16[80,2048]{1,0:T(8,128)(2,1)S(1)}, bf16[80,2048]{1,0:T(8,128)(2,1)S(1)}, u32[]{:S(2)}, u32[]{:S(2)}) collective-permute-start(bf16[80,2048]{1,0:T(8,128)(2,1)S(1)} %collective-permute-done.3.refs_2_.refs_5_), channel_id=1, source_target_pairs={{0,1},{1,0},{2,3},{3,2},{4,5},{5,4},{6,7},{7,6},{8,9},{9,8},{10,11... | collective-permute-start | bytes 983048 | tf_op jit(solution)/shard_map/ppermute | solution.py:565
  36.3 8.2 %collective-permute-start.8 = (bf16[128,512]{1,0:T(8,128)(2,1)S(1)}, bf16[128,512]{1,0:T(8,128)(2,1)S(1)}, u32[]{:S(2)}, u32[]{:S(2)}) collective-permute-start(bf16[128,512]{1,0:T(8,128)(2,1)S(1)} %tie.4.refs_1_), channel_id=1, source_target_pairs={{0,4},{1,5},{2,6},{3,7},{4,0},{5,1},{6,2},{7,3},{8,12},{9,13},{10,... | collective-permute-start | bytes 393224 | tf_op jit(solution)/shard_map/ppermute | solution.py:565
  37.9 7.4 %collective-permute-start.10 = (bf16[128,512]{1,0:T(8,128)(2,1)S(1)}, bf16[128,512]{1,0:T(8,128)(2,1)S(1)}, u32[]{:S(2)}, u32[]{:S(2)}) collective-permute-start(bf16[128,512]{1,0:T(8,128)(2,1)S(1)} %tie.4.refs_1_), channel_id=1, source_target_pairs={{0,6},{1,7},{2,4},{3,5},{4,2},{5,3},{6,0},{7,1},{8,14},{9,15},{10,... | collective-permute-start | bytes 393224 | tf_op jit(solution)/shard_map/ppermute | solution.py:565
  38.5 14.2 %collective-permute-start.18 = (bf16[128,1536]{1,0:T(8,128)(2,1)S(1)}, bf16[128,1536]{1,0:T(8,128)(2,1)S(1)}, u32[]{:S(2)}, u32[]{:S(2)}) collective-permute-start(bf16[128,1536]{1,0:T(8,128)(2,1)S(1)} %tie.5.refs_2_), channel_id=1, source_target_pairs={{0,2},{1,3},{2,0},{3,1},{4,6},{5,7},{6,4},{7,5},{8,10},{9,11},{10,... | collective-permute-start | bytes 1179656 | tf_op jit(solution)/shard_map/ppermute | solution.py:565
  41.0 11.9 %collective-permute-start.19 = (bf16[128,1536]{1,0:T(8,128)(2,1)S(1)}, bf16[128,1536]{1,0:T(8,128)(2,1)S(1)}, u32[]{:S(2)}, u32[]{:S(2)}) collective-permute-start(bf16[128,1536]{1,0:T(8,128)(2,1)S(1)} %tie.5.refs_2_), channel_id=1, source_target_pairs={{0,4},{1,5},{2,6},{3,7},{4,0},{5,1},{6,2},{7,3},{8,12},{9,13},{10,... | collective-permute-start | bytes 1179656 | tf_op jit(solution)/shard_map/ppermute | solution.py:565
  44.5 6.8 %collective-permute-start.7 = (bf16[128,512]{1,0:T(8,128)(2,1)S(1)}, bf16[128,512]{1,0:T(8,128)(2,1)S(1)}, u32[]{:S(2)}, u32[]{:S(2)}) collective-permute-start(bf16[128,512]{1,0:T(8,128)(2,1)S(1)} %collective-permute-done.6.refs_3_), channel_id=1, source_target_pairs={{0,1},{1,0},{2,3},{3,2},{4,5},{5,4},{6,7},{7,6},{8,9},{9,8},{10,11... | collective-permute-start | bytes 393224 | tf_op jit(solution)/shard_map/ppermute | solution.py:565
  53.5 6.8 %collective-permute-start.20 = (bf16[64,1536]{1,0:T(8,128)(2,1)S(1)}, bf16[64,1536]{1,0:T(8,128)(2,1)S(1)}, u32[]{:S(2)}, u32[]{:S(2)}) collective-permute-start(bf16[64,1536]{1,0:T(8,128)(2,1)S(1)} %get-tuple-element.77), channel_id=1, source_target_pairs={{0,2},{1,3},{2,0},{3,1},{4,6},{5,7},{6,4},{7,5},{8,10},{9,11},{10,... | collective-permute-start | bytes 589832 | tf_op jit(solution)/shard_map/ppermute | solution.py:565
  54.7 6.5 %collective-permute-start.21 = (bf16[64,1536]{1,0:T(8,128)(2,1)S(1)}, bf16[64,1536]{1,0:T(8,128)(2,1)S(1)}, u32[]{:S(2)}, u32[]{:S(2)}) collective-permute-start(bf16[64,1536]{1,0:T(8,128)(2,1)S(1)} %get-tuple-element.78), channel_id=1, source_target_pairs={{0,4},{1,5},{2,6},{3,7},{4,0},{5,1},{6,2},{7,3},{8,12},{9,13},{10,... | collective-permute-start | bytes 589832 | tf_op jit(solution)/shard_map/ppermute | solution.py:565
  55.5 10.1 %collective-permute-start.22 = (bf16[128,1536]{1,0:T(8,128)(2,1)S(1)}, bf16[128,1536]{1,0:T(8,128)(2,1)S(1)}, u32[]{:S(2)}, u32[]{:S(2)}) collective-permute-start(bf16[128,1536]{1,0:T(8,128)(2,1)S(1)} %tie.5.refs_2_), channel_id=1, source_target_pairs={{0,1},{1,0},{2,3},{3,2},{4,5},{5,4},{6,7},{7,6},{8,9},{9,8},{10,11... | collective-permute-start | bytes 1179656 | tf_op jit(solution)/shard_map/ppermute | solution.py:565
  61.2 29.2 %collective-permute-start.27 = (bf16[272,2048]{1,0:T(8,128)(2,1)S(1)}, bf16[272,2048]{1,0:T(8,128)(2,1)S(1)}, u32[]{:S(2)}, u32[]{:S(2)}) collective-permute-start(bf16[272,2048]{1,0:T(8,128)(2,1)S(1)} %tie.6.refs_5_), channel_id=1, source_target_pairs={{0,2},{1,3},{2,0},{3,1},{4,6},{5,7},{6,4},{7,5},{8,10},{9,11},{10,... | collective-permute-start | bytes 3342344 | tf_op jit(solution)/shard_map/ppermute | solution.py:565
  62.5 27.9 %collective-permute-start.28 = (bf16[272,2048]{1,0:T(8,128)(2,1)S(1)}, bf16[272,2048]{1,0:T(8,128)(2,1)S(1)}, u32[]{:S(2)}, u32[]{:S(2)}) collective-permute-start(bf16[272,2048]{1,0:T(8,128)(2,1)S(1)} %tie.6.refs_5_), channel_id=1, source_target_pairs={{0,4},{1,5},{2,6},{3,7},{4,0},{5,1},{6,2},{7,3},{8,12},{9,13},{10,... | collective-permute-start | bytes 3342344 | tf_op jit(solution)/shard_map/ppermute | solution.py:565
  64.2 22.4 %collective-permute-start.17 = (bf16[512,768]{1,0:T(8,128)(2,1)S(1)}, bf16[512,768]{1,0:T(8,128)(2,1)S(1)}, u32[]{:S(2)}, u32[]{:S(2)}) collective-permute-start(bf16[512,768]{1,0:T(8,128)(2,1)S(1)} %get-tuple-element.73.refs_3_), channel_id=1, source_target_pairs={{0,8},{24,16},{1,9},{25,17},{2,10},{26,18},{3,11},{27,19},{4,12},{... | collective-permute-start | bytes 2359304 | tf_op jit(solution)/shard_map/ppermute | solution.py:573
  74.3 29.2 %collective-permute-start.29 = (bf16[512,768]{1,0:T(8,128)(2,1)S(1)}, bf16[512,768]{1,0:T(8,128)(2,1)S(1)}, u32[]{:S(2)}, u32[]{:S(2)}) collective-permute-start(bf16[512,768]{1,0:T(8,128)(2,1)S(1)} %get-tuple-element.89.refs_3_), channel_id=1, source_target_pairs={{0,8},{24,16},{1,9},{25,17},{2,10},{26,18},{3,11},{27,19},{4,12},{... | collective-permute-start | bytes 2359304 | tf_op jit(solution)/shard_map/ppermute | solution.py:573
  92.0 26.0 %collective-permute-start.30 = (bf16[512,768]{1,0:T(8,128)(2,1)S(1)}, bf16[512,768]{1,0:T(8,128)(2,1)S(1)}, u32[]{:S(2)}, u32[]{:S(2)}) collective-permute-start(bf16[512,768]{1,0:T(8,128)(2,1)S(1)} %get-tuple-element.92), channel_id=1, source_target_pairs={{0,8},{24,16},{8,24},{16,0},{1,9},{25,17},{9,25},{17,1},{2,10},{26... | collective-permute-start | bytes 2359304 | tf_op jit(solution)/shard_map/ppermute | solution.py:573
  92.6 12.4 %collective-permute-start.31 = (bf16[144,2048]{1,0:T(8,128)(2,1)S(1)}, bf16[144,2048]{1,0:T(8,128)(2,1)S(1)}, u32[]{:S(2)}, u32[]{:S(2)}) collective-permute-start(bf16[144,2048]{1,0:T(8,128)(2,1)S(1)} %get-tuple-element.93), channel_id=1, source_target_pairs={{0,2},{1,3},{2,0},{3,1},{4,6},{5,7},{6,4},{7,5},{8,10},{9,11},{10,... | collective-permute-start | bytes 1769480 | tf_op jit(solution)/shard_map/ppermute | solution.py:565
  92.9 12.1 %collective-permute-start.32 = (bf16[128,2048]{1,0:T(8,128)(2,1)S(1)}, bf16[128,2048]{1,0:T(8,128)(2,1)S(1)}, u32[]{:S(2)}, u32[]{:S(2)}) collective-permute-start(bf16[128,2048]{1,0:T(8,128)(2,1)S(1)} %get-tuple-element.94), channel_id=1, source_target_pairs={{0,4},{1,5},{2,6},{3,7},{4,0},{5,1},{6,2},{7,3},{8,12},{9,13},{10,... | collective-permute-start | bytes 1572872 | tf_op jit(solution)/shard_map/ppermute | solution.py:565
  122.0 42.7 %collective-permute-start.35 = (bf16[4,272,2048]{2,1,0:T(8,128)(2,1)}, bf16[4,272,2048]{2,1,0:T(8,128)(2,1)}, u32[]{:S(2)}, u32[]{:S(2)}) collective-permute-start(bf16[4,272,2048]{2,1,0:T(8,128)(2,1)} %get-tuple-element.100.refs_2_), channel_id=1, source_target_pairs={{0,1},{1,0},{2,3},{3,2},{4,5},{5,4},{6,7},{7,6},{8,9},{9,8},{10,11... | collective-permute-start | bytes 13369352 | tf_op jit(solution)/shard_map/ppermute | solution.py:565
  122.0 25.3 %collective-permute-start.33 = (bf16[512,768]{1,0:T(8,128)(2,1)}, bf16[512,768]{1,0:T(8,128)(2,1)}, u32[]{:S(2)}, u32[]{:S(2)}) collective-permute-start(bf16[512,768]{1,0:T(8,128)(2,1)} %get-tuple-element.96), channel_id=1, source_target_pairs={{0,8},{24,16},{8,24},{16,0},{1,9},{25,17},{9,25},{17,1},{2,10},{26... | collective-permute-start | bytes 2359304 | tf_op jit(solution)/shard_map/ppermute | solution.py:573
  122.6 36.9 %collective-permute-start.34 = (bf16[512,768]{1,0:T(8,128)(2,1)}, bf16[512,768]{1,0:T(8,128)(2,1)}, u32[]{:S(2)}, u32[]{:S(2)}) collective-permute-start(bf16[512,768]{1,0:T(8,128)(2,1)} %copy-done.32), channel_id=1, source_target_pairs={{0,8},{24,16},{8,24},{16,0},{1,9},{25,17},{9,25},{17,1},{2,10},{26... | collective-permute-start | bytes 2359304 | tf_op jit(solution)/shard_map/ppermute | solution.py:573
  139.3 55.9 %all-to-all-start = ((bf16[8,128,2048]{2,1,0:T(8,128)(2,1)}), bf16[8,128,2048]{2,1,0:T(8,128)(2,1)}, u32[]{:S(2)}, u32[]{:S(2)}) async-start(bf16[8,128,2048]{2,1,0:T(8,128)(2,1)} %copy-done.1), calls=%async_computation | async-start | bytes 8388608 | tf_op jit(solution)/shard_map/all_to_all | solution.py:612
  145.9 30.7 %collective-permute-start.36 = (bf16[512,768]{1,0:T(8,128)(2,1)}, bf16[512,768]{1,0:T(8,128)(2,1)S(1)}, u32[]{:S(2)}, u32[]{:S(2)}) collective-permute-start(bf16[512,768]{1,0:T(8,128)(2,1)} %copy-done.12), channel_id=1, source_target_pairs={{0,8},{24,16},{1,9},{25,17},{2,10},{26,18},{3,11},{27,19},{4,12},{... | collective-permute-start | bytes 2359304 | tf_op jit(solution)/shard_map/ppermute | solution.py:573
  148.7 45.3 %collective-permute-start.39 = (bf16[512,768]{1,0:T(8,128)(2,1)S(1)}, bf16[512,768]{1,0:T(8,128)(2,1)S(1)}, u32[]{:S(2)}, u32[]{:S(2)}) collective-permute-start(bf16[512,768]{1,0:T(8,128)(2,1)S(1)} %get-tuple-element.120), channel_id=1, source_target_pairs={{8,16},{16,8},{9,17},{17,9},{10,18},{18,10},{11,19},{19,11},{12,20... | collective-permute-start | bytes 2359304 | tf_op jit(solution)/shard_map/ppermute | solution.py:573
  161.1 31.7 %collective-permute-start.37 = (bf16[512,768]{1,0:T(8,128)(2,1)S(1)}, bf16[512,768]{1,0:T(8,128)(2,1)S(1)}, u32[]{:S(2)}, u32[]{:S(2)}) collective-permute-start(bf16[512,768]{1,0:T(8,128)(2,1)S(1)} %get-tuple-element.116), channel_id=1, source_target_pairs={{8,16},{16,8},{9,17},{17,9},{10,18},{18,10},{11,19},{19,11},{12,20... | collective-permute-start | bytes 2359304 | tf_op jit(solution)/shard_map/ppermute | solution.py:573
  177.4 32.0 %collective-permute-start.38 = (bf16[512,768]{1,0:T(8,128)(2,1)S(1)}, bf16[512,768]{1,0:T(8,128)(2,1)S(1)}, u32[]{:S(2)}, u32[]{:S(2)}) collective-permute-start(bf16[512,768]{1,0:T(8,128)(2,1)S(1)} %get-tuple-element.118), channel_id=1, source_target_pairs={{8,16},{16,8},{9,17},{17,9},{10,18},{18,10},{11,19},{19,11},{12,20... | collective-permute-start | bytes 2359304 | tf_op jit(solution)/shard_map/ppermute | solution.py:573
  (46 other events, 257.1 us)

commit v4 on v3

--- a/solution.py
+++ b/solution.py
@@ -116,7 +116,7 @@
         out_shape=list(outs) + [shape(8, 128, dtype=F32)],
         scratch_shapes=list(scratch),
         compiler_params=pltpu.CompilerParams(vmem_limit_bytes=limit * 1024 * 1024),
-        cost_estimate=pl.CostEstimate(flops=int(us * 1e9), bytes_accessed=1 << 16, transcendentals=0),
+        cost_estimate=pl.CostEstimate(flops=int(us * 50e7), bytes_accessed=1 << 10, transcendentals=0),
         name=name,
     )(*after, *operands)
 
@@ -319,7 +319,7 @@
         [pos, *groups, rank, prob, h],
         [shape(slots, chunk), shape(chunk, hid)],
         held=[SMEM] + [VMEM] * 11,
-        us=3,
+        us=0.5,
     )
 
 
@@ -356,7 +356,7 @@
         [shape(slots, width)] + [shape(slots, hid)] * 2 + [shape(chunk, hid)],
         after,
         held=[SMEM] + [VMEM] * 17,
-        us=1,
+        us=0.1,
         limit=12,
     )
 
@@ -376,38 +376,43 @@
         [shape(chunk, h.shape[1])] * 7,
         after,
         held=[SMEM] + [VMEM] * 5,
-        us=0.5,
-    )
-
-
-def step_kernel(extra, pos_ref, raw_ref, mine_ref, got_ref, *refs):
-    out_ref = refs[-1 - extra[1]]
+        us=14,
+    )
+
+
+def step_kernel(pos_ref, raw_ref, mine_ref, got_ref, *refs):
+    out_ref = refs[len(refs) // 2]
     total = (mine_ref[...].astype(F32) + got_ref[...].astype(F32)).astype(BF16)
     out_ref[...] = jnp.where(pos_ref[4] == 1, raw_ref[...], total)
-    if extra == (2, 2):
-        bx_ref, by_ref, _, top_ref, bottom_ref = refs
-        half = top_ref.shape[0]
-        top_ref[...] = by_ref[:half]
-        bottom_ref[...] = bx_ref[half:]
-    if extra == (5, 1):
-        half = refs[3].shape[0]
-        for k in range(3):
-            refs[-1][k] = refs[k][...]
-        refs[-1][3, :half] = refs[3][...]
-        refs[-1][3, half:] = refs[4][...]
-
-
-def step(pos, raw, mine, got, after, extra=(), outs=()):
+    if len(refs) > 1:
+        split_kernel(*refs[:2], *refs[3:])
+
+
+def step(pos, raw, mine, got, after, passed=(), half=0):
+    outs = [shape(*mine.shape)]
+    if passed:
+        rows, width = passed[0].shape
+        outs += [shape(half, width), shape(rows - half, width)]
     return run(
         "step",
-        functools.partial(step_kernel, (len(extra), len(outs))),
-        [pos, raw, mine, got, *extra],
-        [shape(*mine.shape), *outs],
-        after,
-        held=[SMEM] + [VMEM] * (3 + len(extra)),
-        us=8,
-        limit=14 if extra else 6,
-    )
+        step_kernel,
+        [pos, raw, mine, got, *passed],
+        outs,
+        after,
+        held=[SMEM] + [VMEM] * (3 + len(passed)),
+        us=16,
+        limit=10 if passed else 6,
+    )
+
+
+def total_kernel(pos_ref, own_ref, far_ref, near_ref, out_ref):
+    got = jnp.where(pos_ref[4] == 1, far_ref[...], near_ref[...])
+    out_ref[...] = (own_ref[...].astype(F32) + got.astype(F32)).astype(BF16)
+
+
+def total(pos, own, far_sum, near_sum, after):
+    held = [SMEM] + [VMEM] * 3
+    return run("total", total_kernel, [pos, own, far_sum, near_sum], [shape(*own.shape)], after, held=held, us=0.5, limit=6)
 
 
 def rows_kernel(capacity, h_ref, dg_ref, du_ref, wd_ref, wg_ref, wu_ref, out_ref):
@@ -429,7 +434,7 @@
         [h, dg, du, w_down, w_gate, w_up],
         [shape(slots // capacity, 2 * capacity, w_gate.shape[0])],
         after,
-        us=7,
+        us=0.1,
     )
 
 
@@ -488,23 +493,22 @@
         scratch=[pltpu.VMEM((parts, slots, width // parts), BF16)]
         + [pltpu.VMEM((parts, count, width // parts), BF16)] * 2
         + [pltpu.SemaphoreType.DMA((parts,)), pltpu.SemaphoreType.DMA((parts, 2))],
-        us=5,
-    )
-
-
-def partner_kernel(capacity, pos_ref, own_ref, core_ref, wg_ref, wu_ref, wd_ref, *refs):
-    x_ref, dy_ref, dg_ref, du_ref, h_ref, rank_ref, prob_ref = refs
+        us=0.5,
+    )
+
+
+def partner_kernel(capacity, pos_ref, *refs):
+    own, bx, by, da, db, c_own, c_bx, c_by, c_da, c_db = refs[:10]
+    wg_ref, wu_ref, wd_ref, x_ref, dy_ref, dg_ref, du_ref, h_ref, rank_ref, prob_ref = refs[10:]
     count = rank_ref.shape[1]
-    groups = [(ref, k) for ref in (own_ref, core_ref) for k in range(4)]
-    route(pos_ref[0], [ref[k, count : count + EXTRA, :count] for ref, k in groups], rank_ref, prob_ref)
-    for n, ref in enumerate((own_ref, core_ref)):
-
-        @pl.loop(0, 4)
-        def _(k):
-            at = pl.ds(pl.multiple_of((4 * n + k) * capacity, capacity), capacity)
-            rank, prob = rank_ref[pl.ds(4 * n + k, 1), :], prob_ref[pl.ds(4 * n + k, 1), :]
-            x_ref[at, :] = slot_rows(ref[k, :count], rank, None, capacity)
-            dy_ref[at, :] = slot_rows(ref[k, count + EXTRA :], rank, prob, capacity)
+    behind = pl.ds(count + EXTRA, count)
+    groups = [(ref, ref.at[behind, :]) for ref in (own, bx, by, c_own, c_bx, c_by)] + [(da, db), (c_da, c_db)]
+    route(pos_ref[0], [rows[count : count + EXTRA, :count] for rows, _ in groups], rank_ref, prob_ref)
+    for n, (rows, grads) in enumerate(groups):
+        at = pl.ds(n * capacity, capacity)
+        rank, prob = rank_ref[n : n + 1], prob_ref[n : n + 1]
+        x_ref[at, :] = slot_rows(rows[:count], rank, None, capacity)
+        dy_ref[at, :] = slot_rows(grads[...], rank, prob, capacity)
 
     def step(cols):
         a, b = activate(cols, x_ref[...], wg_ref, wu_ref, h_ref)
@@ -513,18 +517,19 @@
     tiles(wg_ref.shape[1], step)
 
 
-def partner(pos, own, core, weights, capacity, count, after):
+def partner(pos, groups, weights, capacity, count, after):
     width, hid = weights[0].shape
     slots = 8 * capacity
     return run(
         "partner",
         functools.partial(partner_kernel, capacity),
-        [pos, own, core, *weights],
+        [pos, *groups, *weights],
         [shape(slots, width)] * 2 + [shape(slots, hid)] * 3,
         after,
-        held=[SMEM] + [VMEM] * 5,
+        held=[SMEM] + [VMEM] * 13,
         scratch=[pltpu.VMEM((8, count), F32)] * 2,
-        us=7,
+        us=1,
+        limit=14,
     )
 
 
@@ -542,7 +547,7 @@
         [shape(*m.shape) for m in mine],
         after,
         held=[SMEM] + [VMEM] * 8,
-        us=3,
+        us=0.5,
     )
 
 
@@ -603,35 +608,33 @@
         pos, rest_groups, far_rows, rank, prob, x, a, b, w_down, capacity, [token]
     )
     y2 = along(far_gate, inwards)
-    far_up, near_gate, near_up, near_down, *mine, token = gradients(pos, x, dy, dg, du, h, chunk, [y1])
-    halves = [shape(count + EXTRA, width), shape(count, width)]
-    x3, top, bottom, token = step(pos, far_up, far_down, y1, [token], [raw_x, raw_y], halves)
+    back, token = rows_back(h, dg, du, w_down, w_gate, w_up, capacity, [token])
+    far_up, near_gate, near_up, near_down, *mine, token = gradients(pos, x, dy, dg, du, h, chunk, [token, y1])
+    x3, top, bottom, token = step(pos, far_up, far_down, y1, [token], [raw_x, raw_y], count + EXTRA)
     y3 = along(x3, inwards + across)
     raw_a, raw_b = over(top, 2), over(bottom, 4)
-    back, _ = rows_back(h, dg, du, w_down, w_gate, w_up, capacity)
-    back = lax.all_to_all(back, "expert", split_axis=0, concat_axis=0, tiled=True)
-    x4, token = step(pos, near_down, far_gate, y2, [token])
+    raw_groups = doubled(raw, raw_x, raw_y, raw_a, raw_b)
+    back = lax.all_to_all(tie(back, [token]), "expert", split_axis=0, concat_axis=0, tiled=True)
+    x4, token = step(pos, near_down, far_gate, y2, [token, raw_a, raw_b])
     y4 = along(x4, inwards + across)
-    blocks = [raw, raw_x, raw_y, raw_a, raw_b]
-    x5, raw_own, token = step(pos, near_gate, far_up, y3, [token], blocks, [shape(4, *raw.shape)])
+    x5, token = step(pos, near_gate, far_up, y3, [token])
     y5 = along(x5, inwards + across)
     near_up = tie(near_up, [token])
     y6 = along(near_up, inwards)
-    raw_core = over(raw_own, 1)
     x6, token = step(pos, near_down, near_down, y4, [token])
     z_down = along(x6, middle)
-    x7, token = step(pos, near_gate, near_gate, y5, [token])
-    z_gate = along(x7, middle)
-    *slots, token = partner(pos, raw_own, raw_core, (w_gate, w_up, w_down), capacity, count, [token])
-    x8, token = step(pos, near_up, near_up, y6, [token])
-    z_up = along(x8, middle)
-    *mine, _ = both(pos, slots, mine, [token])
-    mixed, tokens_grad, _ = combine(meta, back.reshape(2 * peers * capacity, width), capacity, [token])
-
-    grads = []
-    for own, far_sum, near_sum in zip(mine, (y4, y5, y3), (z_gate, z_up, z_down)):
-        total = own.astype(F32) + jnp.where(outer == 1, far_sum, near_sum).astype(F32)
-        grads.append(total.astype(BF16)[None])
+    x7, token = step(pos, near_up, near_up, y6, [token, z_down])
+    z_up = along(x7, middle)
+    *slots, token = partner(pos, raw_groups, (w_gate, w_up, w_down), capacity, count, [token])
+    x8, token = step(pos, near_gate, near_gate, y5, [token])
+    z_gate = along(x8, middle)
+    *mine, token = both(pos, slots, mine, [token])
+    mixed, tokens_grad, token = combine(meta, back.reshape(2 * peers * capacity, width), capacity, [token])
+
+    down, token = total(pos, mine[2], y3, z_down, [token])
+    up, token = total(pos, mine[1], y5, z_up, [token])
+    gate, _ = total(pos, mine[0], y4, z_gate, [token])
+    grads = [g[None] for g in (gate, up, down)]
     return (mixed, tokens_grad, *grads)
 
 

time: 212 us -> 199 us (0.939)
  waiting for transfers between devices: 93.1 us -> 84.1 us
  local copies, waits for them, and re-layouts: 20.3 us -> 14.5 us
  other arithmetic: 3.62 us -> 0 us
  Pallas kernels: 51.4 us -> 54.6 us
  starting transfers between devices: 41 us -> 44.2 us
    ppermute x9, waiting for transfers between devices: 61.8 us -> 39.2 us  [along(): return lax.ppermute(x, 'dp', pairs)]
    ppermute x30 -> x34, waiting for transfers between devices: 30.2 us -> 44.6 us  [over(): return lax.ppermute(x, 'expert', [(i, i ^ bit) for i in range(peers)])]
    ppermute x9, starting transfers between devices: 16.3 us -> 22.2 us  [along(): return lax.ppermute(x, 'dp', pairs)]
    unnamed x74 -> x80, local copies, waits for them, and re-layouts: 20.2 us -> 14.4 us
    broadcast_in_dim x3 -> x0, other arithmetic: 3.62 us -> none  [local_pairs(): grads.append(total.astype(BF16)[None])]
    pallas_call x18 -> x21, Pallas kernels: 51.4 us -> 54.6 us  [run(): pl.pallas_call(body, in_specs=[ANY] * skip + list(held or [VMEM] * len(op...]
    ppermute x30 -> x34, starting transfers between devices: 19.7 us -> 17 us  [over(): return lax.ppermute(x, 'expert', [(i, i ^ bit) for i in range(peers)])]
  transfers between devices with their start and end apart: 41 -> 45, of which waited for: 21 -> 23; matrix products, arithmetic and copies ran while one was open for 1% -> 0% of each run, Pallas kernels for 22% -> 26%
where the time goes in v4:
time: 199 us
  waiting for transfers between devices  84.1 us (42%)
  Pallas kernels  54.6 us (27%)
  starting transfers between devices  44.2 us (22%)
  local copies, waits for them, and re-layouts  14.5 us (7%)
    pallas_call x21, Pallas kernels, run(): pl.pallas_call(body, in_specs=[ANY] * skip + list(held or [VMEM] * len(op...  54.6 us
    ppermute x34, waiting for transfers between devices, over(): return lax.ppermute(x, 'expert', [(i, i ^ bit) for i in range(peers)])  44.6 us
    ppermute x9, waiting for transfers between devices, along(): return lax.ppermute(x, 'dp', pairs)  39.2 us
    ppermute x9, starting transfers between devices, along(): return lax.ppermute(x, 'dp', pairs)  22.2 us
    ppermute x34, starting transfers between devices, over(): return lax.ppermute(x, 'expert', [(i, i ^ bit) for i in range(peers)])  17 us
    unnamed x80, local copies, waits for them, and re-layouts  14.4 us
    all_to_all x1, starting transfers between devices, local_pairs(): lax.all_to_all(tie(back, [token]), 'expert', split_axis=0, concat_axis=0,...  4.54 us
  transfers between devices with their start and end apart: 45, of which 23 were waited for; matrix products, arithmetic and copies ran while one was open for 0% of the time, Pallas kernels for 26%

profile of v4, /device:TPU:8, one launch (start us, length us, event | category | flops | bytes accessed | tf_op | source)
XLA Modules:
  0.0 198.5 jit_solution(18283072977554533239)
XLA Ops:
  9.2 1.9 copy-done
  11.1 1.9 copy-done.2
  14.9 5.9 %collective-permute-done.1.refs_2_.refs_3_ = bf16[144,2048]{1,0:T(8,128)(2,1)S(1)} collective-permute-done((bf16[144,2048]{1,0:T(8,128)(2,1)S(1)}, bf16[144,2048]{1,0:T(8,128)(2,1)S(1)}, u32[]{:S(2)}, u32[]{:S(2)}) %collective-permute-start.1) | collective-permute-done | bytes 589856 | tf_op jit(solution)/shard_map/ppermute | solution.py:570
  24.9 4.7 %collective-permute-done.2.refs_1_.refs_4_ = bf16[64,2048]{1,0:T(8,128)(2,1)S(1)} collective-permute-done((bf16[64,2048]{1,0:T(8,128)(2,1)S(1)}, bf16[64,2048]{1,0:T(8,128)(2,1)S(1)}, u32[]{:S(2)}, u32[]{:S(2)}) %collective-permute-start.2) | collective-permute-done | bytes 262176 | tf_op jit(solution)/shard_map/ppermute | solution.py:570
  29.6 4.7 %collective-permute-done.3.refs_2_.refs_5_ = bf16[80,2048]{1,0:T(8,128)(2,1)S(1)} collective-permute-done((bf16[80,2048]{1,0:T(8,128)(2,1)S(1)}, bf16[80,2048]{1,0:T(8,128)(2,1)S(1)}, u32[]{:S(2)}, u32[]{:S(2)}) %collective-permute-start.3) | collective-permute-done | bytes 327712 | tf_op jit(solution)/shard_map/ppermute | solution.py:570
  39.0 3.1 %collective-permute-done.10.refs_7_ = bf16[128,512]{1,0:T(8,128)(2,1)S(1)} collective-permute-done((bf16[128,512]{1,0:T(8,128)(2,1)S(1)}, bf16[128,512]{1,0:T(8,128)(2,1)S(1)}, u32[]{:S(2)}, u32[]{:S(2)}) %collective-permute-start.10) | collective-permute-done | bytes 131104 | tf_op jit(solution)/shard_map/ppermute | solution.py:570
  44.9 5.5 %forward.1 = (bf16[512,2048]{1,0:T(8,128)(2,1)S(1)}, f32[8,128]{1,0:T(8,128)S(1)}, f32[8,128]{1,0:T(8,128)S(1)}, bf16[512,768]{1,0:T(8,128)(2,1)S(1)}, f32[512,7...) custom-call(s32[5]{0:T(128)S(1)} %get-tuple-element.71.refs_0_.refs_1_.refs_2_.refs_3_, ...), custom_call_target="tpu_custom_call" | custom-call | flops 3000000000 | bytes 1024 | tf_op jit(solution)/shard_map/forward/pallas_call | solution.py:112
  55.8 4.4 %collective-permute-done.19.refs_5_.refs_1_ = bf16[64,1536]{1,0:T(8,128)(2,1)S(1)} collective-permute-done((bf16[64,1536]{1,0:T(8,128)(2,1)S(1)}, bf16[64,1536]{1,0:T(8,128)(2,1)S(1)}, u32[]{:S(2)}, u32[]{:S(2)}) %collective-permute-start.19) | collective-permute-done | bytes 196640 | tf_op jit(solution)/shard_map/ppermute | solution.py:570
  65.8 4.7 %backward.1 = (bf16[512,2048]{1,0:T(8,128)(2,1)S(1)}, bf16[512,768]{1,0:T(8,128)(2,1)S(1)}, bf16[512,768]{1,0:T(8,128)(2,1)S(1)}, bf16[512,768]{1,0:T(8,128)(2,1)S(1)}, f32[8,128]{1,0:T(8,128)S(1)}) custom-call(f32[8,128]{1,0:T(8,128)S(1)} %get-tuple-element.81.refs_0_, s32[5]{0:T(128)S(1)} %get-tuple-element.71.refs_0_.refs_1_.refs_2_.refs_3_, ...), custom_call_target="tpu_custom_call" | custom-call | flops 50000000 | bytes 1024 | tf_op jit(solution)/shard_map/backward/pallas_call | solution.py:112
  72.0 5.1 %rows_back.1 = (bf16[8,128,2048]{2,1,0:T(8,128)(2,1)S(1)}, f32[8,128]{1,0:T(8,128)S(1)}) custom-call(f32[8,128]{1,0:T(8,128)S(1)} %get-tuple-element.89.refs_0_, bf16[512,768]{1,0:T(8,128)(2,1)S(1)} %get-tuple-element.80.refs_11_.refs_1_.refs_7_, bf16[512,768]{1,0:T(8,128)(2,1)S(1)} %get-tuple-element.90.refs_2_.refs_5_, ...), custom_call_target="tpu_custom_call" | custom-call | flops 50000000 | bytes 1024 | tf_op jit(solution)/shard_map/rows_back/pallas_call | solution.py:112
  77.1 3.7 %gradients.1 = (bf16[512,768]{1,0:T(8,128)(2,1)S(1)}, bf16[512,768]{1,0:T(8,128)(2,1)S(1)}, bf16[512,768]{1,0:T(8,128)(2,1)S(1)}, bf16[512,768]{1,0:T(8,128)(2,1...) custom-call(f32[8,128]{1,0:T(8,128)S(1)} %get-tuple-element.92.refs_, ...), custom_call_target="tpu_custom_call" | custom-call | flops 7000000000 | bytes 1024 | tf_op jit(solution)/shard_map/gradients/pallas_call | solution.py:112
  81.7 5.8 %collective-permute-done.28.refs_6_.refs_4_ = bf16[272,2048]{1,0:T(8,128)(2,1)S(1)} collective-permute-done((bf16[272,2048]{1,0:T(8,128)(2,1)}, bf16[272,2048]{1,0:T(8,128)(2,1)S(1)}, u32[]{:S(2)}, u32[]{:S(2)}) %collective-permute-start.28) | collective-permute-done | bytes 1114144 | tf_op jit(solution)/shard_map/ppermute | solution.py:570
  92.3 3.1 %collective-permute-start.32 = (bf16[512,768]{1,0:T(8,128)(2,1)}, bf16[512,768]{1,0:T(8,128)(2,1)}, u32[]{:S(2)}, u32[]{:S(2)}) collective-permute-start(bf16[512,768]{1,0:T(8,128)(2,1)} %get-tuple-element.104), channel_id=1, source_target_pairs={{0,8},{24,16},{8,24},{16,0},{1,9},{25,17},{9,25},{17,1},{2,10},{26... | collective-permute-start | bytes 2359304 | tf_op jit(solution)/shard_map/ppermute | solution.py:578
  95.4 7.4 %collective-permute-done.30.refs_2_.refs_6_ = bf16[128,2048]{1,0:T(8,128)(2,1)S(1)} collective-permute-done((bf16[128,2048]{1,0:T(8,128)(2,1)S(1)}, bf16[128,2048]{1,0:T(8,128)(2,1)S(1)}, u32[]{:S(2)}, u32[]{:S(2)}) %collective-permute-start.30) | collective-permute-done | bytes 524320 | tf_op jit(solution)/shard_map/ppermute | solution.py:570
  105.1 2.8 %collective-permute-start.33 = (bf16[512,768]{1,0:T(8,128)(2,1)}, bf16[512,768]{1,0:T(8,128)(2,1)}, u32[]{:S(2)}, u32[]{:S(2)}) collective-permute-start(bf16[512,768]{1,0:T(8,128)(2,1)} %get-tuple-element.106), channel_id=1, source_target_pairs={{0,8},{24,16},{8,24},{16,0},{1,9},{25,17},{9,25},{17,1},{2,10},{26... | collective-permute-start | bytes 2359304 | tf_op jit(solution)/shard_map/ppermute | solution.py:578
  107.8 2.0 %copy-done.8 = bf16[8,128,2048]{2,1,0:T(8,128)(2,1)} copy-done((bf16[8,128,2048]{2,1,0:T(8,128)(2,1)}, bf16[8,128,2048]{2,1,0:T(8,128)(2,1)S(1)}, u32[]{:S(2)}) %copy-start.8) | copy-done | bytes 4194328
  109.8 4.5 %all-to-all-start = ((bf16[8,128,2048]{2,1,0:T(8,128)(2,1)}), bf16[8,128,2048]{2,1,0:T(8,128)(2,1)}, u32[]{:S(2)}, u32[]{:S(2)}) async-start(bf16[8,128,2048]{2,1,0:T(8,128)(2,1)} %copy-done.8), calls=%async_computation | async-start | bytes 8388608 | tf_op jit(solution)/shard_map/all_to_all | solution.py:617
  119.8 8.7 %collective-permute-done.33.refs_4_.refs_3_ = bf16[512,768]{1,0:T(8,128)(2,1)} collective-permute-done((bf16[512,768]{1,0:T(8,128)(2,1)}, bf16[512,768]{1,0:T(8,128)(2,1)}, u32[]{:S(2)}, u32[]{:S(2)}) %collective-permute-start.33) | collective-permute-done | bytes 786464 | tf_op jit(solution)/shard_map/ppermute | solution.py:578
  129.9 4.6 %collective-permute-start.34 = (bf16[512,768]{1,0:T(8,128)(2,1)S(1)}, bf16[512,768]{1,0:T(8,128)(2,1)S(1)}, u32[]{:S(2)}, u32[]{:S(2)}) collective-permute-start(bf16[512,768]{1,0:T(8,128)(2,1)S(1)} %get-tuple-element.108), channel_id=1, source_target_pairs={{8,16},{16,8},{9,17},{17,9},{10,18},{18,10},{11,19},{19,11},{12,20... | collective-permute-start | bytes 2359304 | tf_op jit(solution)/shard_map/ppermute | solution.py:578
  135.2 7.7 %collective-permute-done.35.refs_5_ = bf16[512,768]{1,0:T(8,128)(2,1)S(1)} collective-permute-done((bf16[512,768]{1,0:T(8,128)(2,1)S(1)}, bf16[512,768]{1,0:T(8,128)(2,1)S(1)}, u32[]{:S(2)}, u32[]{:S(2)}) %collective-permute-start.35) | collective-permute-done | bytes 786464 | tf_op jit(solution)/shard_map/ppermute | solution.py:578
  142.8 2.1 %collective-permute-done.34.refs_1_.refs_4_ = bf16[512,768]{1,0:T(8,128)(2,1)S(1)} collective-permute-done((bf16[512,768]{1,0:T(8,128)(2,1)S(1)}, bf16[512,768]{1,0:T(8,128)(2,1)S(1)}, u32[]{:S(2)}, u32[]{:S(2)}) %collective-permute-start.34) | collective-permute-done | bytes 786464 | tf_op jit(solution)/shard_map/ppermute | solution.py:578
  146.6 3.7 %collective-permute-start.42 = (bf16[512,768]{1,0:T(8,128)(2,1)}, bf16[512,768]{1,0:T(8,128)(2,1)}, u32[]{:S(2)}, u32[]{:S(2)}) collective-permute-start(bf16[512,768]{1,0:T(8,128)(2,1)} %get-tuple-element.130), channel_id=1, source_target_pairs={{8,16},{16,8},{9,17},{17,9},{10,18},{18,10},{11,19},{19,11},{12,20... | collective-permute-start | bytes 2359304 | tf_op jit(solution)/shard_map/ppermute | solution.py:578
  150.4 8.7 %partner.1 = (bf16[512,2048]{1,0:T(8,128)(2,1)S(1)}, bf16[512,2048]{1,0:T(8,128)(2,1)S(1)}, bf16[512,768]{1,0:T(8,128)(2,1)S(1)}, bf16[512,768]{1,0:T(8,128)(2,1...) custom-call(f32[8,128]{1,0:T(8,128)S(1)} %get-tuple-element.110.refs_0_, ...), custom_call_target="tpu_custom_call" | custom-call | flops 500000000 | bytes 1024 | tf_op jit(solution)/shard_map/partner/pallas_call | solution.py:112
  159.1 3.9 %collective-permute-done.41.refs_4_.refs_3_ = bf16[512,768]{1,0:T(8,128)(2,1)S(1)} collective-permute-done((bf16[512,768]{1,0:T(8,128)(2,1)S(1)}, bf16[512,768]{1,0:T(8,128)(2,1)S(1)}, u32[]{:S(2)}, u32[]{:S(2)}) %collective-permute-start.41) | collective-permute-done | bytes 786464 | tf_op jit(solution)/shard_map/ppermute | solution.py:578
  164.6 3.7 %collective-permute-start.43 = (bf16[512,768]{1,0:T(8,128)(2,1)}, bf16[512,768]{1,0:T(8,128)(2,1)S(1)}, u32[]{:S(2)}, u32[]{:S(2)}) collective-permute-start(bf16[512,768]{1,0:T(8,128)(2,1)} %get-tuple-element.133), channel_id=1, source_target_pairs={{8,16},{16,8},{9,17},{17,9},{10,18},{18,10},{11,19},{19,11},{12,20... | collective-permute-start | bytes 2359304 | tf_op jit(solution)/shard_map/ppermute | solution.py:578
  168.4 2.0 %both.1 = (bf16[512,768]{1,0:T(8,128)(2,1)S(1)}, bf16[512,768]{1,0:T(8,128)(2,1)S(1)}, bf16[512,768]{1,0:T(8,128)(2,1)S(1)}, f32[8,128]{1,0:T(8,128)S(1)}) custom-call(f32[8,128]{1,0:T(8,128)S(1)} %get-tuple-element.113.refs_0_, s32[5]{0:T(128)S(1)} %get-tuple-element.71.refs_0_.refs_1_.refs_2_.refs_3_, bf16[512,2048]{1,0:T(8,128)(2,1)S(1)} %get-tuple-element.114.refs_2_, ...), custom_call_target="tpu_custom_call" | custom-call | flops 250000000 | bytes 1024 | tf_op jit(solution)/shard_map/both/pallas_call | solution.py:112
  170.4 4.4 %combine.1 = (bf16[128,2048]{1,0:T(8,128)(2,1)}, bf16[128,2048]{1,0:T(8,128)(2,1)}, f32[8,128]{1,0:T(8,128)S(1)}) custom-call(f32[8,128]{1,0:T(8,128)S(1)} %get-tuple-element.122.refs_0_, bf16[16,128]{1,0:T(8,128)(2,1)S(1)} %get-tuple-element.73.refs_0_.refs_1_, bf16[1024,2048]{1,0:T(8,128)(2,1)} %bitcast.10.refs_2_), custom_call_target="tpu_custom_call" | custom-call | flops 250000000 | bytes 1024 | tf_op jit(solution)/shard_map/combine/pallas_call | solution.py:112
  174.9 2.3 %total.3 = (bf16[512,768]{1,0:T(8,128)(2,1)}, f32[8,128]{1,0:T(8,128)S(1)}) custom-call(f32[8,128]{1,0:T(8,128)S(1)} %get-tuple-element.126.refs_0_, s32[5]{0:T(128)S(1)} %get-tuple-element.71.refs_0_.refs_1_.refs_2_.refs_3_, bf16[512,768]{1,0:T(8,128)(2,1)S(1)} %get-tuple-element.127.refs_2_, bf16[512,768]{1,0:T(8,128)(2,1)} %collective-permute-done.32.refs_4_.refs_3_, ...), custom_call_target="tpu_custom_call" | custom-call | flops 250000000 | bytes 1024 | tf_op jit(solution)/shard_map/total/pallas_call | solution.py:112
  177.2 4.7 %collective-permute-done.42.refs_4_ = bf16[512,768]{1,0:T(8,128)(2,1)} collective-permute-done((bf16[512,768]{1,0:T(8,128)(2,1)}, bf16[512,768]{1,0:T(8,128)(2,1)}, u32[]{:S(2)}, u32[]{:S(2)}) %collective-permute-start.42) | collective-permute-done | bytes 786464 | tf_op jit(solution)/shard_map/ppermute | solution.py:578
  181.9 2.3 %total.4 = (bf16[512,768]{1,0:T(8,128)(2,1)}, f32[8,128]{1,0:T(8,128)S(1)}) custom-call(f32[8,128]{1,0:T(8,128)S(1)} %get-tuple-element.128.refs_0_, s32[5]{0:T(128)S(1)} %get-tuple-element.71.refs_0_.refs_1_.refs_2_.refs_3_, bf16[512,768]{1,0:T(8,128)(2,1)S(1)} %get-tuple-element.129.refs_2_, bf16[512,768]{1,0:T(8,128)(2,1)S(1)} %copy-done.24, ...), custom_call_target="tpu_custom_call" | custom-call | flops 250000000 | bytes 1024 | tf_op jit(solution)/shard_map/total/pallas_call | solution.py:112
  184.2 12.1 %collective-permute-done.43.refs_4_ = bf16[512,768]{1,0:T(8,128)(2,1)S(1)} collective-permute-done((bf16[512,768]{1,0:T(8,128)(2,1)}, bf16[512,768]{1,0:T(8,128)(2,1)S(1)}, u32[]{:S(2)}, u32[]{:S(2)}) %collective-permute-start.43) | collective-permute-done | bytes 786464 | tf_op jit(solution)/shard_map/ppermute | solution.py:578
  196.3 2.2 %total.5 = (bf16[512,768]{1,0:T(8,128)(2,1)}, f32[8,128]{1,0:T(8,128)}) custom-call(f32[8,128]{1,0:T(8,128)S(1)} %get-tuple-element.131.refs_0_, s32[5]{0:T(128)S(1)} %get-tuple-element.71.refs_0_.refs_1_.refs_2_.refs_3_, bf16[512,768]{1,0:T(8,128)(2,1)S(1)} %get-tuple-element.132.refs_2_, bf16[512,768]{1,0:T(8,128)(2,1)} %collective-permute-done.33.refs_4_.refs_3_, ...), custom_call_target="tpu_custom_call" | custom-call | flops 250000000 | bytes 1024 | tf_op jit(solution)/shard_map/total/pallas_call | solution.py:112
  (165 shorter events, 53.0 us)
Async XLA Ops:
  5.7 15.1 %collective-permute-start.1 = (bf16[144,2048]{1,0:T(8,128)(2,1)S(1)}, bf16[144,2048]{1,0:T(8,128)(2,1)S(1)}, u32[]{:S(2)}, u32[]{:S(2)}) collective-permute-start(bf16[144,2048]{1,0:T(8,128)(2,1)S(1)} %get-tuple-element.74.refs_1_), channel_id=1, source_target_pairs={{0,4},{1,5},{2,6},{3,7},{4,0},{5,1},{6,2},{7,3},{8,12},{9,13},{10,... | collective-permute-start | bytes 1769480 | tf_op jit(solution)/shard_map/ppermute | solution.py:570
  7.3 14.8 %collective-permute-start = (bf16[144,2048]{1,0:T(8,128)(2,1)S(1)}, bf16[144,2048]{1,0:T(8,128)(2,1)S(1)}, u32[]{:S(2)}, u32[]{:S(2)}) collective-permute-start(bf16[144,2048]{1,0:T(8,128)(2,1)S(1)} %get-tuple-element.74.refs_1_), channel_id=1, source_target_pairs={{0,2},{1,3},{2,0},{3,1},{4,6},{5,7},{6,4},{7,5},{8,10},{9,11},{10,... | collective-permute-start | bytes 1769480 | tf_op jit(solution)/shard_map/ppermute | solution.py:570
  8.8 25.8 %collective-permute-start.4 = (bf16[272,2048]{1,0:T(8,128)(2,1)S(1)}, bf16[272,2048]{1,0:T(8,128)(2,1)}, u32[]{:S(2)}, u32[]{:S(2)}) collective-permute-start(bf16[272,2048]{1,0:T(8,128)(2,1)S(1)} %get-tuple-element.77), channel_id=1, source_target_pairs={{0,8},{8,0},{16,24},{24,16},{1,9},{9,1},{17,25},{25,17},{2,10},{10... | collective-permute-start | bytes 3342344 | tf_op jit(solution)/shard_map/ppermute | solution.py:573
  24.2 10.6 %collective-permute-start.12 = (bf16[144,2048]{1,0:T(8,128)(2,1)S(1)}, bf16[144,2048]{1,0:T(8,128)(2,1)S(1)}, u32[]{:S(2)}, u32[]{:S(2)}) collective-permute-start(bf16[144,2048]{1,0:T(8,128)(2,1)S(1)} %get-tuple-element.74.refs_1_), channel_id=1, source_target_pairs={{0,1},{1,0},{2,3},{3,2},{4,5},{5,4},{6,7},{7,6},{8,9},{9,8},{10,11... | collective-permute-start | bytes 1769480 | tf_op jit(solution)/shard_map/ppermute | solution.py:570
  24.2 10.1 %collective-permute-start.3 = (bf16[80,2048]{1,0:T(8,128)(2,1)S(1)}, bf16[80,2048]{1,0:T(8,128)(2,1)S(1)}, u32[]{:S(2)}, u32[]{:S(2)}) collective-permute-start(bf16[80,2048]{1,0:T(8,128)(2,1)S(1)} %get-tuple-element.76), channel_id=1, source_target_pairs={{0,4},{1,5},{2,6},{3,7},{4,0},{5,1},{6,2},{7,3},{8,12},{9,13},{10,... | collective-permute-start | bytes 983048 | tf_op jit(solution)/shard_map/ppermute | solution.py:570
  24.7 12.1 %collective-permute-start.14 = (bf16[144,2048]{1,0:T(8,128)(2,1)S(1)}, bf16[144,2048]{1,0:T(8,128)(2,1)S(1)}, u32[]{:S(2)}, u32[]{:S(2)}) collective-permute-start(bf16[144,2048]{1,0:T(8,128)(2,1)S(1)} %collective-permute-done.1.refs_2_.refs_3_), channel_id=1, source_target_pairs={{0,1},{1,0},{2,3},{3,2},{4,5},{5,4},{6,7},{7,6},{8,9},{9,8},{10,11... | collective-permute-start | bytes 1769480 | tf_op jit(solution)/shard_map/ppermute | solution.py:570
  29.6 8.7 %collective-permute-start.13 = (bf16[144,2048]{1,0:T(8,128)(2,1)S(1)}, bf16[144,2048]{1,0:T(8,128)(2,1)S(1)}, u32[]{:S(2)}, u32[]{:S(2)}) collective-permute-start(bf16[144,2048]{1,0:T(8,128)(2,1)S(1)} %collective-permute-done.refs_1_.refs_2_), channel_id=1, source_target_pairs={{0,1},{1,0},{2,3},{3,2},{4,5},{5,4},{6,7},{7,6},{8,9},{9,8},{10,11... | collective-permute-start | bytes 1769480 | tf_op jit(solution)/shard_map/ppermute | solution.py:570
  36.3 8.0 %collective-permute-start.8 = (bf16[128,512]{1,0:T(8,128)(2,1)S(1)}, bf16[128,512]{1,0:T(8,128)(2,1)S(1)}, u32[]{:S(2)}, u32[]{:S(2)}) collective-permute-start(bf16[128,512]{1,0:T(8,128)(2,1)S(1)} %tie.5.refs_1_), channel_id=1, source_target_pairs={{0,4},{1,5},{2,6},{3,7},{4,0},{5,1},{6,2},{7,3},{8,12},{9,13},{10,... | collective-permute-start | bytes 393224 | tf_op jit(solution)/shard_map/ppermute | solution.py:570
  36.8 7.5 %collective-permute-start.6 = (bf16[128,512]{1,0:T(8,128)(2,1)S(1)}, bf16[128,512]{1,0:T(8,128)(2,1)S(1)}, u32[]{:S(2)}, u32[]{:S(2)}) collective-permute-start(bf16[128,512]{1,0:T(8,128)(2,1)S(1)} %tie.5.refs_1_), channel_id=1, source_target_pairs={{0,2},{1,3},{2,0},{3,1},{4,6},{5,7},{6,4},{7,5},{8,10},{9,11},{10,... | collective-permute-start | bytes 393224 | tf_op jit(solution)/shard_map/ppermute | solution.py:570
  38.3 14.3 %collective-permute-start.18 = (bf16[128,1536]{1,0:T(8,128)(2,1)S(1)}, bf16[128,1536]{1,0:T(8,128)(2,1)S(1)}, u32[]{:S(2)}, u32[]{:S(2)}) collective-permute-start(bf16[128,1536]{1,0:T(8,128)(2,1)S(1)} %tie.6.refs_2_), channel_id=1, source_target_pairs={{0,4},{1,5},{2,6},{3,7},{4,0},{5,1},{6,2},{7,3},{8,12},{9,13},{10,... | collective-permute-start | bytes 1179656 | tf_op jit(solution)/shard_map/ppermute | solution.py:570
  42.1 10.6 %collective-permute-start.17 = (bf16[128,1536]{1,0:T(8,128)(2,1)S(1)}, bf16[128,1536]{1,0:T(8,128)(2,1)S(1)}, u32[]{:S(2)}, u32[]{:S(2)}) collective-permute-start(bf16[128,1536]{1,0:T(8,128)(2,1)S(1)} %tie.6.refs_2_), channel_id=1, source_target_pairs={{0,2},{1,3},{2,0},{3,1},{4,6},{5,7},{6,4},{7,5},{8,10},{9,11},{10,... | collective-permute-start | bytes 1179656 | tf_op jit(solution)/shard_map/ppermute | solution.py:570
  50.4 12.2 %collective-permute-start.21 = (bf16[128,1536]{1,0:T(8,128)(2,1)S(1)}, bf16[128,1536]{1,0:T(8,128)(2,1)S(1)}, u32[]{:S(2)}, u32[]{:S(2)}) collective-permute-start(bf16[128,1536]{1,0:T(8,128)(2,1)S(1)} %tie.6.refs_2_), channel_id=1, source_target_pairs={{0,1},{1,0},{2,3},{3,2},{4,5},{5,4},{6,7},{7,6},{8,9},{9,8},{10,11... | collective-permute-start | bytes 1179656 | tf_op jit(solution)/shard_map/ppermute | solution.py:570
  53.8 23.3 %collective-permute-start.26 = (bf16[512,768]{1,0:T(8,128)(2,1)S(1)}, bf16[512,768]{1,0:T(8,128)(2,1)S(1)}, u32[]{:S(2)}, u32[]{:S(2)}) collective-permute-start(bf16[512,768]{1,0:T(8,128)(2,1)S(1)} %get-tuple-element.93.refs_3_), channel_id=1, source_target_pairs={{0,8},{24,16},{1,9},{25,17},{2,10},{26,18},{3,11},{27,19},{4,12},{... | collective-permute-start | bytes 2359304 | tf_op jit(solution)/shard_map/ppermute | solution.py:578
  55.8 8.3 %collective-permute-start.23 = (bf16[128,1536]{1,0:T(8,128)(2,1)S(1)}, bf16[128,1536]{1,0:T(8,128)(2,1)S(1)}, u32[]{:S(2)}, u32[]{:S(2)}) collective-permute-start(bf16[128,1536]{1,0:T(8,128)(2,1)S(1)} %collective-permute-done.18.refs_2_.refs_4_), channel_id=1, source_target_pairs={{0,1},{1,0},{2,3},{3,2},{4,5},{5,4},{6,7},{7,6},{8,9},{9,8},{10,11... | collective-permute-start | bytes 1179656 | tf_op jit(solution)/shard_map/ppermute | solution.py:570
  61.9 25.7 %collective-permute-start.28 = (bf16[272,2048]{1,0:T(8,128)(2,1)}, bf16[272,2048]{1,0:T(8,128)(2,1)S(1)}, u32[]{:S(2)}, u32[]{:S(2)}) collective-permute-start(bf16[272,2048]{1,0:T(8,128)(2,1)} %tie.7.refs_2_), channel_id=1, source_target_pairs={{0,4},{1,5},{2,6},{3,7},{4,0},{5,1},{6,2},{7,3},{8,12},{9,13},{10,... | collective-permute-start | bytes 3342344 | tf_op jit(solution)/shard_map/ppermute | solution.py:570
  62.7 25.6 %collective-permute-start.27 = (bf16[272,2048]{1,0:T(8,128)(2,1)}, bf16[272,2048]{1,0:T(8,128)(2,1)S(1)}, u32[]{:S(2)}, u32[]{:S(2)}) collective-permute-start(bf16[272,2048]{1,0:T(8,128)(2,1)} %tie.7.refs_2_), channel_id=1, source_target_pairs={{0,2},{1,3},{2,0},{3,1},{4,6},{5,7},{6,4},{7,5},{8,10},{9,11},{10,... | collective-permute-start | bytes 3342344 | tf_op jit(solution)/shard_map/ppermute | solution.py:570
  70.5 24.9 %collective-permute-start.31 = (bf16[512,768]{1,0:T(8,128)(2,1)S(1)}, bf16[512,768]{1,0:T(8,128)(2,1)S(1)}, u32[]{:S(2)}, u32[]{:S(2)}) collective-permute-start(bf16[512,768]{1,0:T(8,128)(2,1)S(1)} %get-tuple-element.101.refs_5_), channel_id=1, source_target_pairs={{0,8},{24,16},{1,9},{25,17},{2,10},{26,18},{3,11},{27,19},{4,12},{... | collective-permute-start | bytes 2359304 | tf_op jit(solution)/shard_map/ppermute | solution.py:578
  90.0 13.3 %collective-permute-start.29 = (bf16[144,2048]{1,0:T(8,128)(2,1)S(1)}, bf16[144,2048]{1,0:T(8,128)(2,1)S(1)}, u32[]{:S(2)}, u32[]{:S(2)}) collective-permute-start(bf16[144,2048]{1,0:T(8,128)(2,1)S(1)} %get-tuple-element.98), channel_id=1, source_target_pairs={{0,2},{1,3},{2,0},{3,1},{4,6},{5,7},{6,4},{7,5},{8,10},{9,11},{10,... | collective-permute-start | bytes 1769480 | tf_op jit(solution)/shard_map/ppermute | solution.py:570
  91.3 11.5 %collective-permute-start.30 = (bf16[128,2048]{1,0:T(8,128)(2,1)S(1)}, bf16[128,2048]{1,0:T(8,128)(2,1)S(1)}, u32[]{:S(2)}, u32[]{:S(2)}) collective-permute-start(bf16[128,2048]{1,0:T(8,128)(2,1)S(1)} %get-tuple-element.99), channel_id=1, source_target_pairs={{0,4},{1,5},{2,6},{3,7},{4,0},{5,1},{6,2},{7,3},{8,12},{9,13},{10,... | collective-permute-start | bytes 1572872 | tf_op jit(solution)/shard_map/ppermute | solution.py:570
  92.3 22.1 %collective-permute-start.32 = (bf16[512,768]{1,0:T(8,128)(2,1)}, bf16[512,768]{1,0:T(8,128)(2,1)}, u32[]{:S(2)}, u32[]{:S(2)}) collective-permute-start(bf16[512,768]{1,0:T(8,128)(2,1)} %get-tuple-element.104), channel_id=1, source_target_pairs={{0,8},{24,16},{8,24},{16,0},{1,9},{25,17},{9,25},{17,1},{2,10},{26... | collective-permute-start | bytes 2359304 | tf_op jit(solution)/shard_map/ppermute | solution.py:578
  105.1 23.5 %collective-permute-start.33 = (bf16[512,768]{1,0:T(8,128)(2,1)}, bf16[512,768]{1,0:T(8,128)(2,1)}, u32[]{:S(2)}, u32[]{:S(2)}) collective-permute-start(bf16[512,768]{1,0:T(8,128)(2,1)} %get-tuple-element.106), channel_id=1, source_target_pairs={{0,8},{24,16},{8,24},{16,0},{1,9},{25,17},{9,25},{17,1},{2,10},{26... | collective-permute-start | bytes 2359304 | tf_op jit(solution)/shard_map/ppermute | solution.py:578
  107.8 27.2 %collective-permute-start.36 = (bf16[272,2048]{1,0:T(8,128)(2,1)}, bf16[272,2048]{1,0:T(8,128)(2,1)}, u32[]{:S(2)}, u32[]{:S(2)}) collective-permute-start(bf16[272,2048]{1,0:T(8,128)(2,1)} %tie.7.refs_2_), channel_id=1, source_target_pairs={{0,1},{1,0},{2,3},{3,2},{4,5},{5,4},{6,7},{7,6},{8,9},{9,8},{10,11... | collective-permute-start | bytes 3342344 | tf_op jit(solution)/shard_map/ppermute | solution.py:570
  109.8 60.6 %all-to-all-start = ((bf16[8,128,2048]{2,1,0:T(8,128)(2,1)}), bf16[8,128,2048]{2,1,0:T(8,128)(2,1)}, u32[]{:S(2)}, u32[]{:S(2)}) async-start(bf16[8,128,2048]{2,1,0:T(8,128)(2,1)} %copy-done.8), calls=%async_computation | async-start | bytes 8388608 | tf_op jit(solution)/shard_map/all_to_all | solution.py:617
  118.2 24.6 %collective-permute-start.35 = (bf16[512,768]{1,0:T(8,128)(2,1)S(1)}, bf16[512,768]{1,0:T(8,128)(2,1)S(1)}, u32[]{:S(2)}, u32[]{:S(2)}) collective-permute-start(bf16[512,768]{1,0:T(8,128)(2,1)S(1)} %tie.8.refs_3_.refs_4_), channel_id=1, source_target_pairs={{0,8},{24,16},{1,9},{25,17},{2,10},{26,18},{3,11},{27,19},{4,12},{... | collective-permute-start | bytes 2359304 | tf_op jit(solution)/shard_map/ppermute | solution.py:578
  129.9 15.0 %collective-permute-start.34 = (bf16[512,768]{1,0:T(8,128)(2,1)S(1)}, bf16[512,768]{1,0:T(8,128)(2,1)S(1)}, u32[]{:S(2)}, u32[]{:S(2)}) collective-permute-start(bf16[512,768]{1,0:T(8,128)(2,1)S(1)} %get-tuple-element.108), channel_id=1, source_target_pairs={{8,16},{16,8},{9,17},{17,9},{10,18},{18,10},{11,19},{19,11},{12,20... | collective-permute-start | bytes 2359304 | tf_op jit(solution)/shard_map/ppermute | solution.py:578
  134.5 15.8 %collective-permute-start.38 = (bf16[272,2048]{1,0:T(8,128)(2,1)S(1)}, bf16[272,2048]{1,0:T(8,128)(2,1)S(1)}, u32[]{:S(2)}, u32[]{:S(2)}) collective-permute-start(bf16[272,2048]{1,0:T(8,128)(2,1)S(1)} %copy-done.10), channel_id=1, source_target_pairs={{0,1},{1,0},{2,3},{3,2},{4,5},{5,4},{6,7},{7,6},{8,9},{9,8},{10,11... | collective-permute-start | bytes 3342344 | tf_op jit(solution)/shard_map/ppermute | solution.py:570
  134.6 15.7 %collective-permute-start.37 = (bf16[272,2048]{1,0:T(8,128)(2,1)S(1)}, bf16[272,2048]{1,0:T(8,128)(2,1)S(1)}, u32[]{:S(2)}, u32[]{:S(2)}) collective-permute-start(bf16[272,2048]{1,0:T(8,128)(2,1)S(1)} %copy-done.12), channel_id=1, source_target_pairs={{0,1},{1,0},{2,3},{3,2},{4,5},{5,4},{6,7},{7,6},{8,9},{9,8},{10,11... | collective-permute-start | bytes 3342344 | tf_op jit(solution)/shard_map/ppermute | solution.py:570
  135.1 11.5 %collective-permute-start.40 = (bf16[128,2048]{1,0:T(8,128)(2,1)S(1)}, bf16[128,2048]{1,0:T(8,128)(2,1)S(1)}, u32[]{:S(2)}, u32[]{:S(2)}) collective-permute-start(bf16[128,2048]{1,0:T(8,128)(2,1)S(1)} %copy-done.28), channel_id=1, source_target_pairs={{0,1},{1,0},{2,3},{3,2},{4,5},{5,4},{6,7},{7,6},{8,9},{9,8},{10,11... | collective-permute-start | bytes 1572872 | tf_op jit(solution)/shard_map/ppermute | solution.py:570
  142.8 7.5 %collective-permute-start.39 = (bf16[144,2048]{1,0:T(8,128)(2,1)S(1)}, bf16[144,2048]{1,0:T(8,128)(2,1)S(1)}, u32[]{:S(2)}, u32[]{:S(2)}) collective-permute-start(bf16[144,2048]{1,0:T(8,128)(2,1)S(1)} %copy-done.26), channel_id=1, source_target_pairs={{0,1},{1,0},{2,3},{3,2},{4,5},{5,4},{6,7},{7,6},{8,9},{9,8},{10,11... | collective-permute-start | bytes 1769480 | tf_op jit(solution)/shard_map/ppermute | solution.py:570
  144.9 18.0 %collective-permute-start.41 = (bf16[512,768]{1,0:T(8,128)(2,1)S(1)}, bf16[512,768]{1,0:T(8,128)(2,1)S(1)}, u32[]{:S(2)}, u32[]{:S(2)}) collective-permute-start(bf16[512,768]{1,0:T(8,128)(2,1)S(1)} %get-tuple-element.112), channel_id=1, source_target_pairs={{0,8},{24,16},{8,24},{16,0},{1,9},{25,17},{9,25},{17,1},{2,10},{26... | collective-permute-start | bytes 2359304 | tf_op jit(solution)/shard_map/ppermute | solution.py:578
  146.6 35.3 %collective-permute-start.42 = (bf16[512,768]{1,0:T(8,128)(2,1)}, bf16[512,768]{1,0:T(8,128)(2,1)}, u32[]{:S(2)}, u32[]{:S(2)}) collective-permute-start(bf16[512,768]{1,0:T(8,128)(2,1)} %get-tuple-element.130), channel_id=1, source_target_pairs={{8,16},{16,8},{9,17},{17,9},{10,18},{18,10},{11,19},{19,11},{12,20... | collective-permute-start | bytes 2359304 | tf_op jit(solution)/shard_map/ppermute | solution.py:578
  164.6 31.7 %collective-permute-start.43 = (bf16[512,768]{1,0:T(8,128)(2,1)}, bf16[512,768]{1,0:T(8,128)(2,1)S(1)}, u32[]{:S(2)}, u32[]{:S(2)}) collective-permute-start(bf16[512,768]{1,0:T(8,128)(2,1)} %get-tuple-element.133), channel_id=1, source_target_pairs={{8,16},{16,8},{9,17},{17,9},{10,18},{18,10},{11,19},{19,11},{12,20... | collective-permute-start | bytes 2359304 | tf_op jit(solution)/shard_map/ppermute | solution.py:578
  (53 other events, 335.1 us)

commit v5 on v4

--- a/solution.py
+++ b/solution.py
@@ -608,32 +608,34 @@
         pos, rest_groups, far_rows, rank, prob, x, a, b, w_down, capacity, [token]
     )
     y2 = along(far_gate, inwards)
+    far_up, near_gate, near_up, near_down, *mine, token = gradients(pos, x, dy, dg, du, h, chunk, [token, y1])
+    x3, token = step(pos, far_up, far_down, y1, [token])
+    y3 = along(x3, inwards + across)
     back, token = rows_back(h, dg, du, w_down, w_gate, w_up, capacity, [token])
-    far_up, near_gate, near_up, near_down, *mine, token = gradients(pos, x, dy, dg, du, h, chunk, [token, y1])
-    x3, top, bottom, token = step(pos, far_up, far_down, y1, [token], [raw_x, raw_y], count + EXTRA)
-    y3 = along(x3, inwards + across)
+    x4, top, bottom, token = step(pos, near_down, far_gate, y2, [token], [raw_x, raw_y], count + EXTRA)
+    y4 = along(x4, inwards + across)
     raw_a, raw_b = over(top, 2), over(bottom, 4)
     raw_groups = doubled(raw, raw_x, raw_y, raw_a, raw_b)
     back = lax.all_to_all(tie(back, [token]), "expert", split_axis=0, concat_axis=0, tiled=True)
-    x4, token = step(pos, near_down, far_gate, y2, [token, raw_a, raw_b])
-    y4 = along(x4, inwards + across)
-    x5, token = step(pos, near_gate, far_up, y3, [token])
-    y5 = along(x5, inwards + across)
+    near_gate = tie(near_gate, [token])
+    y5 = along(near_gate, inwards)
+    x5, token = step(pos, far_up, far_up, y3, [token, raw_a, raw_b])
+    far_sum = along(x5, across)
     near_up = tie(near_up, [token])
     y6 = along(near_up, inwards)
     x6, token = step(pos, near_down, near_down, y4, [token])
     z_down = along(x6, middle)
-    x7, token = step(pos, near_up, near_up, y6, [token, z_down])
-    z_up = along(x7, middle)
+    x7, token = step(pos, near_gate, near_gate, y5, [token, z_down, far_sum])
+    z_gate = along(x7, middle)
     *slots, token = partner(pos, raw_groups, (w_gate, w_up, w_down), capacity, count, [token])
-    x8, token = step(pos, near_gate, near_gate, y5, [token])
-    z_gate = along(x8, middle)
+    x8, token = step(pos, near_up, near_up, y6, [token])
+    z_up = along(x8, middle)
     *mine, token = both(pos, slots, mine, [token])
     mixed, tokens_grad, token = combine(meta, back.reshape(2 * peers * capacity, width), capacity, [token])
 
     down, token = total(pos, mine[2], y3, z_down, [token])
-    up, token = total(pos, mine[1], y5, z_up, [token])
-    gate, _ = total(pos, mine[0], y4, z_gate, [token])
+    gate, token = total(pos, mine[0], y4, z_gate, [token])
+    up, _ = total(pos, mine[1], far_sum, z_up, [token])
     grads = [g[None] for g in (gate, up, down)]
     return (mixed, tokens_grad, *grads)
 

time: 199 us -> 198 us (level); the launches traced: 199 us -> 195 us
  waiting for transfers between devices: 84.1 us -> 75.5 us
  starting transfers between devices: 44.2 us -> 48.6 us
    ppermute x34, waiting for transfers between devices: 44.6 us -> 26 us  [over(): return lax.ppermute(x, 'expert', [(i, i ^ bit) for i in range(peers)])]
    ppermute x9 -> x10, waiting for transfers between devices: 39.2 us -> 48.2 us  [along(): return lax.ppermute(x, 'dp', pairs)]
    ppermute x34, starting transfers between devices: 17 us -> 19.5 us  [over(): return lax.ppermute(x, 'expert', [(i, i ^ bit) for i in range(peers)])]
    ppermute x9 -> x10, starting transfers between devices: 22.2 us -> 24.1 us  [along(): return lax.ppermute(x, 'dp', pairs)]
    unnamed x80 -> x70, local copies, waits for them, and re-layouts: 14.4 us -> 14.8 us
  transfers between devices with their start and end apart: 45 -> 46, of which waited for: 23 -> 17; matrix products, arithmetic and copies ran while one was open for 0% -> 0% of each run, Pallas kernels for 26% -> 26%
where the time goes in v5:
time: 198 us; the launch traced here: 195 us
  waiting for transfers between devices  75.5 us (38%)
  Pallas kernels  54.8 us (28%)
  starting transfers between devices  48.6 us (25%)
  local copies, waits for them, and re-layouts  14.9 us (8%)
    pallas_call x21, Pallas kernels, run(): pl.pallas_call(body, in_specs=[ANY] * skip + list(held or [VMEM] * len(op...  54.7 us
    ppermute x10, waiting for transfers between devices, along(): return lax.ppermute(x, 'dp', pairs)  48.2 us
    ppermute x34, waiting for transfers between devices, over(): return lax.ppermute(x, 'expert', [(i, i ^ bit) for i in range(peers)])  26 us
    ppermute x10, starting transfers between devices, along(): return lax.ppermute(x, 'dp', pairs)  24.1 us
    ppermute x34, starting transfers between devices, over(): return lax.ppermute(x, 'expert', [(i, i ^ bit) for i in range(peers)])  19.5 us
    unnamed x70, local copies, waits for them, and re-layouts  14.8 us
    all_to_all x1, starting transfers between devices, local_pairs(): lax.all_to_all(tie(back, [token]), 'expert', split_axis=0, concat_axis=0,...  4.54 us
  transfers between devices with their start and end apart: 46, of which 17 were waited for; matrix products, arithmetic and copies ran while one was open for 0% of the time, Pallas kernels for 26%

profile of v5, /device:TPU:8, one launch (start us, length us, event | category | flops | bytes accessed | tf_op | source)
XLA Modules:
  0.0 194.9 jit_solution(3826597401911703960)
XLA Ops:
  9.2 1.9 copy-done
  11.1 1.9 copy-done.2
  13.0 1.9 copy-done.5
  14.9 5.9 %collective-permute-done.refs_1_.refs_2_ = bf16[144,2048]{1,0:T(8,128)(2,1)S(1)} collective-permute-done((bf16[144,2048]{1,0:T(8,128)(2,1)S(1)}, bf16[144,2048]{1,0:T(8,128)(2,1)S(1)}, u32[]{:S(2)}, u32[]{:S(2)}) %collective-permute-start) | collective-permute-done | bytes 589856 | tf_op jit(solution)/shard_map/ppermute | solution.py:570
  24.9 4.7 %collective-permute-done.2.refs_1_.refs_4_ = bf16[64,2048]{1,0:T(8,128)(2,1)S(1)} collective-permute-done((bf16[64,2048]{1,0:T(8,128)(2,1)S(1)}, bf16[64,2048]{1,0:T(8,128)(2,1)S(1)}, u32[]{:S(2)}, u32[]{:S(2)}) %collective-permute-start.2) | collective-permute-done | bytes 262176 | tf_op jit(solution)/shard_map/ppermute | solution.py:570
  29.6 3.7 %collective-permute-done.3.refs_2_.refs_5_ = bf16[80,2048]{1,0:T(8,128)(2,1)S(1)} collective-permute-done((bf16[80,2048]{1,0:T(8,128)(2,1)S(1)}, bf16[80,2048]{1,0:T(8,128)(2,1)S(1)}, u32[]{:S(2)}, u32[]{:S(2)}) %collective-permute-start.3) | collective-permute-done | bytes 327712 | tf_op jit(solution)/shard_map/ppermute | solution.py:570
  42.3 2.1 %collective-permute-done.8.refs_5_ = bf16[128,512]{1,0:T(8,128)(2,1)S(1)} collective-permute-done((bf16[128,512]{1,0:T(8,128)(2,1)S(1)}, bf16[128,512]{1,0:T(8,128)(2,1)S(1)}, u32[]{:S(2)}, u32[]{:S(2)}) %collective-permute-start.8) | collective-permute-done | bytes 131104 | tf_op jit(solution)/shard_map/ppermute | solution.py:570
  45.8 5.5 %forward.1 = (bf16[512,2048]{1,0:T(8,128)(2,1)S(1)}, f32[8,128]{1,0:T(8,128)S(1)}, f32[8,128]{1,0:T(8,128)S(1)}, bf16[512,768]{1,0:T(8,128)(2,1)S(1)}, f32[512,7...) custom-call(s32[5]{0:T(128)S(1)} %get-tuple-element.71.refs_0_.refs_1_.refs_2_.refs_3_, ...), custom_call_target="tpu_custom_call" | custom-call | flops 3000000000 | bytes 1024 | tf_op jit(solution)/shard_map/forward/pallas_call | solution.py:112
  57.4 5.2 %collective-permute-done.19.refs_5_.refs_1_ = bf16[64,1536]{1,0:T(8,128)(2,1)S(1)} collective-permute-done((bf16[64,1536]{1,0:T(8,128)(2,1)S(1)}, bf16[64,1536]{1,0:T(8,128)(2,1)S(1)}, u32[]{:S(2)}, u32[]{:S(2)}) %collective-permute-start.19) | collective-permute-done | bytes 196640 | tf_op jit(solution)/shard_map/ppermute | solution.py:570
  66.1 4.7 %backward.1 = (bf16[512,2048]{1,0:T(8,128)(2,1)S(1)}, bf16[512,768]{1,0:T(8,128)(2,1)S(1)}, bf16[512,768]{1,0:T(8,128)(2,1)S(1)}, bf16[512,768]{1,0:T(8,128)(2,1)S(1)}, f32[8,128]{1,0:T(8,128)S(1)}) custom-call(f32[8,128]{1,0:T(8,128)S(1)} %get-tuple-element.81.refs_0_, s32[5]{0:T(128)S(1)} %get-tuple-element.71.refs_0_.refs_1_.refs_2_.refs_3_, ...), custom_call_target="tpu_custom_call" | custom-call | flops 50000000 | bytes 1024 | tf_op jit(solution)/shard_map/backward/pallas_call | solution.py:112
  72.1 2.5 %collective-permute-done.26.refs_1_.refs_4_ = bf16[512,768]{1,0:T(8,128)(2,1)S(1)} collective-permute-done((bf16[512,768]{1,0:T(8,128)(2,1)S(1)}, bf16[512,768]{1,0:T(8,128)(2,1)S(1)}, u32[]{:S(2)}, u32[]{:S(2)}) %collective-permute-start.26) | collective-permute-done | bytes 786464 | tf_op jit(solution)/shard_map/ppermute | solution.py:578
  74.6 3.7 %gradients.1 = (bf16[512,768]{1,0:T(8,128)(2,1)S(1)}, bf16[512,768]{1,0:T(8,128)(2,1)S(1)}, bf16[512,768]{1,0:T(8,128)(2,1)S(1)}, bf16[512,768]{1,0:T(8,128)(2,1...) custom-call(f32[8,128]{1,0:T(8,128)S(1)} %get-tuple-element.89.refs_, ...), custom_call_target="tpu_custom_call" | custom-call | flops 7000000000 | bytes 1024 | tf_op jit(solution)/shard_map/gradients/pallas_call | solution.py:112
  82.8 5.1 %rows_back.1 = (bf16[8,128,2048]{2,1,0:T(8,128)(2,1)S(1)}, f32[8,128]{1,0:T(8,128)S(1)}) custom-call(f32[8,128]{1,0:T(8,128)S(1)} %get-tuple-element.96.refs_0_, bf16[512,768]{1,0:T(8,128)(2,1)S(1)} %get-tuple-element.80.refs_11_.refs_7_.refs_1_, bf16[512,768]{1,0:T(8,128)(2,1)S(1)} %get-tuple-element.92.refs_5_.refs_2_, ...), custom_call_target="tpu_custom_call" | custom-call | flops 50000000 | bytes 1024 | tf_op jit(solution)/shard_map/rows_back/pallas_call | solution.py:112
  87.9 5.3 %collective-permute-done.27.refs_4_ = bf16[512,768]{1,0:T(8,128)(2,1)S(1)} collective-permute-done((bf16[512,768]{1,0:T(8,128)(2,1)S(1)}, bf16[512,768]{1,0:T(8,128)(2,1)S(1)}, u32[]{:S(2)}, u32[]{:S(2)}) %collective-permute-start.27) | collective-permute-done | bytes 786464 | tf_op jit(solution)/shard_map/ppermute | solution.py:578
  93.1 2.0 %step.7 = (bf16[512,768]{1,0:T(8,128)(2,1)}, bf16[144,2048]{1,0:T(8,128)(2,1)}, bf16[128,2048]{1,0:T(8,128)(2,1)}, f32[8,128]{1,0:T(8,128)S(1)}) custom-call(f32[8,128]{1,0:T(8,128)S(1)} %get-tuple-element.97.refs_0_, s32[5]{0:T(128)S(1)} %get-tuple-element.71.refs_0_.refs_1_.refs_2_.refs_3_, bf16[512,768]{1,0:T(8,128)(2,1)S(1)} %get-tuple-element.98.refs_2_.refs_3_, ...), custom_call_target="tpu_custom_call" | custom-call | flops 8000000000 | bytes 1024 | tf_op jit(solution)/shard_map/step/pallas_call | solution.py:112
  96.7 2.3 %collective-permute-start.33 = (bf16[512,768]{1,0:T(8,128)(2,1)}, bf16[512,768]{1,0:T(8,128)(2,1)}, u32[]{:S(2)}, u32[]{:S(2)}) collective-permute-start(bf16[512,768]{1,0:T(8,128)(2,1)} %get-tuple-element.105), channel_id=1, source_target_pairs={{0,8},{24,16},{8,24},{16,0},{1,9},{25,17},{9,25},{17,1},{2,10},{26... | collective-permute-start | bytes 2359304 | tf_op jit(solution)/shard_map/ppermute | solution.py:578
  99.9 2.0 %copy-done.8 = bf16[8,128,2048]{2,1,0:T(8,128)(2,1)} copy-done((bf16[8,128,2048]{2,1,0:T(8,128)(2,1)}, bf16[8,128,2048]{2,1,0:T(8,128)(2,1)S(1)}, u32[]{:S(2)}) %copy-start.8) | copy-done | bytes 4194328
  101.9 4.5 %all-to-all-start = ((bf16[8,128,2048]{2,1,0:T(8,128)(2,1)}), bf16[8,128,2048]{2,1,0:T(8,128)(2,1)}, u32[]{:S(2)}, u32[]{:S(2)}) async-start(bf16[8,128,2048]{2,1,0:T(8,128)(2,1)} %copy-done.8), calls=%async_computation | async-start | bytes 8388608 | tf_op jit(solution)/shard_map/all_to_all | solution.py:619
  106.5 3.6 %collective-permute-done.32.refs_6_.refs_3_ = bf16[512,768]{1,0:T(8,128)(2,1)} collective-permute-done((bf16[512,768]{1,0:T(8,128)(2,1)}, bf16[512,768]{1,0:T(8,128)(2,1)}, u32[]{:S(2)}, u32[]{:S(2)}) %collective-permute-start.32) | collective-permute-done | bytes 786464 | tf_op jit(solution)/shard_map/ppermute | solution.py:578
  113.9 5.6 %collective-permute-start.35 = (bf16[512,768]{1,0:T(8,128)(2,1)S(1)}, bf16[512,768]{1,0:T(8,128)(2,1)S(1)}, u32[]{:S(2)}, u32[]{:S(2)}) collective-permute-start(bf16[512,768]{1,0:T(8,128)(2,1)S(1)} %get-tuple-element.108), channel_id=1, source_target_pairs={{8,24},{16,0},{9,25},{17,1},{10,26},{18,2},{11,27},{19,3},{12,28},... | collective-permute-start | bytes 2359304 | tf_op jit(solution)/shard_map/ppermute | solution.py:578
  119.5 7.4 %collective-permute-done.33.refs_4_.refs_3_ = bf16[512,768]{1,0:T(8,128)(2,1)} collective-permute-done((bf16[512,768]{1,0:T(8,128)(2,1)}, bf16[512,768]{1,0:T(8,128)(2,1)}, u32[]{:S(2)}, u32[]{:S(2)}) %collective-permute-start.33) | collective-permute-done | bytes 786464 | tf_op jit(solution)/shard_map/ppermute | solution.py:578
  128.5 3.5 %collective-permute-start.34 = (bf16[512,768]{1,0:T(8,128)(2,1)S(1)}, bf16[512,768]{1,0:T(8,128)(2,1)S(1)}, u32[]{:S(2)}, u32[]{:S(2)}) collective-permute-start(bf16[512,768]{1,0:T(8,128)(2,1)S(1)} %get-tuple-element.107), channel_id=1, source_target_pairs={{8,16},{16,8},{9,17},{17,9},{10,18},{18,10},{11,19},{19,11},{12,20... | collective-permute-start | bytes 2359304 | tf_op jit(solution)/shard_map/ppermute | solution.py:578
  132.5 10.4 %collective-permute-done.36.refs_6_ = bf16[512,768]{1,0:T(8,128)(2,1)S(1)} collective-permute-done((bf16[512,768]{1,0:T(8,128)(2,1)}, bf16[512,768]{1,0:T(8,128)(2,1)S(1)}, u32[]{:S(2)}, u32[]{:S(2)}) %collective-permute-start.36) | collective-permute-done | bytes 786464 | tf_op jit(solution)/shard_map/ppermute | solution.py:578
  144.2 8.3 %collective-permute-done.34.refs_1_.refs_4_ = bf16[512,768]{1,0:T(8,128)(2,1)S(1)} collective-permute-done((bf16[512,768]{1,0:T(8,128)(2,1)S(1)}, bf16[512,768]{1,0:T(8,128)(2,1)S(1)}, u32[]{:S(2)}, u32[]{:S(2)}) %collective-permute-start.34) | collective-permute-done | bytes 786464 | tf_op jit(solution)/shard_map/ppermute | solution.py:578
  154.1 3.6 %collective-permute-start.43 = (bf16[512,768]{1,0:T(8,128)(2,1)}, bf16[512,768]{1,0:T(8,128)(2,1)}, u32[]{:S(2)}, u32[]{:S(2)}) collective-permute-start(bf16[512,768]{1,0:T(8,128)(2,1)} %get-tuple-element.130), channel_id=1, source_target_pairs={{8,16},{16,8},{9,17},{17,9},{10,18},{18,10},{11,19},{19,11},{12,20... | collective-permute-start | bytes 2359304 | tf_op jit(solution)/shard_map/ppermute | solution.py:578
  157.8 8.9 %partner.1 = (bf16[512,2048]{1,0:T(8,128)(2,1)S(1)}, bf16[512,2048]{1,0:T(8,128)(2,1)S(1)}, bf16[512,768]{1,0:T(8,128)(2,1)S(1)}, bf16[512,768]{1,0:T(8,128)(2,1...) custom-call(f32[8,128]{1,0:T(8,128)S(1)} %get-tuple-element.110.refs_0_, ...), custom_call_target="tpu_custom_call" | custom-call | flops 500000000 | bytes 1024 | tf_op jit(solution)/shard_map/partner/pallas_call | solution.py:112
  168.4 2.6 %collective-permute-start.44 = (bf16[512,768]{1,0:T(8,128)(2,1)}, bf16[512,768]{1,0:T(8,128)(2,1)S(1)}, u32[]{:S(2)}, u32[]{:S(2)}) collective-permute-start(bf16[512,768]{1,0:T(8,128)(2,1)} %get-tuple-element.134), channel_id=1, source_target_pairs={{8,16},{16,8},{9,17},{17,9},{10,18},{18,10},{11,19},{19,11},{12,20... | collective-permute-start | bytes 2359304 | tf_op jit(solution)/shard_map/ppermute | solution.py:578
  171.0 2.0 %both.1 = (bf16[512,768]{1,0:T(8,128)(2,1)S(1)}, bf16[512,768]{1,0:T(8,128)(2,1)S(1)}, bf16[512,768]{1,0:T(8,128)(2,1)S(1)}, f32[8,128]{1,0:T(8,128)S(1)}) custom-call(f32[8,128]{1,0:T(8,128)S(1)} %get-tuple-element.113.refs_0_, s32[5]{0:T(128)S(1)} %get-tuple-element.71.refs_0_.refs_1_.refs_2_.refs_3_, bf16[512,2048]{1,0:T(8,128)(2,1)S(1)} %get-tuple-element.114.refs_2_, ...), custom_call_target="tpu_custom_call" | custom-call | flops 250000000 | bytes 1024 | tf_op jit(solution)/shard_map/both/pallas_call | solution.py:112
  173.1 4.4 %combine.1 = (bf16[128,2048]{1,0:T(8,128)(2,1)}, bf16[128,2048]{1,0:T(8,128)(2,1)}, f32[8,128]{1,0:T(8,128)S(1)}) custom-call(f32[8,128]{1,0:T(8,128)S(1)} %get-tuple-element.122.refs_0_, bf16[16,128]{1,0:T(8,128)(2,1)S(1)} %get-tuple-element.73.refs_0_.refs_1_, bf16[1024,2048]{1,0:T(8,128)(2,1)} %bitcast.10.refs_2_), custom_call_target="tpu_custom_call" | custom-call | flops 250000000 | bytes 1024 | tf_op jit(solution)/shard_map/combine/pallas_call | solution.py:112
  177.6 2.3 %total.3 = (bf16[512,768]{1,0:T(8,128)(2,1)}, f32[8,128]{1,0:T(8,128)S(1)}) custom-call(f32[8,128]{1,0:T(8,128)S(1)} %get-tuple-element.126.refs_0_, s32[5]{0:T(128)S(1)} %get-tuple-element.71.refs_0_.refs_1_.refs_2_.refs_3_, bf16[512,768]{1,0:T(8,128)(2,1)S(1)} %get-tuple-element.127.refs_2_, bf16[512,768]{1,0:T(8,128)(2,1)} %collective-permute-done.32.refs_6_.refs_3_, ...), custom_call_target="tpu_custom_call" | custom-call | flops 250000000 | bytes 1024 | tf_op jit(solution)/shard_map/total/pallas_call | solution.py:112
  179.9 2.5 %total.4 = (bf16[512,768]{1,0:T(8,128)(2,1)}, f32[8,128]{1,0:T(8,128)S(1)}) custom-call(f32[8,128]{1,0:T(8,128)S(1)} %get-tuple-element.128.refs_0_, s32[5]{0:T(128)S(1)} %get-tuple-element.71.refs_0_.refs_1_.refs_2_.refs_3_, bf16[512,768]{1,0:T(8,128)(2,1)S(1)} %get-tuple-element.129.refs_2_, bf16[512,768]{1,0:T(8,128)(2,1)} %collective-permute-done.33.refs_4_.refs_3_, ...), custom_call_target="tpu_custom_call" | custom-call | flops 250000000 | bytes 1024 | tf_op jit(solution)/shard_map/total/pallas_call | solution.py:112
  182.3 10.8 %collective-permute-done.44.refs_4_ = bf16[512,768]{1,0:T(8,128)(2,1)S(1)} collective-permute-done((bf16[512,768]{1,0:T(8,128)(2,1)}, bf16[512,768]{1,0:T(8,128)(2,1)S(1)}, u32[]{:S(2)}, u32[]{:S(2)}) %collective-permute-start.44) | collective-permute-done | bytes 786464 | tf_op jit(solution)/shard_map/ppermute | solution.py:578
  (158 shorter events, 52.9 us)
Async XLA Ops:
  5.7 15.1 %collective-permute-start = (bf16[144,2048]{1,0:T(8,128)(2,1)S(1)}, bf16[144,2048]{1,0:T(8,128)(2,1)S(1)}, u32[]{:S(2)}, u32[]{:S(2)}) collective-permute-start(bf16[144,2048]{1,0:T(8,128)(2,1)S(1)} %get-tuple-element.74.refs_1_), channel_id=1, source_target_pairs={{0,2},{1,3},{2,0},{3,1},{4,6},{5,7},{6,4},{7,5},{8,10},{9,11},{10,... | collective-permute-start | bytes 1769480 | tf_op jit(solution)/shard_map/ppermute | solution.py:570
  7.2 14.8 %collective-permute-start.1 = (bf16[144,2048]{1,0:T(8,128)(2,1)S(1)}, bf16[144,2048]{1,0:T(8,128)(2,1)S(1)}, u32[]{:S(2)}, u32[]{:S(2)}) collective-permute-start(bf16[144,2048]{1,0:T(8,128)(2,1)S(1)} %get-tuple-element.74.refs_1_), channel_id=1, source_target_pairs={{0,4},{1,5},{2,6},{3,7},{4,0},{5,1},{6,2},{7,3},{8,12},{9,13},{10,... | collective-permute-start | bytes 1769480 | tf_op jit(solution)/shard_map/ppermute | solution.py:570
  8.8 25.8 %collective-permute-start.4 = (bf16[272,2048]{1,0:T(8,128)(2,1)S(1)}, bf16[272,2048]{1,0:T(8,128)(2,1)}, u32[]{:S(2)}, u32[]{:S(2)}) collective-permute-start(bf16[272,2048]{1,0:T(8,128)(2,1)S(1)} %get-tuple-element.77), channel_id=1, source_target_pairs={{0,8},{8,0},{16,24},{24,16},{1,9},{9,1},{17,25},{25,17},{2,10},{10... | collective-permute-start | bytes 3342344 | tf_op jit(solution)/shard_map/ppermute | solution.py:573
  23.2 11.4 %collective-permute-start.12 = (bf16[144,2048]{1,0:T(8,128)(2,1)S(1)}, bf16[144,2048]{1,0:T(8,128)(2,1)S(1)}, u32[]{:S(2)}, u32[]{:S(2)}) collective-permute-start(bf16[144,2048]{1,0:T(8,128)(2,1)S(1)} %get-tuple-element.74.refs_1_), channel_id=1, source_target_pairs={{0,1},{1,0},{2,3},{3,2},{4,5},{5,4},{6,7},{7,6},{8,9},{9,8},{10,11... | collective-permute-start | bytes 1769480 | tf_op jit(solution)/shard_map/ppermute | solution.py:570
  23.2 10.1 %collective-permute-start.3 = (bf16[80,2048]{1,0:T(8,128)(2,1)S(1)}, bf16[80,2048]{1,0:T(8,128)(2,1)S(1)}, u32[]{:S(2)}, u32[]{:S(2)}) collective-permute-start(bf16[80,2048]{1,0:T(8,128)(2,1)S(1)} %get-tuple-element.76), channel_id=1, source_target_pairs={{0,4},{1,5},{2,6},{3,7},{4,0},{5,1},{6,2},{7,3},{8,12},{9,13},{10,... | collective-permute-start | bytes 983048 | tf_op jit(solution)/shard_map/ppermute | solution.py:570
  24.7 11.6 %collective-permute-start.13 = (bf16[144,2048]{1,0:T(8,128)(2,1)S(1)}, bf16[144,2048]{1,0:T(8,128)(2,1)S(1)}, u32[]{:S(2)}, u32[]{:S(2)}) collective-permute-start(bf16[144,2048]{1,0:T(8,128)(2,1)S(1)} %collective-permute-done.refs_1_.refs_2_), channel_id=1, source_target_pairs={{0,1},{1,0},{2,3},{3,2},{4,5},{5,4},{6,7},{7,6},{8,9},{9,8},{10,11... | collective-permute-start | bytes 1769480 | tf_op jit(solution)/shard_map/ppermute | solution.py:570
  29.6 8.3 %collective-permute-start.14 = (bf16[144,2048]{1,0:T(8,128)(2,1)S(1)}, bf16[144,2048]{1,0:T(8,128)(2,1)S(1)}, u32[]{:S(2)}, u32[]{:S(2)}) collective-permute-start(bf16[144,2048]{1,0:T(8,128)(2,1)S(1)} %collective-permute-done.1.refs_2_.refs_3_), channel_id=1, source_target_pairs={{0,1},{1,0},{2,3},{3,2},{4,5},{5,4},{6,7},{7,6},{8,9},{9,8},{10,11... | collective-permute-start | bytes 1769480 | tf_op jit(solution)/shard_map/ppermute | solution.py:570
  34.6 10.6 %collective-permute-start.16 = (bf16[80,2048]{1,0:T(8,128)(2,1)S(1)}, bf16[80,2048]{1,0:T(8,128)(2,1)S(1)}, u32[]{:S(2)}, u32[]{:S(2)}) collective-permute-start(bf16[80,2048]{1,0:T(8,128)(2,1)S(1)} %collective-permute-done.3.refs_2_.refs_5_), channel_id=1, source_target_pairs={{0,1},{1,0},{2,3},{3,2},{4,5},{5,4},{6,7},{7,6},{8,9},{9,8},{10,11... | collective-permute-start | bytes 983048 | tf_op jit(solution)/shard_map/ppermute | solution.py:570
  36.3 8.0 %collective-permute-start.8 = (bf16[128,512]{1,0:T(8,128)(2,1)S(1)}, bf16[128,512]{1,0:T(8,128)(2,1)S(1)}, u32[]{:S(2)}, u32[]{:S(2)}) collective-permute-start(bf16[128,512]{1,0:T(8,128)(2,1)S(1)} %tie.6.refs_1_), channel_id=1, source_target_pairs={{0,4},{1,5},{2,6},{3,7},{4,0},{5,1},{6,2},{7,3},{8,12},{9,13},{10,... | collective-permute-start | bytes 393224 | tf_op jit(solution)/shard_map/ppermute | solution.py:570
  38.6 15.4 %collective-permute-start.17 = (bf16[128,1536]{1,0:T(8,128)(2,1)S(1)}, bf16[128,1536]{1,0:T(8,128)(2,1)S(1)}, u32[]{:S(2)}, u32[]{:S(2)}) collective-permute-start(bf16[128,1536]{1,0:T(8,128)(2,1)S(1)} %tie.7.refs_2_), channel_id=1, source_target_pairs={{0,2},{1,3},{2,0},{3,1},{4,6},{5,7},{6,4},{7,5},{8,10},{9,11},{10,... | collective-permute-start | bytes 1179656 | tf_op jit(solution)/shard_map/ppermute | solution.py:570
  41.2 13.5 %collective-permute-start.18 = (bf16[128,1536]{1,0:T(8,128)(2,1)S(1)}, bf16[128,1536]{1,0:T(8,128)(2,1)S(1)}, u32[]{:S(2)}, u32[]{:S(2)}) collective-permute-start(bf16[128,1536]{1,0:T(8,128)(2,1)S(1)} %tie.7.refs_2_), channel_id=1, source_target_pairs={{0,4},{1,5},{2,6},{3,7},{4,0},{5,1},{6,2},{7,3},{8,12},{9,13},{10,... | collective-permute-start | bytes 1179656 | tf_op jit(solution)/shard_map/ppermute | solution.py:570
  52.7 21.8 %collective-permute-start.26 = (bf16[512,768]{1,0:T(8,128)(2,1)S(1)}, bf16[512,768]{1,0:T(8,128)(2,1)S(1)}, u32[]{:S(2)}, u32[]{:S(2)}) collective-permute-start(bf16[512,768]{1,0:T(8,128)(2,1)S(1)} %get-tuple-element.90.refs_3_), channel_id=1, source_target_pairs={{0,8},{24,16},{1,9},{25,17},{2,10},{26,18},{3,11},{27,19},{4,12},{... | collective-permute-start | bytes 2359304 | tf_op jit(solution)/shard_map/ppermute | solution.py:578
  54.1 9.5 %collective-permute-start.22 = (bf16[128,1536]{1,0:T(8,128)(2,1)S(1)}, bf16[128,1536]{1,0:T(8,128)(2,1)S(1)}, u32[]{:S(2)}, u32[]{:S(2)}) collective-permute-start(bf16[128,1536]{1,0:T(8,128)(2,1)S(1)} %collective-permute-done.17.refs_1_.refs_3_), channel_id=1, source_target_pairs={{0,1},{1,0},{2,3},{3,2},{4,5},{5,4},{6,7},{7,6},{8,9},{9,8},{10,11... | collective-permute-start | bytes 1179656 | tf_op jit(solution)/shard_map/ppermute | solution.py:570
  54.6 9.8 %collective-permute-start.23 = (bf16[128,1536]{1,0:T(8,128)(2,1)S(1)}, bf16[128,1536]{1,0:T(8,128)(2,1)S(1)}, u32[]{:S(2)}, u32[]{:S(2)}) collective-permute-start(bf16[128,1536]{1,0:T(8,128)(2,1)S(1)} %collective-permute-done.18.refs_2_.refs_4_), channel_id=1, source_target_pairs={{0,1},{1,0},{2,3},{3,2},{4,5},{5,4},{6,7},{7,6},{8,9},{9,8},{10,11... | collective-permute-start | bytes 1179656 | tf_op jit(solution)/shard_map/ppermute | solution.py:570
  63.5 29.6 %collective-permute-start.28 = (bf16[272,2048]{1,0:T(8,128)(2,1)}, bf16[272,2048]{1,0:T(8,128)(2,1)S(1)}, u32[]{:S(2)}, u32[]{:S(2)}) collective-permute-start(bf16[272,2048]{1,0:T(8,128)(2,1)} %tie.8.refs_2_), channel_id=1, source_target_pairs={{0,2},{1,3},{2,0},{3,1},{4,6},{5,7},{6,4},{7,5},{8,10},{9,11},{10,... | collective-permute-start | bytes 3342344 | tf_op jit(solution)/shard_map/ppermute | solution.py:570
  64.4 28.7 %collective-permute-start.29 = (bf16[272,2048]{1,0:T(8,128)(2,1)}, bf16[272,2048]{1,0:T(8,128)(2,1)S(1)}, u32[]{:S(2)}, u32[]{:S(2)}) collective-permute-start(bf16[272,2048]{1,0:T(8,128)(2,1)} %tie.8.refs_2_), channel_id=1, source_target_pairs={{0,4},{1,5},{2,6},{3,7},{4,0},{5,1},{6,2},{7,3},{8,12},{9,13},{10,... | collective-permute-start | bytes 3342344 | tf_op jit(solution)/shard_map/ppermute | solution.py:570
  70.8 22.3 %collective-permute-start.27 = (bf16[512,768]{1,0:T(8,128)(2,1)S(1)}, bf16[512,768]{1,0:T(8,128)(2,1)S(1)}, u32[]{:S(2)}, u32[]{:S(2)}) collective-permute-start(bf16[512,768]{1,0:T(8,128)(2,1)S(1)} %get-tuple-element.99.refs_3_), channel_id=1, source_target_pairs={{0,8},{24,16},{1,9},{25,17},{2,10},{26,18},{3,11},{27,19},{4,12},{... | collective-permute-start | bytes 2359304 | tf_op jit(solution)/shard_map/ppermute | solution.py:578
  81.2 28.9 %collective-permute-start.32 = (bf16[512,768]{1,0:T(8,128)(2,1)}, bf16[512,768]{1,0:T(8,128)(2,1)}, u32[]{:S(2)}, u32[]{:S(2)}) collective-permute-start(bf16[512,768]{1,0:T(8,128)(2,1)} %get-tuple-element.103), channel_id=1, source_target_pairs={{0,8},{24,16},{8,24},{16,0},{1,9},{25,17},{9,25},{17,1},{2,10},{26... | collective-permute-start | bytes 2359304 | tf_op jit(solution)/shard_map/ppermute | solution.py:578
  95.2 16.2 %collective-permute-start.30 = (bf16[144,2048]{1,0:T(8,128)(2,1)}, bf16[144,2048]{1,0:T(8,128)(2,1)}, u32[]{:S(2)}, u32[]{:S(2)}) collective-permute-start(bf16[144,2048]{1,0:T(8,128)(2,1)} %get-tuple-element.101), channel_id=1, source_target_pairs={{0,2},{1,3},{2,0},{3,1},{4,6},{5,7},{6,4},{7,5},{8,10},{9,11},{10,... | collective-permute-start | bytes 1769480 | tf_op jit(solution)/shard_map/ppermute | solution.py:570
  96.0 15.4 %collective-permute-start.31 = (bf16[128,2048]{1,0:T(8,128)(2,1)}, bf16[128,2048]{1,0:T(8,128)(2,1)}, u32[]{:S(2)}, u32[]{:S(2)}) collective-permute-start(bf16[128,2048]{1,0:T(8,128)(2,1)} %get-tuple-element.102), channel_id=1, source_target_pairs={{0,4},{1,5},{2,6},{3,7},{4,0},{5,1},{6,2},{7,3},{8,12},{9,13},{10,... | collective-permute-start | bytes 1572872 | tf_op jit(solution)/shard_map/ppermute | solution.py:570
  96.7 30.2 %collective-permute-start.33 = (bf16[512,768]{1,0:T(8,128)(2,1)}, bf16[512,768]{1,0:T(8,128)(2,1)}, u32[]{:S(2)}, u32[]{:S(2)}) collective-permute-start(bf16[512,768]{1,0:T(8,128)(2,1)} %get-tuple-element.105), channel_id=1, source_target_pairs={{0,8},{24,16},{8,24},{16,0},{1,9},{25,17},{9,25},{17,1},{2,10},{26... | collective-permute-start | bytes 2359304 | tf_op jit(solution)/shard_map/ppermute | solution.py:578
  99.0 33.0 %collective-permute-start.37 = (bf16[272,2048]{1,0:T(8,128)(2,1)}, bf16[272,2048]{1,0:T(8,128)(2,1)}, u32[]{:S(2)}, u32[]{:S(2)}) collective-permute-start(bf16[272,2048]{1,0:T(8,128)(2,1)} %tie.8.refs_2_), channel_id=1, source_target_pairs={{0,1},{1,0},{2,3},{3,2},{4,5},{5,4},{6,7},{7,6},{8,9},{9,8},{10,11... | collective-permute-start | bytes 3342344 | tf_op jit(solution)/shard_map/ppermute | solution.py:570
  101.9 71.2 %all-to-all-start = ((bf16[8,128,2048]{2,1,0:T(8,128)(2,1)}), bf16[8,128,2048]{2,1,0:T(8,128)(2,1)}, u32[]{:S(2)}, u32[]{:S(2)}) async-start(bf16[8,128,2048]{2,1,0:T(8,128)(2,1)} %copy-done.8), calls=%async_computation | async-start | bytes 8388608 | tf_op jit(solution)/shard_map/all_to_all | solution.py:619
  110.1 32.8 %collective-permute-start.36 = (bf16[512,768]{1,0:T(8,128)(2,1)}, bf16[512,768]{1,0:T(8,128)(2,1)S(1)}, u32[]{:S(2)}, u32[]{:S(2)}) collective-permute-start(bf16[512,768]{1,0:T(8,128)(2,1)} %copy-done.21), channel_id=1, source_target_pairs={{0,8},{24,16},{1,9},{25,17},{2,10},{26,18},{3,11},{27,19},{4,12},{... | collective-permute-start | bytes 2359304 | tf_op jit(solution)/shard_map/ppermute | solution.py:578
  113.9 29.0 %collective-permute-start.35 = (bf16[512,768]{1,0:T(8,128)(2,1)S(1)}, bf16[512,768]{1,0:T(8,128)(2,1)S(1)}, u32[]{:S(2)}, u32[]{:S(2)}) collective-permute-start(bf16[512,768]{1,0:T(8,128)(2,1)S(1)} %get-tuple-element.108), channel_id=1, source_target_pairs={{8,24},{16,0},{9,25},{17,1},{10,26},{18,2},{11,27},{19,3},{12,28},... | collective-permute-start | bytes 2359304 | tf_op jit(solution)/shard_map/ppermute | solution.py:578
  128.5 24.0 %collective-permute-start.34 = (bf16[512,768]{1,0:T(8,128)(2,1)S(1)}, bf16[512,768]{1,0:T(8,128)(2,1)S(1)}, u32[]{:S(2)}, u32[]{:S(2)}) collective-permute-start(bf16[512,768]{1,0:T(8,128)(2,1)S(1)} %get-tuple-element.107), channel_id=1, source_target_pairs={{8,16},{16,8},{9,17},{17,9},{10,18},{18,10},{11,19},{19,11},{12,20... | collective-permute-start | bytes 2359304 | tf_op jit(solution)/shard_map/ppermute | solution.py:578
  132.0 25.8 %collective-permute-start.38 = (bf16[272,2048]{1,0:T(8,128)(2,1)S(1)}, bf16[272,2048]{1,0:T(8,128)(2,1)S(1)}, u32[]{:S(2)}, u32[]{:S(2)}) collective-permute-start(bf16[272,2048]{1,0:T(8,128)(2,1)S(1)} %copy-done.10), channel_id=1, source_target_pairs={{0,1},{1,0},{2,3},{3,2},{4,5},{5,4},{6,7},{7,6},{8,9},{9,8},{10,11... | collective-permute-start | bytes 3342344 | tf_op jit(solution)/shard_map/ppermute | solution.py:570
  132.1 25.7 %collective-permute-start.39 = (bf16[272,2048]{1,0:T(8,128)(2,1)S(1)}, bf16[272,2048]{1,0:T(8,128)(2,1)S(1)}, u32[]{:S(2)}, u32[]{:S(2)}) collective-permute-start(bf16[272,2048]{1,0:T(8,128)(2,1)S(1)} %copy-done.12), channel_id=1, source_target_pairs={{0,1},{1,0},{2,3},{3,2},{4,5},{5,4},{6,7},{7,6},{8,9},{9,8},{10,11... | collective-permute-start | bytes 3342344 | tf_op jit(solution)/shard_map/ppermute | solution.py:570
  142.9 11.2 %collective-permute-start.41 = (bf16[128,2048]{1,0:T(8,128)(2,1)}, bf16[128,2048]{1,0:T(8,128)(2,1)S(1)}, u32[]{:S(2)}, u32[]{:S(2)}) collective-permute-start(bf16[128,2048]{1,0:T(8,128)(2,1)} %collective-permute-done.31.refs_2_.refs_6_), channel_id=1, source_target_pairs={{0,1},{1,0},{2,3},{3,2},{4,5},{5,4},{6,7},{7,6},{8,9},{9,8},{10,11... | collective-permute-start | bytes 1572872 | tf_op jit(solution)/shard_map/ppermute | solution.py:570
  142.9 23.8 %collective-permute-start.42 = (bf16[512,768]{1,0:T(8,128)(2,1)S(1)}, bf16[512,768]{1,0:T(8,128)(2,1)S(1)}, u32[]{:S(2)}, u32[]{:S(2)}) collective-permute-start(bf16[512,768]{1,0:T(8,128)(2,1)S(1)} %tie.10.refs_2_.refs_3_), channel_id=1, source_target_pairs={{0,8},{24,16},{1,9},{25,17},{2,10},{26,18},{3,11},{27,19},{4,12},{... | collective-permute-start | bytes 2359304 | tf_op jit(solution)/shard_map/ppermute | solution.py:578
  154.1 25.7 %collective-permute-start.43 = (bf16[512,768]{1,0:T(8,128)(2,1)}, bf16[512,768]{1,0:T(8,128)(2,1)}, u32[]{:S(2)}, u32[]{:S(2)}) collective-permute-start(bf16[512,768]{1,0:T(8,128)(2,1)} %get-tuple-element.130), channel_id=1, source_target_pairs={{8,16},{16,8},{9,17},{17,9},{10,18},{18,10},{11,19},{19,11},{12,20... | collective-permute-start | bytes 2359304 | tf_op jit(solution)/shard_map/ppermute | solution.py:578
  168.4 24.7 %collective-permute-start.44 = (bf16[512,768]{1,0:T(8,128)(2,1)}, bf16[512,768]{1,0:T(8,128)(2,1)S(1)}, u32[]{:S(2)}, u32[]{:S(2)}) collective-permute-start(bf16[512,768]{1,0:T(8,128)(2,1)} %get-tuple-element.134), channel_id=1, source_target_pairs={{8,16},{16,8},{9,17},{17,9},{10,18},{18,10},{11,19},{19,11},{12,20... | collective-permute-start | bytes 2359304 | tf_op jit(solution)/shard_map/ppermute | solution.py:578
  (49 other events, 271.3 us)

commit v6 on v5

--- a/solution.py
+++ b/solution.py
@@ -616,11 +616,11 @@
     y4 = along(x4, inwards + across)
     raw_a, raw_b = over(top, 2), over(bottom, 4)
     raw_groups = doubled(raw, raw_x, raw_y, raw_a, raw_b)
-    back = lax.all_to_all(tie(back, [token]), "expert", split_axis=0, concat_axis=0, tiled=True)
     near_gate = tie(near_gate, [token])
     y5 = along(near_gate, inwards)
     x5, token = step(pos, far_up, far_up, y3, [token, raw_a, raw_b])
     far_sum = along(x5, across)
+    back = lax.all_to_all(tie(back, [token]), "expert", split_axis=0, concat_axis=0, tiled=True)
     near_up = tie(near_up, [token])
     y6 = along(near_up, inwards)
     x6, token = step(pos, near_down, near_down, y4, [token])

time: 198 us -> 197 us (level); the launches traced: 195 us -> 197 us
  no operation moved by 1% of the time
where the time goes in v6:
time: 197 us
  waiting for transfers between devices  76.1 us (39%)
  Pallas kernels  54.9 us (28%)
  starting transfers between devices  50 us (25%)
  local copies, waits for them, and re-layouts  14.5 us (7%)
    pallas_call x21, Pallas kernels, run(): pl.pallas_call(body, in_specs=[ANY] * skip + list(held or [VMEM] * len(op...  54.9 us
    ppermute x10, waiting for transfers between devices, along(): return lax.ppermute(x, 'dp', pairs)  47.1 us
    ppermute x34, waiting for transfers between devices, over(): return lax.ppermute(x, 'expert', [(i, i ^ bit) for i in range(peers)])  26 us
    ppermute x10, starting transfers between devices, along(): return lax.ppermute(x, 'dp', pairs)  25.5 us
    ppermute x34, starting transfers between devices, over(): return lax.ppermute(x, 'expert', [(i, i ^ bit) for i in range(peers)])  19.5 us
    unnamed x70, local copies, waits for them, and re-layouts  14.4 us
    all_to_all x1, starting transfers between devices, local_pairs(): lax.all_to_all(tie(back, [token]), 'expert', split_axis=0, concat_axis=0,...  4.54 us
  transfers between devices with their start and end apart: 46, of which 17 were waited for; matrix products, arithmetic and copies ran while one was open for 0% of the time, Pallas kernels for 26%

profile of v6, /device:TPU:8, one launch (start us, length us, event | category | flops | bytes accessed | tf_op | source)
XLA Modules:
  0.0 196.6 jit_solution(8215777664250530477)
XLA Ops:
  9.2 1.9 copy-done
  11.1 1.9 copy-done.2
  13.0 1.9 copy-done.5
  14.9 5.9 %collective-permute-done.refs_1_.refs_2_ = bf16[144,2048]{1,0:T(8,128)(2,1)S(1)} collective-permute-done((bf16[144,2048]{1,0:T(8,128)(2,1)S(1)}, bf16[144,2048]{1,0:T(8,128)(2,1)S(1)}, u32[]{:S(2)}, u32[]{:S(2)}) %collective-permute-start) | collective-permute-done | bytes 589856 | tf_op jit(solution)/shard_map/ppermute | solution.py:570
  24.9 4.7 %collective-permute-done.2.refs_1_.refs_4_ = bf16[64,2048]{1,0:T(8,128)(2,1)S(1)} collective-permute-done((bf16[64,2048]{1,0:T(8,128)(2,1)S(1)}, bf16[64,2048]{1,0:T(8,128)(2,1)S(1)}, u32[]{:S(2)}, u32[]{:S(2)}) %collective-permute-start.2) | collective-permute-done | bytes 262176 | tf_op jit(solution)/shard_map/ppermute | solution.py:570
  29.6 3.7 %collective-permute-done.3.refs_2_.refs_5_ = bf16[80,2048]{1,0:T(8,128)(2,1)S(1)} collective-permute-done((bf16[80,2048]{1,0:T(8,128)(2,1)S(1)}, bf16[80,2048]{1,0:T(8,128)(2,1)S(1)}, u32[]{:S(2)}, u32[]{:S(2)}) %collective-permute-start.3) | collective-permute-done | bytes 327712 | tf_op jit(solution)/shard_map/ppermute | solution.py:570
  42.3 2.1 %collective-permute-done.8.refs_5_ = bf16[128,512]{1,0:T(8,128)(2,1)S(1)} collective-permute-done((bf16[128,512]{1,0:T(8,128)(2,1)S(1)}, bf16[128,512]{1,0:T(8,128)(2,1)S(1)}, u32[]{:S(2)}, u32[]{:S(2)}) %collective-permute-start.8) | collective-permute-done | bytes 131104 | tf_op jit(solution)/shard_map/ppermute | solution.py:570
  45.8 5.5 %forward.1 = (bf16[512,2048]{1,0:T(8,128)(2,1)S(1)}, f32[8,128]{1,0:T(8,128)S(1)}, f32[8,128]{1,0:T(8,128)S(1)}, bf16[512,768]{1,0:T(8,128)(2,1)S(1)}, f32[512,7...) custom-call(s32[5]{0:T(128)S(1)} %get-tuple-element.71.refs_0_.refs_1_.refs_2_.refs_3_, ...), custom_call_target="tpu_custom_call" | custom-call | flops 3000000000 | bytes 1024 | tf_op jit(solution)/shard_map/forward/pallas_call | solution.py:112
  57.4 5.2 %collective-permute-done.19.refs_5_.refs_1_ = bf16[64,1536]{1,0:T(8,128)(2,1)S(1)} collective-permute-done((bf16[64,1536]{1,0:T(8,128)(2,1)S(1)}, bf16[64,1536]{1,0:T(8,128)(2,1)S(1)}, u32[]{:S(2)}, u32[]{:S(2)}) %collective-permute-start.19) | collective-permute-done | bytes 196640 | tf_op jit(solution)/shard_map/ppermute | solution.py:570
  66.1 4.7 %backward.1 = (bf16[512,2048]{1,0:T(8,128)(2,1)S(1)}, bf16[512,768]{1,0:T(8,128)(2,1)S(1)}, bf16[512,768]{1,0:T(8,128)(2,1)S(1)}, bf16[512,768]{1,0:T(8,128)(2,1)S(1)}, f32[8,128]{1,0:T(8,128)S(1)}) custom-call(f32[8,128]{1,0:T(8,128)S(1)} %get-tuple-element.81.refs_0_, s32[5]{0:T(128)S(1)} %get-tuple-element.71.refs_0_.refs_1_.refs_2_.refs_3_, ...), custom_call_target="tpu_custom_call" | custom-call | flops 50000000 | bytes 1024 | tf_op jit(solution)/shard_map/backward/pallas_call | solution.py:112
  72.1 2.5 %collective-permute-done.26.refs_1_.refs_4_ = bf16[512,768]{1,0:T(8,128)(2,1)S(1)} collective-permute-done((bf16[512,768]{1,0:T(8,128)(2,1)S(1)}, bf16[512,768]{1,0:T(8,128)(2,1)S(1)}, u32[]{:S(2)}, u32[]{:S(2)}) %collective-permute-start.26) | collective-permute-done | bytes 786464 | tf_op jit(solution)/shard_map/ppermute | solution.py:578
  74.6 3.7 %gradients.1 = (bf16[512,768]{1,0:T(8,128)(2,1)S(1)}, bf16[512,768]{1,0:T(8,128)(2,1)}, bf16[512,768]{1,0:T(8,128)(2,1)S(1)}, bf16[512,768]{1,0:T(8,128)(2,1)S(1...) custom-call(f32[8,128]{1,0:T(8,128)S(1)} %get-tuple-element.89.refs_, ...), custom_call_target="tpu_custom_call" | custom-call | flops 7000000000 | bytes 1024 | tf_op jit(solution)/shard_map/gradients/pallas_call | solution.py:112
  82.2 5.1 %rows_back.1 = (bf16[8,128,2048]{2,1,0:T(8,128)(2,1)S(1)}, f32[8,128]{1,0:T(8,128)S(1)}) custom-call(f32[8,128]{1,0:T(8,128)S(1)} %get-tuple-element.96.refs_0_, bf16[512,768]{1,0:T(8,128)(2,1)S(1)} %get-tuple-element.80.refs_11_.refs_7_.refs_1_, bf16[512,768]{1,0:T(8,128)(2,1)S(1)} %get-tuple-element.92.refs_5_.refs_2_, ...), custom_call_target="tpu_custom_call" | custom-call | flops 50000000 | bytes 1024 | tf_op jit(solution)/shard_map/rows_back/pallas_call | solution.py:112
  87.3 5.8 %collective-permute-done.27.refs_4_ = bf16[512,768]{1,0:T(8,128)(2,1)S(1)} collective-permute-done((bf16[512,768]{1,0:T(8,128)(2,1)S(1)}, bf16[512,768]{1,0:T(8,128)(2,1)S(1)}, u32[]{:S(2)}, u32[]{:S(2)}) %collective-permute-start.27) | collective-permute-done | bytes 786464 | tf_op jit(solution)/shard_map/ppermute | solution.py:578
  93.2 1.7 step.7
  96.4 2.3 %collective-permute-start.33 = (bf16[512,768]{1,0:T(8,128)(2,1)}, bf16[512,768]{1,0:T(8,128)(2,1)}, u32[]{:S(2)}, u32[]{:S(2)}) collective-permute-start(bf16[512,768]{1,0:T(8,128)(2,1)} %get-tuple-element.105), channel_id=1, source_target_pairs={{0,8},{24,16},{8,24},{16,0},{1,9},{25,17},{9,25},{17,1},{2,10},{26... | collective-permute-start | bytes 2359304 | tf_op jit(solution)/shard_map/ppermute | solution.py:578
  98.7 11.3 %collective-permute-done.32.refs_6_.refs_3_ = bf16[512,768]{1,0:T(8,128)(2,1)S(1)} collective-permute-done((bf16[512,768]{1,0:T(8,128)(2,1)S(1)}, bf16[512,768]{1,0:T(8,128)(2,1)S(1)}, u32[]{:S(2)}, u32[]{:S(2)}) %collective-permute-start.32) | collective-permute-done | bytes 786464 | tf_op jit(solution)/shard_map/ppermute | solution.py:578
  113.0 7.3 %collective-permute-start.35 = (bf16[512,768]{1,0:T(8,128)(2,1)}, bf16[512,768]{1,0:T(8,128)(2,1)}, u32[]{:S(2)}, u32[]{:S(2)}) collective-permute-start(bf16[512,768]{1,0:T(8,128)(2,1)} %get-tuple-element.108), channel_id=1, source_target_pairs={{8,24},{16,0},{9,25},{17,1},{10,26},{18,2},{11,27},{19,3},{12,28},... | collective-permute-start | bytes 2359304 | tf_op jit(solution)/shard_map/ppermute | solution.py:578
  120.3 2.0 %copy-done.8 = bf16[8,128,2048]{2,1,0:T(8,128)(2,1)} copy-done((bf16[8,128,2048]{2,1,0:T(8,128)(2,1)}, bf16[8,128,2048]{2,1,0:T(8,128)(2,1)S(1)}, u32[]{:S(2)}) %copy-start.8) | copy-done | bytes 4194328
  122.3 4.5 %all-to-all-start = ((bf16[8,128,2048]{2,1,0:T(8,128)(2,1)}), bf16[8,128,2048]{2,1,0:T(8,128)(2,1)}, u32[]{:S(2)}, u32[]{:S(2)}) async-start(bf16[8,128,2048]{2,1,0:T(8,128)(2,1)} %copy-done.8), calls=%async_computation | async-start | bytes 8388608 | tf_op jit(solution)/shard_map/all_to_all | solution.py:623
  129.7 3.3 %collective-permute-start.34 = (bf16[512,768]{1,0:T(8,128)(2,1)S(1)}, bf16[512,768]{1,0:T(8,128)(2,1)S(1)}, u32[]{:S(2)}, u32[]{:S(2)}) collective-permute-start(bf16[512,768]{1,0:T(8,128)(2,1)S(1)} %get-tuple-element.107), channel_id=1, source_target_pairs={{8,16},{16,8},{9,17},{17,9},{10,18},{18,10},{11,19},{19,11},{12,20... | collective-permute-start | bytes 2359304 | tf_op jit(solution)/shard_map/ppermute | solution.py:578
  133.5 9.5 %collective-permute-done.36.refs_6_ = bf16[512,768]{1,0:T(8,128)(2,1)} collective-permute-done((bf16[512,768]{1,0:T(8,128)(2,1)}, bf16[512,768]{1,0:T(8,128)(2,1)}, u32[]{:S(2)}, u32[]{:S(2)}) %collective-permute-start.36) | collective-permute-done | bytes 786464 | tf_op jit(solution)/shard_map/ppermute | solution.py:578
  144.3 8.2 %collective-permute-done.34.refs_1_.refs_4_ = bf16[512,768]{1,0:T(8,128)(2,1)S(1)} collective-permute-done((bf16[512,768]{1,0:T(8,128)(2,1)S(1)}, bf16[512,768]{1,0:T(8,128)(2,1)S(1)}, u32[]{:S(2)}, u32[]{:S(2)}) %collective-permute-start.34) | collective-permute-done | bytes 786464 | tf_op jit(solution)/shard_map/ppermute | solution.py:578
  152.6 3.0 %step.10 = (bf16[512,768]{1,0:T(8,128)(2,1)}, f32[8,128]{1,0:T(8,128)S(1)}) custom-call(f32[8,128]{1,0:T(8,128)S(1)} %get-tuple-element.106.refs_0_, bf16[512,768]{1,0:T(8,128)(2,1)S(1)} %collective-permute-done.34.refs_1_.refs_4_, bf16[512,768]{1,0:T(8,128)(2,1)} %collective-permute-done.35.refs_2_.refs_3_, ...), custom_call_target="tpu_custom_call" | custom-call | flops 8000000000 | bytes 1024 | tf_op jit(solution)/shard_map/step/pallas_call | solution.py:112
  155.6 3.6 %collective-permute-start.43 = (bf16[512,768]{1,0:T(8,128)(2,1)}, bf16[512,768]{1,0:T(8,128)(2,1)}, u32[]{:S(2)}, u32[]{:S(2)}) collective-permute-start(bf16[512,768]{1,0:T(8,128)(2,1)} %get-tuple-element.130), channel_id=1, source_target_pairs={{8,16},{16,8},{9,17},{17,9},{10,18},{18,10},{11,19},{19,11},{12,20... | collective-permute-start | bytes 2359304 | tf_op jit(solution)/shard_map/ppermute | solution.py:578
  159.3 8.6 %partner.1 = (bf16[512,2048]{1,0:T(8,128)(2,1)S(1)}, bf16[512,2048]{1,0:T(8,128)(2,1)S(1)}, bf16[512,768]{1,0:T(8,128)(2,1)S(1)}, bf16[512,768]{1,0:T(8,128)(2,1...) custom-call(f32[8,128]{1,0:T(8,128)S(1)} %get-tuple-element.110.refs_0_, ...), custom_call_target="tpu_custom_call" | custom-call | flops 500000000 | bytes 1024 | tf_op jit(solution)/shard_map/partner/pallas_call | solution.py:112
  169.6 2.6 %collective-permute-start.44 = (bf16[512,768]{1,0:T(8,128)(2,1)}, bf16[512,768]{1,0:T(8,128)(2,1)S(1)}, u32[]{:S(2)}, u32[]{:S(2)}) collective-permute-start(bf16[512,768]{1,0:T(8,128)(2,1)} %get-tuple-element.134), channel_id=1, source_target_pairs={{8,16},{16,8},{9,17},{17,9},{10,18},{18,10},{11,19},{19,11},{12,20... | collective-permute-start | bytes 2359304 | tf_op jit(solution)/shard_map/ppermute | solution.py:578
  172.2 2.0 %both.1 = (bf16[512,768]{1,0:T(8,128)(2,1)S(1)}, bf16[512,768]{1,0:T(8,128)(2,1)S(1)}, bf16[512,768]{1,0:T(8,128)(2,1)S(1)}, f32[8,128]{1,0:T(8,128)S(1)}) custom-call(f32[8,128]{1,0:T(8,128)S(1)} %get-tuple-element.113.refs_0_, s32[5]{0:T(128)S(1)} %get-tuple-element.71.refs_0_.refs_1_.refs_2_.refs_3_, bf16[512,2048]{1,0:T(8,128)(2,1)S(1)} %get-tuple-element.114.refs_2_, ...), custom_call_target="tpu_custom_call" | custom-call | flops 250000000 | bytes 1024 | tf_op jit(solution)/shard_map/both/pallas_call | solution.py:112
  176.0 4.5 %combine.1 = (bf16[128,2048]{1,0:T(8,128)(2,1)}, bf16[128,2048]{1,0:T(8,128)(2,1)}, f32[8,128]{1,0:T(8,128)S(1)}) custom-call(f32[8,128]{1,0:T(8,128)S(1)} %get-tuple-element.122.refs_0_, bf16[16,128]{1,0:T(8,128)(2,1)S(1)} %get-tuple-element.73.refs_0_.refs_1_, bf16[1024,2048]{1,0:T(8,128)(2,1)} %bitcast.10.refs_2_), custom_call_target="tpu_custom_call" | custom-call | flops 250000000 | bytes 1024 | tf_op jit(solution)/shard_map/combine/pallas_call | solution.py:112
  182.2 2.5 %total.4 = (bf16[512,768]{1,0:T(8,128)(2,1)}, f32[8,128]{1,0:T(8,128)S(1)}) custom-call(f32[8,128]{1,0:T(8,128)S(1)} %get-tuple-element.128.refs_0_, s32[5]{0:T(128)S(1)} %get-tuple-element.71.refs_0_.refs_1_.refs_2_.refs_3_, bf16[512,768]{1,0:T(8,128)(2,1)S(1)} %get-tuple-element.129.refs_2_, bf16[512,768]{1,0:T(8,128)(2,1)} %collective-permute-done.33.refs_4_.refs_3_, ...), custom_call_target="tpu_custom_call" | custom-call | flops 250000000 | bytes 1024 | tf_op jit(solution)/shard_map/total/pallas_call | solution.py:112
  184.6 9.7 %collective-permute-done.44.refs_4_ = bf16[512,768]{1,0:T(8,128)(2,1)S(1)} collective-permute-done((bf16[512,768]{1,0:T(8,128)(2,1)}, bf16[512,768]{1,0:T(8,128)(2,1)S(1)}, u32[]{:S(2)}, u32[]{:S(2)}) %collective-permute-start.44) | collective-permute-done | bytes 786464 | tf_op jit(solution)/shard_map/ppermute | solution.py:578
  194.3 2.2 %total.5 = (bf16[512,768]{1,0:T(8,128)(2,1)}, f32[8,128]{1,0:T(8,128)}) custom-call(f32[8,128]{1,0:T(8,128)S(1)} %get-tuple-element.132.refs_0_, s32[5]{0:T(128)S(1)} %get-tuple-element.71.refs_0_.refs_1_.refs_2_.refs_3_, bf16[512,768]{1,0:T(8,128)(2,1)S(1)} %get-tuple-element.133.refs_2_, bf16[512,768]{1,0:T(8,128)(2,1)} %collective-permute-done.35.refs_2_.refs_3_, ...), custom_call_target="tpu_custom_call" | custom-call | flops 250000000 | bytes 1024 | tf_op jit(solution)/shard_map/total/pallas_call | solution.py:112
  (158 shorter events, 52.0 us)
Async XLA Ops:
  5.7 15.1 %collective-permute-start = (bf16[144,2048]{1,0:T(8,128)(2,1)S(1)}, bf16[144,2048]{1,0:T(8,128)(2,1)S(1)}, u32[]{:S(2)}, u32[]{:S(2)}) collective-permute-start(bf16[144,2048]{1,0:T(8,128)(2,1)S(1)} %get-tuple-element.74.refs_1_), channel_id=1, source_target_pairs={{0,2},{1,3},{2,0},{3,1},{4,6},{5,7},{6,4},{7,5},{8,10},{9,11},{10,... | collective-permute-start | bytes 1769480 | tf_op jit(solution)/shard_map/ppermute | solution.py:570
  7.2 14.8 %collective-permute-start.1 = (bf16[144,2048]{1,0:T(8,128)(2,1)S(1)}, bf16[144,2048]{1,0:T(8,128)(2,1)S(1)}, u32[]{:S(2)}, u32[]{:S(2)}) collective-permute-start(bf16[144,2048]{1,0:T(8,128)(2,1)S(1)} %get-tuple-element.74.refs_1_), channel_id=1, source_target_pairs={{0,4},{1,5},{2,6},{3,7},{4,0},{5,1},{6,2},{7,3},{8,12},{9,13},{10,... | collective-permute-start | bytes 1769480 | tf_op jit(solution)/shard_map/ppermute | solution.py:570
  8.8 25.8 %collective-permute-start.4 = (bf16[272,2048]{1,0:T(8,128)(2,1)S(1)}, bf16[272,2048]{1,0:T(8,128)(2,1)}, u32[]{:S(2)}, u32[]{:S(2)}) collective-permute-start(bf16[272,2048]{1,0:T(8,128)(2,1)S(1)} %get-tuple-element.77), channel_id=1, source_target_pairs={{0,8},{8,0},{16,24},{24,16},{1,9},{9,1},{17,25},{25,17},{2,10},{10... | collective-permute-start | bytes 3342344 | tf_op jit(solution)/shard_map/ppermute | solution.py:573
  23.2 11.4 %collective-permute-start.12 = (bf16[144,2048]{1,0:T(8,128)(2,1)S(1)}, bf16[144,2048]{1,0:T(8,128)(2,1)S(1)}, u32[]{:S(2)}, u32[]{:S(2)}) collective-permute-start(bf16[144,2048]{1,0:T(8,128)(2,1)S(1)} %get-tuple-element.74.refs_1_), channel_id=1, source_target_pairs={{0,1},{1,0},{2,3},{3,2},{4,5},{5,4},{6,7},{7,6},{8,9},{9,8},{10,11... | collective-permute-start | bytes 1769480 | tf_op jit(solution)/shard_map/ppermute | solution.py:570
  23.2 10.1 %collective-permute-start.3 = (bf16[80,2048]{1,0:T(8,128)(2,1)S(1)}, bf16[80,2048]{1,0:T(8,128)(2,1)S(1)}, u32[]{:S(2)}, u32[]{:S(2)}) collective-permute-start(bf16[80,2048]{1,0:T(8,128)(2,1)S(1)} %get-tuple-element.76), channel_id=1, source_target_pairs={{0,4},{1,5},{2,6},{3,7},{4,0},{5,1},{6,2},{7,3},{8,12},{9,13},{10,... | collective-permute-start | bytes 983048 | tf_op jit(solution)/shard_map/ppermute | solution.py:570
  24.7 11.6 %collective-permute-start.13 = (bf16[144,2048]{1,0:T(8,128)(2,1)S(1)}, bf16[144,2048]{1,0:T(8,128)(2,1)S(1)}, u32[]{:S(2)}, u32[]{:S(2)}) collective-permute-start(bf16[144,2048]{1,0:T(8,128)(2,1)S(1)} %collective-permute-done.refs_1_.refs_2_), channel_id=1, source_target_pairs={{0,1},{1,0},{2,3},{3,2},{4,5},{5,4},{6,7},{7,6},{8,9},{9,8},{10,11... | collective-permute-start | bytes 1769480 | tf_op jit(solution)/shard_map/ppermute | solution.py:570
  29.6 8.3 %collective-permute-start.14 = (bf16[144,2048]{1,0:T(8,128)(2,1)S(1)}, bf16[144,2048]{1,0:T(8,128)(2,1)S(1)}, u32[]{:S(2)}, u32[]{:S(2)}) collective-permute-start(bf16[144,2048]{1,0:T(8,128)(2,1)S(1)} %collective-permute-done.1.refs_2_.refs_3_), channel_id=1, source_target_pairs={{0,1},{1,0},{2,3},{3,2},{4,5},{5,4},{6,7},{7,6},{8,9},{9,8},{10,11... | collective-permute-start | bytes 1769480 | tf_op jit(solution)/shard_map/ppermute | solution.py:570
  34.6 10.6 %collective-permute-start.16 = (bf16[80,2048]{1,0:T(8,128)(2,1)S(1)}, bf16[80,2048]{1,0:T(8,128)(2,1)S(1)}, u32[]{:S(2)}, u32[]{:S(2)}) collective-permute-start(bf16[80,2048]{1,0:T(8,128)(2,1)S(1)} %collective-permute-done.3.refs_2_.refs_5_), channel_id=1, source_target_pairs={{0,1},{1,0},{2,3},{3,2},{4,5},{5,4},{6,7},{7,6},{8,9},{9,8},{10,11... | collective-permute-start | bytes 983048 | tf_op jit(solution)/shard_map/ppermute | solution.py:570
  36.3 8.0 %collective-permute-start.8 = (bf16[128,512]{1,0:T(8,128)(2,1)S(1)}, bf16[128,512]{1,0:T(8,128)(2,1)S(1)}, u32[]{:S(2)}, u32[]{:S(2)}) collective-permute-start(bf16[128,512]{1,0:T(8,128)(2,1)S(1)} %tie.6.refs_1_), channel_id=1, source_target_pairs={{0,4},{1,5},{2,6},{3,7},{4,0},{5,1},{6,2},{7,3},{8,12},{9,13},{10,... | collective-permute-start | bytes 393224 | tf_op jit(solution)/shard_map/ppermute | solution.py:570
  38.6 15.4 %collective-permute-start.17 = (bf16[128,1536]{1,0:T(8,128)(2,1)S(1)}, bf16[128,1536]{1,0:T(8,128)(2,1)S(1)}, u32[]{:S(2)}, u32[]{:S(2)}) collective-permute-start(bf16[128,1536]{1,0:T(8,128)(2,1)S(1)} %tie.7.refs_2_), channel_id=1, source_target_pairs={{0,2},{1,3},{2,0},{3,1},{4,6},{5,7},{6,4},{7,5},{8,10},{9,11},{10,... | collective-permute-start | bytes 1179656 | tf_op jit(solution)/shard_map/ppermute | solution.py:570
  41.2 13.5 %collective-permute-start.18 = (bf16[128,1536]{1,0:T(8,128)(2,1)S(1)}, bf16[128,1536]{1,0:T(8,128)(2,1)S(1)}, u32[]{:S(2)}, u32[]{:S(2)}) collective-permute-start(bf16[128,1536]{1,0:T(8,128)(2,1)S(1)} %tie.7.refs_2_), channel_id=1, source_target_pairs={{0,4},{1,5},{2,6},{3,7},{4,0},{5,1},{6,2},{7,3},{8,12},{9,13},{10,... | collective-permute-start | bytes 1179656 | tf_op jit(solution)/shard_map/ppermute | solution.py:570
  52.8 21.8 %collective-permute-start.26 = (bf16[512,768]{1,0:T(8,128)(2,1)S(1)}, bf16[512,768]{1,0:T(8,128)(2,1)S(1)}, u32[]{:S(2)}, u32[]{:S(2)}) collective-permute-start(bf16[512,768]{1,0:T(8,128)(2,1)S(1)} %get-tuple-element.90.refs_3_), channel_id=1, source_target_pairs={{0,8},{24,16},{1,9},{25,17},{2,10},{26,18},{3,11},{27,19},{4,12},{... | collective-permute-start | bytes 2359304 | tf_op jit(solution)/shard_map/ppermute | solution.py:578
  54.1 9.5 %collective-permute-start.22 = (bf16[128,1536]{1,0:T(8,128)(2,1)S(1)}, bf16[128,1536]{1,0:T(8,128)(2,1)S(1)}, u32[]{:S(2)}, u32[]{:S(2)}) collective-permute-start(bf16[128,1536]{1,0:T(8,128)(2,1)S(1)} %collective-permute-done.17.refs_1_.refs_3_), channel_id=1, source_target_pairs={{0,1},{1,0},{2,3},{3,2},{4,5},{5,4},{6,7},{7,6},{8,9},{9,8},{10,11... | collective-permute-start | bytes 1179656 | tf_op jit(solution)/shard_map/ppermute | solution.py:570
  54.6 9.8 %collective-permute-start.23 = (bf16[128,1536]{1,0:T(8,128)(2,1)S(1)}, bf16[128,1536]{1,0:T(8,128)(2,1)S(1)}, u32[]{:S(2)}, u32[]{:S(2)}) collective-permute-start(bf16[128,1536]{1,0:T(8,128)(2,1)S(1)} %collective-permute-done.18.refs_2_.refs_4_), channel_id=1, source_target_pairs={{0,1},{1,0},{2,3},{3,2},{4,5},{5,4},{6,7},{7,6},{8,9},{9,8},{10,11... | collective-permute-start | bytes 1179656 | tf_op jit(solution)/shard_map/ppermute | solution.py:570
  63.5 29.6 %collective-permute-start.28 = (bf16[272,2048]{1,0:T(8,128)(2,1)}, bf16[272,2048]{1,0:T(8,128)(2,1)S(1)}, u32[]{:S(2)}, u32[]{:S(2)}) collective-permute-start(bf16[272,2048]{1,0:T(8,128)(2,1)} %tie.8.refs_2_), channel_id=1, source_target_pairs={{0,2},{1,3},{2,0},{3,1},{4,6},{5,7},{6,4},{7,5},{8,10},{9,11},{10,... | collective-permute-start | bytes 3342344 | tf_op jit(solution)/shard_map/ppermute | solution.py:570
  64.4 28.7 %collective-permute-start.29 = (bf16[272,2048]{1,0:T(8,128)(2,1)}, bf16[272,2048]{1,0:T(8,128)(2,1)S(1)}, u32[]{:S(2)}, u32[]{:S(2)}) collective-permute-start(bf16[272,2048]{1,0:T(8,128)(2,1)} %tie.8.refs_2_), channel_id=1, source_target_pairs={{0,4},{1,5},{2,6},{3,7},{4,0},{5,1},{6,2},{7,3},{8,12},{9,13},{10,... | collective-permute-start | bytes 3342344 | tf_op jit(solution)/shard_map/ppermute | solution.py:570
  70.8 22.3 %collective-permute-start.27 = (bf16[512,768]{1,0:T(8,128)(2,1)S(1)}, bf16[512,768]{1,0:T(8,128)(2,1)S(1)}, u32[]{:S(2)}, u32[]{:S(2)}) collective-permute-start(bf16[512,768]{1,0:T(8,128)(2,1)S(1)} %get-tuple-element.99.refs_3_), channel_id=1, source_target_pairs={{0,8},{24,16},{1,9},{25,17},{2,10},{26,18},{3,11},{27,19},{4,12},{... | collective-permute-start | bytes 2359304 | tf_op jit(solution)/shard_map/ppermute | solution.py:578
  80.6 29.4 %collective-permute-start.32 = (bf16[512,768]{1,0:T(8,128)(2,1)S(1)}, bf16[512,768]{1,0:T(8,128)(2,1)S(1)}, u32[]{:S(2)}, u32[]{:S(2)}) collective-permute-start(bf16[512,768]{1,0:T(8,128)(2,1)S(1)} %get-tuple-element.103), channel_id=1, source_target_pairs={{0,8},{24,16},{8,24},{16,0},{1,9},{25,17},{9,25},{17,1},{2,10},{26... | collective-permute-start | bytes 2359304 | tf_op jit(solution)/shard_map/ppermute | solution.py:578
  94.9 16.4 %collective-permute-start.30 = (bf16[144,2048]{1,0:T(8,128)(2,1)S(1)}, bf16[144,2048]{1,0:T(8,128)(2,1)S(1)}, u32[]{:S(2)}, u32[]{:S(2)}) collective-permute-start(bf16[144,2048]{1,0:T(8,128)(2,1)S(1)} %get-tuple-element.101), channel_id=1, source_target_pairs={{0,2},{1,3},{2,0},{3,1},{4,6},{5,7},{6,4},{7,5},{8,10},{9,11},{10,... | collective-permute-start | bytes 1769480 | tf_op jit(solution)/shard_map/ppermute | solution.py:570
  95.7 15.6 %collective-permute-start.31 = (bf16[128,2048]{1,0:T(8,128)(2,1)S(1)}, bf16[128,2048]{1,0:T(8,128)(2,1)S(1)}, u32[]{:S(2)}, u32[]{:S(2)}) collective-permute-start(bf16[128,2048]{1,0:T(8,128)(2,1)S(1)} %get-tuple-element.102), channel_id=1, source_target_pairs={{0,4},{1,5},{2,6},{3,7},{4,0},{5,1},{6,2},{7,3},{8,12},{9,13},{10,... | collective-permute-start | bytes 1572872 | tf_op jit(solution)/shard_map/ppermute | solution.py:570
  96.4 30.5 %collective-permute-start.33 = (bf16[512,768]{1,0:T(8,128)(2,1)}, bf16[512,768]{1,0:T(8,128)(2,1)}, u32[]{:S(2)}, u32[]{:S(2)}) collective-permute-start(bf16[512,768]{1,0:T(8,128)(2,1)} %get-tuple-element.105), channel_id=1, source_target_pairs={{0,8},{24,16},{8,24},{16,0},{1,9},{25,17},{9,25},{17,1},{2,10},{26... | collective-permute-start | bytes 2359304 | tf_op jit(solution)/shard_map/ppermute | solution.py:578
  98.7 34.3 %collective-permute-start.37 = (bf16[272,2048]{1,0:T(8,128)(2,1)}, bf16[272,2048]{1,0:T(8,128)(2,1)}, u32[]{:S(2)}, u32[]{:S(2)}) collective-permute-start(bf16[272,2048]{1,0:T(8,128)(2,1)} %tie.8.refs_2_), channel_id=1, source_target_pairs={{0,1},{1,0},{2,3},{3,2},{4,5},{5,4},{6,7},{7,6},{8,9},{9,8},{10,11... | collective-permute-start | bytes 3342344 | tf_op jit(solution)/shard_map/ppermute | solution.py:570
  110.0 33.0 %collective-permute-start.36 = (bf16[512,768]{1,0:T(8,128)(2,1)}, bf16[512,768]{1,0:T(8,128)(2,1)}, u32[]{:S(2)}, u32[]{:S(2)}) collective-permute-start(bf16[512,768]{1,0:T(8,128)(2,1)} %tie.9.refs_4_.refs_5_), channel_id=1, source_target_pairs={{0,8},{24,16},{1,9},{25,17},{2,10},{26,18},{3,11},{27,19},{4,12},{... | collective-permute-start | bytes 2359304 | tf_op jit(solution)/shard_map/ppermute | solution.py:578
  113.0 30.1 %collective-permute-start.35 = (bf16[512,768]{1,0:T(8,128)(2,1)}, bf16[512,768]{1,0:T(8,128)(2,1)}, u32[]{:S(2)}, u32[]{:S(2)}) collective-permute-start(bf16[512,768]{1,0:T(8,128)(2,1)} %get-tuple-element.108), channel_id=1, source_target_pairs={{8,24},{16,0},{9,25},{17,1},{10,26},{18,2},{11,27},{19,3},{12,28},... | collective-permute-start | bytes 2359304 | tf_op jit(solution)/shard_map/ppermute | solution.py:578
  122.3 53.7 %all-to-all-start = ((bf16[8,128,2048]{2,1,0:T(8,128)(2,1)}), bf16[8,128,2048]{2,1,0:T(8,128)(2,1)}, u32[]{:S(2)}, u32[]{:S(2)}) async-start(bf16[8,128,2048]{2,1,0:T(8,128)(2,1)} %copy-done.8), calls=%async_computation | async-start | bytes 8388608 | tf_op jit(solution)/shard_map/all_to_all | solution.py:623
  129.7 22.9 %collective-permute-start.34 = (bf16[512,768]{1,0:T(8,128)(2,1)S(1)}, bf16[512,768]{1,0:T(8,128)(2,1)S(1)}, u32[]{:S(2)}, u32[]{:S(2)}) collective-permute-start(bf16[512,768]{1,0:T(8,128)(2,1)S(1)} %get-tuple-element.107), channel_id=1, source_target_pairs={{8,16},{16,8},{9,17},{17,9},{10,18},{18,10},{11,19},{19,11},{12,20... | collective-permute-start | bytes 2359304 | tf_op jit(solution)/shard_map/ppermute | solution.py:578
  133.0 26.3 %collective-permute-start.38 = (bf16[272,2048]{1,0:T(8,128)(2,1)S(1)}, bf16[272,2048]{1,0:T(8,128)(2,1)S(1)}, u32[]{:S(2)}, u32[]{:S(2)}) collective-permute-start(bf16[272,2048]{1,0:T(8,128)(2,1)S(1)} %copy-done.10), channel_id=1, source_target_pairs={{0,1},{1,0},{2,3},{3,2},{4,5},{5,4},{6,7},{7,6},{8,9},{9,8},{10,11... | collective-permute-start | bytes 3342344 | tf_op jit(solution)/shard_map/ppermute | solution.py:570
  133.1 26.2 %collective-permute-start.39 = (bf16[272,2048]{1,0:T(8,128)(2,1)S(1)}, bf16[272,2048]{1,0:T(8,128)(2,1)S(1)}, u32[]{:S(2)}, u32[]{:S(2)}) collective-permute-start(bf16[272,2048]{1,0:T(8,128)(2,1)S(1)} %copy-done.12), channel_id=1, source_target_pairs={{0,1},{1,0},{2,3},{3,2},{4,5},{5,4},{6,7},{7,6},{8,9},{9,8},{10,11... | collective-permute-start | bytes 3342344 | tf_op jit(solution)/shard_map/ppermute | solution.py:570
  143.0 12.6 %collective-permute-start.41 = (bf16[128,2048]{1,0:T(8,128)(2,1)S(1)}, bf16[128,2048]{1,0:T(8,128)(2,1)S(1)}, u32[]{:S(2)}, u32[]{:S(2)}) collective-permute-start(bf16[128,2048]{1,0:T(8,128)(2,1)S(1)} %copy-done.28), channel_id=1, source_target_pairs={{0,1},{1,0},{2,3},{3,2},{4,5},{5,4},{6,7},{7,6},{8,9},{9,8},{10,11... | collective-permute-start | bytes 1572872 | tf_op jit(solution)/shard_map/ppermute | solution.py:570
  143.0 24.9 %collective-permute-start.42 = (bf16[512,768]{1,0:T(8,128)(2,1)S(1)}, bf16[512,768]{1,0:T(8,128)(2,1)S(1)}, u32[]{:S(2)}, u32[]{:S(2)}) collective-permute-start(bf16[512,768]{1,0:T(8,128)(2,1)S(1)} %tie.10.refs_2_.refs_3_), channel_id=1, source_target_pairs={{0,8},{24,16},{1,9},{25,17},{2,10},{26,18},{3,11},{27,19},{4,12},{... | collective-permute-start | bytes 2359304 | tf_op jit(solution)/shard_map/ppermute | solution.py:578
  155.6 26.5 %collective-permute-start.43 = (bf16[512,768]{1,0:T(8,128)(2,1)}, bf16[512,768]{1,0:T(8,128)(2,1)}, u32[]{:S(2)}, u32[]{:S(2)}) collective-permute-start(bf16[512,768]{1,0:T(8,128)(2,1)} %get-tuple-element.130), channel_id=1, source_target_pairs={{8,16},{16,8},{9,17},{17,9},{10,18},{18,10},{11,19},{19,11},{12,20... | collective-permute-start | bytes 2359304 | tf_op jit(solution)/shard_map/ppermute | solution.py:578
  169.6 24.7 %collective-permute-start.44 = (bf16[512,768]{1,0:T(8,128)(2,1)}, bf16[512,768]{1,0:T(8,128)(2,1)S(1)}, u32[]{:S(2)}, u32[]{:S(2)}) collective-permute-start(bf16[512,768]{1,0:T(8,128)(2,1)} %get-tuple-element.134), channel_id=1, source_target_pairs={{8,16},{16,8},{9,17},{17,9},{10,18},{18,10},{11,19},{19,11},{12,20... | collective-permute-start | bytes 2359304 | tf_op jit(solution)/shard_map/ppermute | solution.py:578
  (49 other events, 254.3 us)

commit v7 on v6

--- a/solution.py
+++ b/solution.py
@@ -627,9 +627,9 @@
     z_down = along(x6, middle)
     x7, token = step(pos, near_gate, near_gate, y5, [token, z_down, far_sum])
     z_gate = along(x7, middle)
-    *slots, token = partner(pos, raw_groups, (w_gate, w_up, w_down), capacity, count, [token])
     x8, token = step(pos, near_up, near_up, y6, [token])
     z_up = along(x8, middle)
+    *slots, token = partner(pos, raw_groups, (w_gate, w_up, w_down), capacity, count, [token])
     *mine, token = both(pos, slots, mine, [token])
     mixed, tokens_grad, token = combine(meta, back.reshape(2 * peers * capacity, width), capacity, [token])
 

time: 197 us -> 201 us (1.020)
  waiting for transfers between devices: 76.1 us -> 85.9 us
  starting transfers between devices: 50 us -> 43.6 us
    ppermute x10, waiting for transfers between devices: 47.1 us -> 56 us  [along(): return lax.ppermute(x, 'dp', pairs)]
    ppermute x10, starting transfers between devices: 25.5 us -> 20.9 us  [along(): return lax.ppermute(x, 'dp', pairs)]
    ppermute x34, waiting for transfers between devices: 26 us -> 29.7 us  [over(): return lax.ppermute(x, 'expert', [(i, i ^ bit) for i in range(peers)])]
    unnamed x70 -> x80, local copies, waits for them, and re-layouts: 14.4 us -> 16.1 us
  transfers between devices with their start and end apart: 46 -> 46, of which waited for: 17 -> 18; matrix products, arithmetic and copies ran while one was open for 0% -> 0% of each run, Pallas kernels for 26% -> 25%
where the time goes in v7:
time: 201 us; the launch traced here: 200 us
  waiting for transfers between devices  85.9 us (43%)
  Pallas kernels  52.9 us (26%)
  starting transfers between devices  43.6 us (22%)
  local copies, waits for them, and re-layouts  16.2 us (8%)
    ppermute x10, waiting for transfers between devices, along(): return lax.ppermute(x, 'dp', pairs)  56 us
    pallas_call x21, Pallas kernels, run(): pl.pallas_call(body, in_specs=[ANY] * skip + list(held or [VMEM] * len(op...  52.9 us
    ppermute x34, waiting for transfers between devices, over(): return lax.ppermute(x, 'expert', [(i, i ^ bit) for i in range(peers)])  29.7 us
    ppermute x10, starting transfers between devices, along(): return lax.ppermute(x, 'dp', pairs)  20.9 us
    ppermute x34, starting transfers between devices, over(): return lax.ppermute(x, 'expert', [(i, i ^ bit) for i in range(peers)])  17.7 us
    unnamed x80, local copies, waits for them, and re-layouts  16.1 us
    all_to_all x1, starting transfers between devices, local_pairs(): lax.all_to_all(tie(back, [token]), 'expert', split_axis=0, concat_axis=0,...  4.55 us
  transfers between devices with their start and end apart: 46, of which 18 were waited for; matrix products, arithmetic and copies ran while one was open for 0% of the time, Pallas kernels for 25%

profile of v7, /device:TPU:8, one launch (start us, length us, event | category | flops | bytes accessed | tf_op | source)
XLA Modules:
  0.0 199.7 jit_solution(11751864465961326881)
XLA Ops:
  9.2 1.9 copy-done
  11.1 1.9 copy-done.2
  14.9 5.9 %collective-permute-done.1.refs_2_.refs_3_ = bf16[144,2048]{1,0:T(8,128)(2,1)S(1)} collective-permute-done((bf16[144,2048]{1,0:T(8,128)(2,1)S(1)}, bf16[144,2048]{1,0:T(8,128)(2,1)S(1)}, u32[]{:S(2)}, u32[]{:S(2)}) %collective-permute-start.1) | collective-permute-done | bytes 589856 | tf_op jit(solution)/shard_map/ppermute | solution.py:570
  24.9 4.6 %collective-permute-done.2.refs_1_.refs_4_ = bf16[64,2048]{1,0:T(8,128)(2,1)S(1)} collective-permute-done((bf16[64,2048]{1,0:T(8,128)(2,1)S(1)}, bf16[64,2048]{1,0:T(8,128)(2,1)S(1)}, u32[]{:S(2)}, u32[]{:S(2)}) %collective-permute-start.2) | collective-permute-done | bytes 262176 | tf_op jit(solution)/shard_map/ppermute | solution.py:570
  29.5 4.8 %collective-permute-done.3.refs_2_.refs_5_ = bf16[80,2048]{1,0:T(8,128)(2,1)S(1)} collective-permute-done((bf16[80,2048]{1,0:T(8,128)(2,1)S(1)}, bf16[80,2048]{1,0:T(8,128)(2,1)S(1)}, u32[]{:S(2)}, u32[]{:S(2)}) %collective-permute-start.3) | collective-permute-done | bytes 327712 | tf_op jit(solution)/shard_map/ppermute | solution.py:570
  38.9 3.2 %collective-permute-done.10.refs_7_ = bf16[128,512]{1,0:T(8,128)(2,1)S(1)} collective-permute-done((bf16[128,512]{1,0:T(8,128)(2,1)S(1)}, bf16[128,512]{1,0:T(8,128)(2,1)S(1)}, u32[]{:S(2)}, u32[]{:S(2)}) %collective-permute-start.10) | collective-permute-done | bytes 131104 | tf_op jit(solution)/shard_map/ppermute | solution.py:570
  44.8 5.5 %forward.1 = (bf16[512,2048]{1,0:T(8,128)(2,1)S(1)}, f32[8,128]{1,0:T(8,128)S(1)}, f32[8,128]{1,0:T(8,128)S(1)}, bf16[512,768]{1,0:T(8,128)(2,1)S(1)}, f32[512,7...) custom-call(s32[5]{0:T(128)S(1)} %get-tuple-element.71.refs_0_.refs_1_.refs_2_.refs_3_, ...), custom_call_target="tpu_custom_call" | custom-call | flops 3000000000 | bytes 1024 | tf_op jit(solution)/shard_map/forward/pallas_call | solution.py:112
  56.1 5.5 %collective-permute-done.19.refs_5_.refs_1_ = bf16[64,1536]{1,0:T(8,128)(2,1)S(1)} collective-permute-done((bf16[64,1536]{1,0:T(8,128)(2,1)S(1)}, bf16[64,1536]{1,0:T(8,128)(2,1)S(1)}, u32[]{:S(2)}, u32[]{:S(2)}) %collective-permute-start.19) | collective-permute-done | bytes 196640 | tf_op jit(solution)/shard_map/ppermute | solution.py:570
  64.7 4.7 %backward.1 = (bf16[512,2048]{1,0:T(8,128)(2,1)S(1)}, bf16[512,768]{1,0:T(8,128)(2,1)S(1)}, bf16[512,768]{1,0:T(8,128)(2,1)S(1)}, bf16[512,768]{1,0:T(8,128)(2,1)S(1)}, f32[8,128]{1,0:T(8,128)S(1)}) custom-call(f32[8,128]{1,0:T(8,128)S(1)} %get-tuple-element.81.refs_0_, s32[5]{0:T(128)S(1)} %get-tuple-element.71.refs_0_.refs_1_.refs_2_.refs_3_, ...), custom_call_target="tpu_custom_call" | custom-call | flops 50000000 | bytes 1024 | tf_op jit(solution)/shard_map/backward/pallas_call | solution.py:112
  70.7 3.0 %collective-permute-done.26.refs_1_.refs_4_ = bf16[512,768]{1,0:T(8,128)(2,1)S(1)} collective-permute-done((bf16[512,768]{1,0:T(8,128)(2,1)S(1)}, bf16[512,768]{1,0:T(8,128)(2,1)S(1)}, u32[]{:S(2)}, u32[]{:S(2)}) %collective-permute-start.26) | collective-permute-done | bytes 786464 | tf_op jit(solution)/shard_map/ppermute | solution.py:578
  73.6 3.7 %gradients.1 = (bf16[512,768]{1,0:T(8,128)(2,1)S(1)}, bf16[512,768]{1,0:T(8,128)(2,1)}, bf16[512,768]{1,0:T(8,128)(2,1)S(1)}, bf16[512,768]{1,0:T(8,128)(2,1)S(1...) custom-call(f32[8,128]{1,0:T(8,128)S(1)} %get-tuple-element.89.refs_, ...), custom_call_target="tpu_custom_call" | custom-call | flops 7000000000 | bytes 1024 | tf_op jit(solution)/shard_map/gradients/pallas_call | solution.py:112
  81.2 5.1 %rows_back.1 = (bf16[8,128,2048]{2,1,0:T(8,128)(2,1)S(1)}, f32[8,128]{1,0:T(8,128)S(1)}) custom-call(f32[8,128]{1,0:T(8,128)S(1)} %get-tuple-element.96.refs_0_, bf16[512,768]{1,0:T(8,128)(2,1)S(1)} %get-tuple-element.80.refs_11_.refs_7_.refs_1_, bf16[512,768]{1,0:T(8,128)(2,1)S(1)} %get-tuple-element.92.refs_5_.refs_2_, ...), custom_call_target="tpu_custom_call" | custom-call | flops 50000000 | bytes 1024 | tf_op jit(solution)/shard_map/rows_back/pallas_call | solution.py:112
  86.3 5.4 %collective-permute-done.27.refs_4_ = bf16[512,768]{1,0:T(8,128)(2,1)S(1)} collective-permute-done((bf16[512,768]{1,0:T(8,128)(2,1)S(1)}, bf16[512,768]{1,0:T(8,128)(2,1)S(1)}, u32[]{:S(2)}, u32[]{:S(2)}) %collective-permute-start.27) | collective-permute-done | bytes 786464 | tf_op jit(solution)/shard_map/ppermute | solution.py:578
  95.0 2.5 %collective-permute-start.33 = (bf16[512,768]{1,0:T(8,128)(2,1)}, bf16[512,768]{1,0:T(8,128)(2,1)}, u32[]{:S(2)}, u32[]{:S(2)}) collective-permute-start(bf16[512,768]{1,0:T(8,128)(2,1)} %get-tuple-element.105), channel_id=1, source_target_pairs={{0,8},{24,16},{8,24},{16,0},{1,9},{25,17},{9,25},{17,1},{2,10},{26... | collective-permute-start | bytes 2359304 | tf_op jit(solution)/shard_map/ppermute | solution.py:578
  98.8 9.7 %collective-permute-done.32.refs_6_.refs_3_ = bf16[512,768]{1,0:T(8,128)(2,1)S(1)} collective-permute-done((bf16[512,768]{1,0:T(8,128)(2,1)S(1)}, bf16[512,768]{1,0:T(8,128)(2,1)S(1)}, u32[]{:S(2)}, u32[]{:S(2)}) %collective-permute-start.32) | collective-permute-done | bytes 786464 | tf_op jit(solution)/shard_map/ppermute | solution.py:578
  110.7 2.0 %copy-done.8 = bf16[8,128,2048]{2,1,0:T(8,128)(2,1)} copy-done((bf16[8,128,2048]{2,1,0:T(8,128)(2,1)}, bf16[8,128,2048]{2,1,0:T(8,128)(2,1)S(1)}, u32[]{:S(2)}) %copy-start.8) | copy-done | bytes 4194328
  112.7 4.6 %all-to-all-start = ((bf16[8,128,2048]{2,1,0:T(8,128)(2,1)}), bf16[8,128,2048]{2,1,0:T(8,128)(2,1)}, u32[]{:S(2)}, u32[]{:S(2)}) async-start(bf16[8,128,2048]{2,1,0:T(8,128)(2,1)} %copy-done.8), calls=%async_computation | async-start | bytes 8388608 | tf_op jit(solution)/shard_map/all_to_all | solution.py:623
  117.3 2.8 %collective-permute-start.35 = (bf16[512,768]{1,0:T(8,128)(2,1)}, bf16[512,768]{1,0:T(8,128)(2,1)S(1)}, u32[]{:S(2)}, u32[]{:S(2)}) collective-permute-start(bf16[512,768]{1,0:T(8,128)(2,1)} %copy-done.33), channel_id=1, source_target_pairs={{8,24},{16,0},{9,25},{17,1},{10,26},{18,2},{11,27},{19,3},{12,28},... | collective-permute-start | bytes 2359304 | tf_op jit(solution)/shard_map/ppermute | solution.py:578
  120.1 5.4 %collective-permute-done.33.refs_4_.refs_3_ = bf16[512,768]{1,0:T(8,128)(2,1)} collective-permute-done((bf16[512,768]{1,0:T(8,128)(2,1)}, bf16[512,768]{1,0:T(8,128)(2,1)}, u32[]{:S(2)}, u32[]{:S(2)}) %collective-permute-start.33) | collective-permute-done | bytes 786464 | tf_op jit(solution)/shard_map/ppermute | solution.py:578
  128.0 3.5 %collective-permute-start.34 = (bf16[512,768]{1,0:T(8,128)(2,1)S(1)}, bf16[512,768]{1,0:T(8,128)(2,1)S(1)}, u32[]{:S(2)}, u32[]{:S(2)}) collective-permute-start(bf16[512,768]{1,0:T(8,128)(2,1)S(1)} %get-tuple-element.107), channel_id=1, source_target_pairs={{8,16},{16,8},{9,17},{17,9},{10,18},{18,10},{11,19},{19,11},{12,20... | collective-permute-start | bytes 2359304 | tf_op jit(solution)/shard_map/ppermute | solution.py:578
  132.9 9.5 %collective-permute-done.36.refs_6_ = bf16[512,768]{1,0:T(8,128)(2,1)} collective-permute-done((bf16[512,768]{1,0:T(8,128)(2,1)}, bf16[512,768]{1,0:T(8,128)(2,1)}, u32[]{:S(2)}, u32[]{:S(2)}) %collective-permute-start.36) | collective-permute-done | bytes 786464 | tf_op jit(solution)/shard_map/ppermute | solution.py:578
  142.9 12.6 %collective-permute-done.34.refs_1_.refs_4_ = bf16[512,768]{1,0:T(8,128)(2,1)S(1)} collective-permute-done((bf16[512,768]{1,0:T(8,128)(2,1)S(1)}, bf16[512,768]{1,0:T(8,128)(2,1)S(1)}, u32[]{:S(2)}, u32[]{:S(2)}) %collective-permute-start.34) | collective-permute-done | bytes 786464 | tf_op jit(solution)/shard_map/ppermute | solution.py:578
  155.6 3.0 %step.10 = (bf16[512,768]{1,0:T(8,128)(2,1)}, f32[8,128]{1,0:T(8,128)S(1)}) custom-call(f32[8,128]{1,0:T(8,128)S(1)} %get-tuple-element.106.refs_0_, bf16[512,768]{1,0:T(8,128)(2,1)S(1)} %collective-permute-done.34.refs_1_.refs_4_, bf16[512,768]{1,0:T(8,128)(2,1)S(1)} %collective-permute-done.35.refs_2_.refs_3_, ...), custom_call_target="tpu_custom_call" | custom-call | flops 8000000000 | bytes 1024 | tf_op jit(solution)/shard_map/step/pallas_call | solution.py:112
  158.6 3.3 %collective-permute-start.43 = (bf16[512,768]{1,0:T(8,128)(2,1)}, bf16[512,768]{1,0:T(8,128)(2,1)}, u32[]{:S(2)}, u32[]{:S(2)}) collective-permute-start(bf16[512,768]{1,0:T(8,128)(2,1)} %get-tuple-element.130), channel_id=1, source_target_pairs={{8,16},{16,8},{9,17},{17,9},{10,18},{18,10},{11,19},{19,11},{12,20... | collective-permute-start | bytes 2359304 | tf_op jit(solution)/shard_map/ppermute | solution.py:578
  163.5 2.9 %collective-permute-start.44 = (bf16[512,768]{1,0:T(8,128)(2,1)}, bf16[512,768]{1,0:T(8,128)(2,1)}, u32[]{:S(2)}, u32[]{:S(2)}) collective-permute-start(bf16[512,768]{1,0:T(8,128)(2,1)} %get-tuple-element.134), channel_id=1, source_target_pairs={{8,16},{16,8},{9,17},{17,9},{10,18},{18,10},{11,19},{19,11},{12,20... | collective-permute-start | bytes 2359304 | tf_op jit(solution)/shard_map/ppermute | solution.py:578
  166.5 2.0 collective-permute-done.41.refs_10_
  168.5 7.6 %partner.1 = (bf16[512,2048]{1,0:T(8,128)(2,1)S(1)}, bf16[512,2048]{1,0:T(8,128)(2,1)S(1)}, bf16[512,768]{1,0:T(8,128)(2,1)S(1)}, bf16[512,768]{1,0:T(8,128)(2,1...) custom-call(f32[8,128]{1,0:T(8,128)S(1)} %get-tuple-element.112.refs_0_, ...), custom_call_target="tpu_custom_call" | custom-call | flops 500000000 | bytes 1024 | tf_op jit(solution)/shard_map/partner/pallas_call | solution.py:112
  176.1 2.1 %both.1 = (bf16[512,768]{1,0:T(8,128)(2,1)S(1)}, bf16[512,768]{1,0:T(8,128)(2,1)S(1)}, bf16[512,768]{1,0:T(8,128)(2,1)S(1)}, f32[8,128]{1,0:T(8,128)S(1)}) custom-call(f32[8,128]{1,0:T(8,128)S(1)} %get-tuple-element.113.refs_0_, s32[5]{0:T(128)S(1)} %get-tuple-element.71.refs_0_.refs_1_.refs_2_.refs_3_, bf16[512,2048]{1,0:T(8,128)(2,1)S(1)} %get-tuple-element.114.refs_2_, ...), custom_call_target="tpu_custom_call" | custom-call | flops 250000000 | bytes 1024 | tf_op jit(solution)/shard_map/both/pallas_call | solution.py:112
  178.3 4.5 %combine.1 = (bf16[128,2048]{1,0:T(8,128)(2,1)}, bf16[128,2048]{1,0:T(8,128)(2,1)}, f32[8,128]{1,0:T(8,128)S(1)}) custom-call(f32[8,128]{1,0:T(8,128)S(1)} %get-tuple-element.122.refs_0_, bf16[16,128]{1,0:T(8,128)(2,1)S(1)} %get-tuple-element.73.refs_0_.refs_1_, bf16[1024,2048]{1,0:T(8,128)(2,1)} %bitcast.10.refs_2_), custom_call_target="tpu_custom_call" | custom-call | flops 250000000 | bytes 1024 | tf_op jit(solution)/shard_map/combine/pallas_call | solution.py:112
  184.4 2.5 %total.4 = (bf16[512,768]{1,0:T(8,128)(2,1)}, f32[8,128]{1,0:T(8,128)S(1)}) custom-call(f32[8,128]{1,0:T(8,128)S(1)} %get-tuple-element.128.refs_0_, s32[5]{0:T(128)S(1)} %get-tuple-element.71.refs_0_.refs_1_.refs_2_.refs_3_, bf16[512,768]{1,0:T(8,128)(2,1)S(1)} %get-tuple-element.129.refs_2_, bf16[512,768]{1,0:T(8,128)(2,1)} %collective-permute-done.33.refs_4_.refs_3_, ...), custom_call_target="tpu_custom_call" | custom-call | flops 250000000 | bytes 1024 | tf_op jit(solution)/shard_map/total/pallas_call | solution.py:112
  186.9 10.4 %collective-permute-done.44.refs_4_ = bf16[512,768]{1,0:T(8,128)(2,1)} collective-permute-done((bf16[512,768]{1,0:T(8,128)(2,1)}, bf16[512,768]{1,0:T(8,128)(2,1)}, u32[]{:S(2)}, u32[]{:S(2)}) %collective-permute-start.44) | collective-permute-done | bytes 786464 | tf_op jit(solution)/shard_map/ppermute | solution.py:578
  197.4 2.3 %total.5 = (bf16[512,768]{1,0:T(8,128)(2,1)}, f32[8,128]{1,0:T(8,128)}) custom-call(f32[8,128]{1,0:T(8,128)S(1)} %get-tuple-element.132.refs_0_, s32[5]{0:T(128)S(1)} %get-tuple-element.71.refs_0_.refs_1_.refs_2_.refs_3_, bf16[512,768]{1,0:T(8,128)(2,1)S(1)} %get-tuple-element.133.refs_2_, bf16[512,768]{1,0:T(8,128)(2,1)S(1)} %copy-done.26, ...), custom_call_target="tpu_custom_call" | custom-call | flops 250000000 | bytes 1024 | tf_op jit(solution)/shard_map/total/pallas_call | solution.py:112
  (168 shorter events, 50.3 us)
Async XLA Ops:
  5.7 15.1 %collective-permute-start.1 = (bf16[144,2048]{1,0:T(8,128)(2,1)S(1)}, bf16[144,2048]{1,0:T(8,128)(2,1)S(1)}, u32[]{:S(2)}, u32[]{:S(2)}) collective-permute-start(bf16[144,2048]{1,0:T(8,128)(2,1)S(1)} %get-tuple-element.74.refs_1_), channel_id=1, source_target_pairs={{0,4},{1,5},{2,6},{3,7},{4,0},{5,1},{6,2},{7,3},{8,12},{9,13},{10,... | collective-permute-start | bytes 1769480 | tf_op jit(solution)/shard_map/ppermute | solution.py:570
  7.3 14.8 %collective-permute-start = (bf16[144,2048]{1,0:T(8,128)(2,1)S(1)}, bf16[144,2048]{1,0:T(8,128)(2,1)S(1)}, u32[]{:S(2)}, u32[]{:S(2)}) collective-permute-start(bf16[144,2048]{1,0:T(8,128)(2,1)S(1)} %get-tuple-element.74.refs_1_), channel_id=1, source_target_pairs={{0,2},{1,3},{2,0},{3,1},{4,6},{5,7},{6,4},{7,5},{8,10},{9,11},{10,... | collective-permute-start | bytes 1769480 | tf_op jit(solution)/shard_map/ppermute | solution.py:570
  8.8 25.7 %collective-permute-start.4 = (bf16[272,2048]{1,0:T(8,128)(2,1)S(1)}, bf16[272,2048]{1,0:T(8,128)(2,1)S(1)}, u32[]{:S(2)}, u32[]{:S(2)}) collective-permute-start(bf16[272,2048]{1,0:T(8,128)(2,1)S(1)} %get-tuple-element.77), channel_id=1, source_target_pairs={{0,8},{8,0},{16,24},{24,16},{1,9},{9,1},{17,25},{25,17},{2,10},{10... | collective-permute-start | bytes 3342344 | tf_op jit(solution)/shard_map/ppermute | solution.py:573
  24.2 10.6 %collective-permute-start.12 = (bf16[144,2048]{1,0:T(8,128)(2,1)S(1)}, bf16[144,2048]{1,0:T(8,128)(2,1)S(1)}, u32[]{:S(2)}, u32[]{:S(2)}) collective-permute-start(bf16[144,2048]{1,0:T(8,128)(2,1)S(1)} %get-tuple-element.74.refs_1_), channel_id=1, source_target_pairs={{0,1},{1,0},{2,3},{3,2},{4,5},{5,4},{6,7},{7,6},{8,9},{9,8},{10,11... | collective-permute-start | bytes 1769480 | tf_op jit(solution)/shard_map/ppermute | solution.py:570
  24.2 10.1 %collective-permute-start.3 = (bf16[80,2048]{1,0:T(8,128)(2,1)S(1)}, bf16[80,2048]{1,0:T(8,128)(2,1)S(1)}, u32[]{:S(2)}, u32[]{:S(2)}) collective-permute-start(bf16[80,2048]{1,0:T(8,128)(2,1)S(1)} %get-tuple-element.76), channel_id=1, source_target_pairs={{0,4},{1,5},{2,6},{3,7},{4,0},{5,1},{6,2},{7,3},{8,12},{9,13},{10,... | collective-permute-start | bytes 983048 | tf_op jit(solution)/shard_map/ppermute | solution.py:570
  24.7 12.1 %collective-permute-start.14 = (bf16[144,2048]{1,0:T(8,128)(2,1)S(1)}, bf16[144,2048]{1,0:T(8,128)(2,1)S(1)}, u32[]{:S(2)}, u32[]{:S(2)}) collective-permute-start(bf16[144,2048]{1,0:T(8,128)(2,1)S(1)} %collective-permute-done.1.refs_2_.refs_3_), channel_id=1, source_target_pairs={{0,1},{1,0},{2,3},{3,2},{4,5},{5,4},{6,7},{7,6},{8,9},{9,8},{10,11... | collective-permute-start | bytes 1769480 | tf_op jit(solution)/shard_map/ppermute | solution.py:570
  29.5 8.8 %collective-permute-start.13 = (bf16[144,2048]{1,0:T(8,128)(2,1)S(1)}, bf16[144,2048]{1,0:T(8,128)(2,1)S(1)}, u32[]{:S(2)}, u32[]{:S(2)}) collective-permute-start(bf16[144,2048]{1,0:T(8,128)(2,1)S(1)} %collective-permute-done.refs_1_.refs_2_), channel_id=1, source_target_pairs={{0,1},{1,0},{2,3},{3,2},{4,5},{5,4},{6,7},{7,6},{8,9},{9,8},{10,11... | collective-permute-start | bytes 1769480 | tf_op jit(solution)/shard_map/ppermute | solution.py:570
  35.8 8.4 %collective-permute-start.8 = (bf16[128,512]{1,0:T(8,128)(2,1)S(1)}, bf16[128,512]{1,0:T(8,128)(2,1)S(1)}, u32[]{:S(2)}, u32[]{:S(2)}) collective-permute-start(bf16[128,512]{1,0:T(8,128)(2,1)S(1)} %tie.6.refs_1_), channel_id=1, source_target_pairs={{0,4},{1,5},{2,6},{3,7},{4,0},{5,1},{6,2},{7,3},{8,12},{9,13},{10,... | collective-permute-start | bytes 393224 | tf_op jit(solution)/shard_map/ppermute | solution.py:570
  36.8 7.4 %collective-permute-start.6 = (bf16[128,512]{1,0:T(8,128)(2,1)S(1)}, bf16[128,512]{1,0:T(8,128)(2,1)S(1)}, u32[]{:S(2)}, u32[]{:S(2)}) collective-permute-start(bf16[128,512]{1,0:T(8,128)(2,1)S(1)} %tie.6.refs_1_), channel_id=1, source_target_pairs={{0,2},{1,3},{2,0},{3,1},{4,6},{5,7},{6,4},{7,5},{8,10},{9,11},{10,... | collective-permute-start | bytes 393224 | tf_op jit(solution)/shard_map/ppermute | solution.py:570
  38.3 15.2 %collective-permute-start.18 = (bf16[128,1536]{1,0:T(8,128)(2,1)S(1)}, bf16[128,1536]{1,0:T(8,128)(2,1)S(1)}, u32[]{:S(2)}, u32[]{:S(2)}) collective-permute-start(bf16[128,1536]{1,0:T(8,128)(2,1)S(1)} %tie.7.refs_2_), channel_id=1, source_target_pairs={{0,4},{1,5},{2,6},{3,7},{4,0},{5,1},{6,2},{7,3},{8,12},{9,13},{10,... | collective-permute-start | bytes 1179656 | tf_op jit(solution)/shard_map/ppermute | solution.py:570
  42.1 11.6 %collective-permute-start.17 = (bf16[128,1536]{1,0:T(8,128)(2,1)S(1)}, bf16[128,1536]{1,0:T(8,128)(2,1)S(1)}, u32[]{:S(2)}, u32[]{:S(2)}) collective-permute-start(bf16[128,1536]{1,0:T(8,128)(2,1)S(1)} %tie.7.refs_2_), channel_id=1, source_target_pairs={{0,2},{1,3},{2,0},{3,1},{4,6},{5,7},{6,4},{7,5},{8,10},{9,11},{10,... | collective-permute-start | bytes 1179656 | tf_op jit(solution)/shard_map/ppermute | solution.py:570
  52.2 21.4 %collective-permute-start.26 = (bf16[512,768]{1,0:T(8,128)(2,1)S(1)}, bf16[512,768]{1,0:T(8,128)(2,1)S(1)}, u32[]{:S(2)}, u32[]{:S(2)}) collective-permute-start(bf16[512,768]{1,0:T(8,128)(2,1)S(1)} %get-tuple-element.90.refs_3_), channel_id=1, source_target_pairs={{0,8},{24,16},{1,9},{25,17},{2,10},{26,18},{3,11},{27,19},{4,12},{... | collective-permute-start | bytes 2359304 | tf_op jit(solution)/shard_map/ppermute | solution.py:578
  53.5 8.6 %collective-permute-start.23 = (bf16[128,1536]{1,0:T(8,128)(2,1)S(1)}, bf16[128,1536]{1,0:T(8,128)(2,1)S(1)}, u32[]{:S(2)}, u32[]{:S(2)}) collective-permute-start(bf16[128,1536]{1,0:T(8,128)(2,1)S(1)} %collective-permute-done.18.refs_2_.refs_4_), channel_id=1, source_target_pairs={{0,1},{1,0},{2,3},{3,2},{4,5},{5,4},{6,7},{7,6},{8,9},{9,8},{10,11... | collective-permute-start | bytes 1179656 | tf_op jit(solution)/shard_map/ppermute | solution.py:570
  53.7 9.7 %collective-permute-start.22 = (bf16[128,1536]{1,0:T(8,128)(2,1)S(1)}, bf16[128,1536]{1,0:T(8,128)(2,1)S(1)}, u32[]{:S(2)}, u32[]{:S(2)}) collective-permute-start(bf16[128,1536]{1,0:T(8,128)(2,1)S(1)} %collective-permute-done.17.refs_1_.refs_3_), channel_id=1, source_target_pairs={{0,1},{1,0},{2,3},{3,2},{4,5},{5,4},{6,7},{7,6},{8,9},{9,8},{10,11... | collective-permute-start | bytes 1179656 | tf_op jit(solution)/shard_map/ppermute | solution.py:570
  62.1 29.5 %collective-permute-start.29 = (bf16[272,2048]{1,0:T(8,128)(2,1)S(1)}, bf16[272,2048]{1,0:T(8,128)(2,1)S(1)}, u32[]{:S(2)}, u32[]{:S(2)}) collective-permute-start(bf16[272,2048]{1,0:T(8,128)(2,1)S(1)} %tie.8.refs_2_), channel_id=1, source_target_pairs={{0,4},{1,5},{2,6},{3,7},{4,0},{5,1},{6,2},{7,3},{8,12},{9,13},{10,... | collective-permute-start | bytes 3342344 | tf_op jit(solution)/shard_map/ppermute | solution.py:570
  63.3 28.3 %collective-permute-start.28 = (bf16[272,2048]{1,0:T(8,128)(2,1)S(1)}, bf16[272,2048]{1,0:T(8,128)(2,1)S(1)}, u32[]{:S(2)}, u32[]{:S(2)}) collective-permute-start(bf16[272,2048]{1,0:T(8,128)(2,1)S(1)} %tie.8.refs_2_), channel_id=1, source_target_pairs={{0,2},{1,3},{2,0},{3,1},{4,6},{5,7},{6,4},{7,5},{8,10},{9,11},{10,... | collective-permute-start | bytes 3342344 | tf_op jit(solution)/shard_map/ppermute | solution.py:570
  69.4 22.3 %collective-permute-start.27 = (bf16[512,768]{1,0:T(8,128)(2,1)S(1)}, bf16[512,768]{1,0:T(8,128)(2,1)S(1)}, u32[]{:S(2)}, u32[]{:S(2)}) collective-permute-start(bf16[512,768]{1,0:T(8,128)(2,1)S(1)} %get-tuple-element.99.refs_3_), channel_id=1, source_target_pairs={{0,8},{24,16},{1,9},{25,17},{2,10},{26,18},{3,11},{27,19},{4,12},{... | collective-permute-start | bytes 2359304 | tf_op jit(solution)/shard_map/ppermute | solution.py:578
  79.6 28.9 %collective-permute-start.32 = (bf16[512,768]{1,0:T(8,128)(2,1)S(1)}, bf16[512,768]{1,0:T(8,128)(2,1)S(1)}, u32[]{:S(2)}, u32[]{:S(2)}) collective-permute-start(bf16[512,768]{1,0:T(8,128)(2,1)S(1)} %get-tuple-element.103), channel_id=1, source_target_pairs={{0,8},{24,16},{8,24},{16,0},{1,9},{25,17},{9,25},{17,1},{2,10},{26... | collective-permute-start | bytes 2359304 | tf_op jit(solution)/shard_map/ppermute | solution.py:578
  93.4 15.1 %collective-permute-start.30 = (bf16[144,2048]{1,0:T(8,128)(2,1)S(1)}, bf16[144,2048]{1,0:T(8,128)(2,1)S(1)}, u32[]{:S(2)}, u32[]{:S(2)}) collective-permute-start(bf16[144,2048]{1,0:T(8,128)(2,1)S(1)} %get-tuple-element.101), channel_id=1, source_target_pairs={{0,2},{1,3},{2,0},{3,1},{4,6},{5,7},{6,4},{7,5},{8,10},{9,11},{10,... | collective-permute-start | bytes 1769480 | tf_op jit(solution)/shard_map/ppermute | solution.py:570
  94.1 14.4 %collective-permute-start.31 = (bf16[128,2048]{1,0:T(8,128)(2,1)S(1)}, bf16[128,2048]{1,0:T(8,128)(2,1)S(1)}, u32[]{:S(2)}, u32[]{:S(2)}) collective-permute-start(bf16[128,2048]{1,0:T(8,128)(2,1)S(1)} %get-tuple-element.102), channel_id=1, source_target_pairs={{0,4},{1,5},{2,6},{3,7},{4,0},{5,1},{6,2},{7,3},{8,12},{9,13},{10,... | collective-permute-start | bytes 1572872 | tf_op jit(solution)/shard_map/ppermute | solution.py:570
  95.0 30.5 %collective-permute-start.33 = (bf16[512,768]{1,0:T(8,128)(2,1)}, bf16[512,768]{1,0:T(8,128)(2,1)}, u32[]{:S(2)}, u32[]{:S(2)}) collective-permute-start(bf16[512,768]{1,0:T(8,128)(2,1)} %get-tuple-element.105), channel_id=1, source_target_pairs={{0,8},{24,16},{8,24},{16,0},{1,9},{25,17},{9,25},{17,1},{2,10},{26... | collective-permute-start | bytes 2359304 | tf_op jit(solution)/shard_map/ppermute | solution.py:578
  97.5 44.8 %collective-permute-start.36 = (bf16[512,768]{1,0:T(8,128)(2,1)}, bf16[512,768]{1,0:T(8,128)(2,1)}, u32[]{:S(2)}, u32[]{:S(2)}) collective-permute-start(bf16[512,768]{1,0:T(8,128)(2,1)} %tie.9.refs_4_.refs_5_), channel_id=1, source_target_pairs={{0,8},{24,16},{1,9},{25,17},{2,10},{26,18},{3,11},{27,19},{4,12},{... | collective-permute-start | bytes 2359304 | tf_op jit(solution)/shard_map/ppermute | solution.py:578
  112.7 65.5 %all-to-all-start = ((bf16[8,128,2048]{2,1,0:T(8,128)(2,1)}), bf16[8,128,2048]{2,1,0:T(8,128)(2,1)}, u32[]{:S(2)}, u32[]{:S(2)}) async-start(bf16[8,128,2048]{2,1,0:T(8,128)(2,1)} %copy-done.8), calls=%async_computation | async-start | bytes 8388608 | tf_op jit(solution)/shard_map/all_to_all | solution.py:623
  117.3 25.1 %collective-permute-start.35 = (bf16[512,768]{1,0:T(8,128)(2,1)}, bf16[512,768]{1,0:T(8,128)(2,1)S(1)}, u32[]{:S(2)}, u32[]{:S(2)}) collective-permute-start(bf16[512,768]{1,0:T(8,128)(2,1)} %copy-done.33), channel_id=1, source_target_pairs={{8,24},{16,0},{9,25},{17,1},{10,26},{18,2},{11,27},{19,3},{12,28},... | collective-permute-start | bytes 2359304 | tf_op jit(solution)/shard_map/ppermute | solution.py:578
  128.0 27.6 %collective-permute-start.34 = (bf16[512,768]{1,0:T(8,128)(2,1)S(1)}, bf16[512,768]{1,0:T(8,128)(2,1)S(1)}, u32[]{:S(2)}, u32[]{:S(2)}) collective-permute-start(bf16[512,768]{1,0:T(8,128)(2,1)S(1)} %get-tuple-element.107), channel_id=1, source_target_pairs={{8,16},{16,8},{9,17},{17,9},{10,18},{18,10},{11,19},{19,11},{12,20... | collective-permute-start | bytes 2359304 | tf_op jit(solution)/shard_map/ppermute | solution.py:578
  131.5 27.1 %collective-permute-start.37 = (bf16[512,768]{1,0:T(8,128)(2,1)S(1)}, bf16[512,768]{1,0:T(8,128)(2,1)S(1)}, u32[]{:S(2)}, u32[]{:S(2)}) collective-permute-start(bf16[512,768]{1,0:T(8,128)(2,1)S(1)} %tie.10.refs_2_.refs_3_), channel_id=1, source_target_pairs={{0,8},{24,16},{1,9},{25,17},{2,10},{26,18},{3,11},{27,19},{4,12},{... | collective-permute-start | bytes 2359304 | tf_op jit(solution)/shard_map/ppermute | solution.py:578
  132.8 30.7 %collective-permute-start.38 = (bf16[272,2048]{1,0:T(8,128)(2,1)S(1)}, bf16[272,2048]{1,0:T(8,128)(2,1)S(1)}, u32[]{:S(2)}, u32[]{:S(2)}) collective-permute-start(bf16[272,2048]{1,0:T(8,128)(2,1)S(1)} %copy-done.10), channel_id=1, source_target_pairs={{0,1},{1,0},{2,3},{3,2},{4,5},{5,4},{6,7},{7,6},{8,9},{9,8},{10,11... | collective-permute-start | bytes 3342344 | tf_op jit(solution)/shard_map/ppermute | solution.py:570
  142.3 24.2 %collective-permute-start.40 = (bf16[272,2048]{1,0:T(8,128)(2,1)S(1)}, bf16[272,2048]{1,0:T(8,128)(2,1)S(1)}, u32[]{:S(2)}, u32[]{:S(2)}) collective-permute-start(bf16[272,2048]{1,0:T(8,128)(2,1)S(1)} %copy-done.12), channel_id=1, source_target_pairs={{0,1},{1,0},{2,3},{3,2},{4,5},{5,4},{6,7},{7,6},{8,9},{9,8},{10,11... | collective-permute-start | bytes 3342344 | tf_op jit(solution)/shard_map/ppermute | solution.py:570
  142.4 24.2 %collective-permute-start.39 = (bf16[272,2048]{1,0:T(8,128)(2,1)S(1)}, bf16[272,2048]{1,0:T(8,128)(2,1)S(1)}, u32[]{:S(2)}, u32[]{:S(2)}) collective-permute-start(bf16[272,2048]{1,0:T(8,128)(2,1)S(1)} %copy-done.14), channel_id=1, source_target_pairs={{0,1},{1,0},{2,3},{3,2},{4,5},{5,4},{6,7},{7,6},{8,9},{9,8},{10,11... | collective-permute-start | bytes 3342344 | tf_op jit(solution)/shard_map/ppermute | solution.py:570
  155.6 10.9 %collective-permute-start.42 = (bf16[128,2048]{1,0:T(8,128)(2,1)S(1)}, bf16[128,2048]{1,0:T(8,128)(2,1)S(1)}, u32[]{:S(2)}, u32[]{:S(2)}) collective-permute-start(bf16[128,2048]{1,0:T(8,128)(2,1)S(1)} %copy-done.32), channel_id=1, source_target_pairs={{0,1},{1,0},{2,3},{3,2},{4,5},{5,4},{6,7},{7,6},{8,9},{9,8},{10,11... | collective-permute-start | bytes 1572872 | tf_op jit(solution)/shard_map/ppermute | solution.py:570
  158.6 25.8 %collective-permute-start.43 = (bf16[512,768]{1,0:T(8,128)(2,1)}, bf16[512,768]{1,0:T(8,128)(2,1)}, u32[]{:S(2)}, u32[]{:S(2)}) collective-permute-start(bf16[512,768]{1,0:T(8,128)(2,1)} %get-tuple-element.130), channel_id=1, source_target_pairs={{8,16},{16,8},{9,17},{17,9},{10,18},{18,10},{11,19},{19,11},{12,20... | collective-permute-start | bytes 2359304 | tf_op jit(solution)/shard_map/ppermute | solution.py:578
  163.5 33.9 %collective-permute-start.44 = (bf16[512,768]{1,0:T(8,128)(2,1)}, bf16[512,768]{1,0:T(8,128)(2,1)}, u32[]{:S(2)}, u32[]{:S(2)}) collective-permute-start(bf16[512,768]{1,0:T(8,128)(2,1)} %get-tuple-element.134), channel_id=1, source_target_pairs={{8,16},{16,8},{9,17},{17,9},{10,18},{18,10},{11,19},{19,11},{12,20... | collective-permute-start | bytes 2359304 | tf_op jit(solution)/shard_map/ppermute | solution.py:578
  (54 other events, 353.2 us)
